TPU v7x, 32 devices: a whole 2x2x4 slice. The times are simulated.
32 devices in a mesh: row: 4 (over z), col: 8 (over y, x, core).
Axes of the slice: x: 2, y: 2, z: 4, core: 2. Of those that a mesh axis runs over, the one named last changes fastest.
Arguments:
- compound_pos: float32 [8192, 128], P(('row', 'col')), may hold values from -1.75 to 1.75
- compound_mom: float32 [8192, 128], P(('row', 'col')), may hold values from -6 to 6
- target_pos: float32 [8192, 128], P(('row', 'col')), may hold values from -1.75 to 1.75
- target_mom: float32 [8192, 128], P(('row', 'col')), may hold values from -6 to 6
- tile_rows: int32 [32, 256], P(('row', 'col')), may hold values from 0 to 63, as said below
- tile_cols: int32 [32, 256], P(('row', 'col')), may hold values from 0 to 63, as said below
- tile_count: int32 [32], P(('row', 'col')), may hold values from 32 to 256, as said below
- tile_values: bfloat16 [32, 256, 128, 128], P(('row', 'col')), may hold values from -6 to 6
- tile_weight: bfloat16 [32, 256, 128, 128], P(('row', 'col')), may hold values from 0 to 2, as said below
Outputs:
- compound_out: float32 [8192, 128], P(('row', 'col'))
- compound_mom_out: float32 [8192, 128], P(('row', 'col'))
- target_out: float32 [8192, 128], P(('row', 'col'))
- target_mom_out: float32 [8192, 128], P(('row', 'col'))
Inputs may be any that keep to these rules, and one draw needn't show every extreme that they name: `tile_rows`: slots of device d = i * 8 + j name compound blocks from i * 8 * 2 to (i + 1) * 8 * 2 - 1. `tile_cols`: slots of device d = i * 8 + j name target blocks (a * 8 + j) * 2 + c with a < 4 and c < 2. `tile_count`: some device has all 256 slots live in every draw. `tile_weight`: unobserved entries are 0; observed ones are positive.
All inputs are finite; a program needn't handle non-finite values.
Results may differ from a plain program's by a relative error of at most 0.0095.
Values may be sent and summed in bfloat16 or wider, within the bound.
No kernel may reach another device: no remote copies, remote signals or barrier semaphores. Data moves between devices by JAX's collectives and lax.ppermute only.
A program may use at most 128 MiB of HBM per device.

v0:
```python
import functools
import math

import jax
import jax.numpy as jnp
from jax import lax
from jax.experimental import pallas as pl
from jax.experimental.pallas import tpu as pltpu
from jax.sharding import PartitionSpec as P

LEAPS = 2
GROUP = 4
UNROLL = 4


degrees_free = 4.0
noise_scale = 0.5
prior_weight = 1.0
step_size = 0.01


def load_kernel(targ_group, shape, pair_ref, live_ref, values_hbm, weight_hbm, *refs):
    values_out, weight_out, lists_ref, sems = refs
    pairs, comp_tiles, targ_tiles = shape
    slots = values_hbm.shape[0]
    chunks = sems.shape[1]
    chunk = slots // chunks

    def copies(index):
        part = pl.ds(index * chunk, chunk)
        return (
            pltpu.make_async_copy(values_hbm.at[part], values_out.at[part], sems.at[0, index]),
            pltpu.make_async_copy(weight_hbm.at[part], weight_out.at[part], sems.at[1, index]),
        )

    for index in range(chunks):

        @pl.when(index * chunk < live_ref[0])
        def _():
            for copy in copies(index):
                copy.start()

    values_out[slots] = jnp.zeros_like(values_out[slots])
    weight_out[slots] = jnp.zeros_like(weight_out[slots])

    across = jnp.broadcast_to(pair_ref[...].astype(jnp.float32), (slots, slots))
    down = across.T
    at = lax.broadcasted_iota(jnp.int32, (slots, slots), 1).astype(jnp.float32)
    mine = lax.broadcasted_iota(jnp.int32, (slots, slots), 0).astype(jnp.float32)
    spare = float(comp_tiles * targ_group)
    same = down == across

    def count(mask, axis):
        return jnp.sum(jnp.where(mask, 1.0, 0.0), axis=axis, keepdims=True)

    earlier = count(same & (mine < at), 0)
    groups = jnp.floor((count(same, 0) + (GROUP - 1.0)) * (1.0 / GROUP))
    opens = (earlier == 0.0) & (across[:1] < spare)
    before = across < down
    rank = jnp.sum(jnp.where(before & opens, 1.0, 0.0), axis=1, keepdims=True)
    first = jnp.sum(jnp.where(before & opens, groups, 0.0), axis=1, keepdims=True)
    pair = down[:, :1]
    earlier = count(same & (at < mine), 1)
    alive = pair < spare
    opens = (earlier == 0.0) & alive
    step = jnp.floor(earlier * (1.0 / GROUP))
    place = jnp.where(alive, first + step, -1.0)
    member = earlier - GROUP * step
    groups = jnp.floor((count(same, 1) + (GROUP - 1.0)) * (1.0 / GROUP))

    def pick(mask, value, rest):
        return jnp.sum(jnp.where(mask, value - rest, 0.0), axis=0, keepdims=True) + rest

    here = place == at
    comp_tile = jnp.floor((pair + 0.5) * (1.0 / targ_group))
    rows = [pick(here & (member == n), mine[:, :1], float(slots)) for n in range(GROUP)]
    rows.append(pick(here & (member == 0.0), rank, float(pairs)))
    here = (rank == at) & opens
    rows.append(pick(here, comp_tile, float(comp_tiles)))
    rows.append(pick(here, pair - targ_group * comp_tile, float(targ_tiles)))
    totals = [jnp.sum(jnp.where(opens, n, 0.0), axis=0, keepdims=True) for n in (groups, 1.0)]
    rows.append(jnp.where(at[:1] == 0.0, totals[0], totals[1]))
    lists_ref[...] = jnp.concatenate(rows, axis=0).astype(jnp.int32)

    for index in range(chunks):

        @pl.when(index * chunk < live_ref[0])
        def _():
            for copy in copies(index):
                copy.wait()


def force_kernel(cols, rows, lists_ref, *refs):
    comp_firsts, comp_seconds, refs = refs[: cols // 2], refs[cols // 2], refs[cols // 2 + 1 :]
    targ_blocks, refs = refs[:rows], refs[rows:]
    values_ref, weight_ref, refs = refs[0], refs[1], refs[2:]
    comp_keep, comp_send, refs = refs[0], refs[1], refs[2:]
    targ_outs, refs = refs[:rows], refs[rows:]
    pred, total, comp_tiles, comp_flip, targ_tiles, targ_flip, comp_acc, targ_acc = refs
    side = values_ref.shape[1]
    comp_rows, targ_rows = comp_firsts[0].shape[0], targ_blocks[0].shape[0]
    comp_per, targ_per = comp_rows // side, targ_rows // side

    def fill(spot, tile, tiles, flip, acc):
        tiles[spot] = tile
        flip[spot] = tile.T
        acc[spot] = jnp.zeros(acc.shape[1:], acc.dtype)

    for n in range(rows):
        for i in range(targ_per):
            tile = targ_blocks[n][i * side : (i + 1) * side]
            fill(n * targ_per + i, tile, targ_tiles, targ_flip, targ_acc)
    for n in range(cols):
        for i in range(comp_per):
            start = (n // 2 * comp_per * (n % 2) + i) * side
            tile = (comp_seconds if n % 2 else comp_firsts[n // 2])[start : start + side]
            fill(n * comp_per + i, tile, comp_tiles, comp_flip, comp_acc)

    def steps(count):
        return lax.div(count + (UNROLL - 1), UNROLL)

    def pair_at(step):
        spots = [step * UNROLL + n for n in range(UNROLL)]
        return [(spot, lists_ref[GROUP + 1, spot], lists_ref[GROUP + 2, spot]) for spot in spots]

    last = pred.shape[0] - 1
    pairs, groups = lists_ref[GROUP + 3, 1], lists_ref[GROUP + 3, 0]

    def predict(step, unused):
        blocks = [
            (spot, jnp.dot(comp_tiles[i], targ_flip[j], preferred_element_type=jnp.float32))
            for spot, i, j in pair_at(step)
        ]
        for spot, block in blocks:
            spot = jnp.minimum(spot, last)
            pred[spot] = block.astype(pred.dtype)
            total[spot] = jnp.zeros(total.shape[1:], total.dtype)
        return unused

    lax.fori_loop(0, steps(pairs), predict, 0)

    one = degrees_free * noise_scale * noise_scale

    def weigh(step, unused):
        sums = []
        for n in range(UNROLL):
            group = step * UNROLL + n
            spot = lists_ref[GROUP, group]
            guess = pred[spot].astype(jnp.float32)
            whole = None
            for m in range(GROUP):
                slot = lists_ref[m, group]
                resid = values_ref[slot].astype(jnp.float32) - guess
                inverse = pl.reciprocal(one + resid * resid, approx=True)
                scaled = resid * weight_ref[slot].astype(jnp.float32) * inverse
                whole = scaled if whole is None else whole + scaled
            sums.append((spot, whole))
        for spot, whole in sums:
            total[spot] += whole
        return unused

    lax.fori_loop(0, steps(groups), weigh, 0)

    def gather(step, unused):
        parts = []
        for spot, i, j in pair_at(step):
            weights = total[jnp.minimum(spot, last)].astype(jnp.bfloat16)
            comp_part = jnp.dot(weights, targ_tiles[j], preferred_element_type=jnp.float32)
            targ_part = jnp.dot(comp_flip[i], weights, preferred_element_type=jnp.float32)
            parts.append((i, comp_part, j, targ_part))
        for i, comp_part, j, targ_part in parts:
            comp_acc[i] += comp_part
            targ_acc[j] += targ_part
        return unused

    lax.fori_loop(0, steps(pairs), gather, 0)

    gain = degrees_free + 1.0
    for n in range(cols):
        out = comp_send if n % 2 else comp_keep
        for i in range(comp_per):
            part = comp_acc[n * comp_per + i] * gain
            out[n // 2, i * side : (i + 1) * side] = part.astype(out.dtype)
    for n in range(rows):
        out = targ_outs[n]
        for i in range(targ_per):
            part = targ_acc[n * targ_per + i] * gain
            out[i * side : (i + 1) * side] = part.T.astype(out.dtype)


smem = pl.BlockSpec(memory_space=pltpu.SMEM)
vmem = pl.BlockSpec(memory_space=pltpu.VMEM)
hbm = pl.BlockSpec(memory_space=pltpu.HBM)


def load_tiles(pairs, live, targ_group, shape, values, weight):
    slots, side, width = values.shape
    chunks = slots // math.gcd(slots, 16)
    held = pltpu.VMEM((slots + 1, side, width), values.dtype)
    values, weight = (pltpu.with_memory_space_constraint(x, pltpu.HBM) for x in (values, weight))
    return pl.pallas_call(
        functools.partial(load_kernel, targ_group, shape),
        out_shape=[held, held, jax.ShapeDtypeStruct((GROUP + 4, slots), jnp.int32)],
        in_specs=[vmem, smem, hbm, hbm],
        out_specs=[vmem] * 3,
        scratch_shapes=[pltpu.SemaphoreType.DMA((2, chunks))],
        compiler_params=pltpu.CompilerParams(vmem_limit_bytes=24 * 2**20),
        name="tile_load",
    )(pairs, live, values, weight)


def local_grads(lists, comp_firsts, comp_seconds, targ_blocks, values, weight, pairs):
    cols, rows = 2 * len(comp_firsts), len(targ_blocks)
    comp_rows, rank = comp_firsts[0].shape
    targ_rows = targ_blocks[0].shape[0]
    side = values.shape[1]
    comp_tiles, targ_tiles = cols * comp_rows // side, rows * targ_rows // side
    comp_shape = jax.ShapeDtypeStruct((cols // 2, comp_rows, rank), jnp.bfloat16)
    targ_shape = jax.ShapeDtypeStruct((targ_rows, rank), jnp.bfloat16)
    held = (pairs + 1) * side * side * 6 + (comp_tiles + targ_tiles + 2) * side * rank * 8
    held += 4 * values.size
    outs = pl.pallas_call(
        functools.partial(force_kernel, cols, rows),
        out_shape=[comp_shape] * 2 + [targ_shape] * rows,
        in_specs=[smem] + [vmem] * (cols // 2 + 1 + rows + 2),
        out_specs=[vmem] * (2 + rows),
        scratch_shapes=[
            pltpu.VMEM((pairs + 1, side, side), jnp.bfloat16),
            pltpu.VMEM((pairs + 1, side, side), jnp.float32),
            pltpu.VMEM((comp_tiles + 1, side, rank), jnp.bfloat16),
            pltpu.VMEM((comp_tiles + 1, rank, side), jnp.bfloat16),
            pltpu.VMEM((targ_tiles + 1, side, rank), jnp.bfloat16),
            pltpu.VMEM((targ_tiles + 1, rank, side), jnp.bfloat16),
            pltpu.VMEM((comp_tiles + 1, side, rank), jnp.float32),
            pltpu.VMEM((targ_tiles + 1, rank, side), jnp.float32),
        ],
        compiler_params=pltpu.CompilerParams(vmem_limit_bytes=held + 4 * 2**20),
        name="tile_force",
    )(lists, *comp_firsts, comp_seconds, *targ_blocks, values, weight)
    return outs[0], outs[1], outs[2:]


def swap(block, axis, offset):
    size = lax.axis_size(axis)
    return lax.ppermute(block, axis, [(i, i ^ offset) for i in range(size)])


def spread(block, axis):
    return [block] + [swap(block, axis, offset) for offset in range(1, lax.axis_size(axis))]


def collect(blocks, axis):
    whole = blocks[0].astype(jnp.float32)
    for offset, block in enumerate(blocks[1:]):
        whole = whole + swap(block, axis, offset + 1).astype(jnp.float32)
    return whole


def spread_pairs(block, axis):
    firsts = [block]
    firsts += [swap(block, axis, offset) for offset in range(2, lax.axis_size(axis), 2)]
    seconds = swap(jnp.concatenate(firsts), axis, 1)
    return firsts, seconds


def collect_pairs(keep, send, axis):
    got = swap(send, axis, 1)
    both = [
        keep[n].astype(jnp.float32) + got[n].astype(jnp.float32) for n in range(keep.shape[0])
    ]
    whole = both[0]
    for n, block in enumerate(both[1:]):
        whole = whole + swap(block.astype(keep.dtype), axis, 2 * n + 2).astype(jnp.float32)
    return whole


def body(
    compound_pos,
    compound_mom,
    target_pos,
    target_mom,
    tile_rows,
    tile_cols,
    tile_count,
    tile_values,
    tile_weight,
):
    side = tile_values.shape[2]
    comp_per = compound_pos.shape[0] // side
    targ_per = target_pos.shape[0] // side
    cols, rows = lax.axis_size("col"), lax.axis_size("row")
    col_index, row_index = lax.axis_index("col"), lax.axis_index("row")
    assert cols & (cols - 1) == 0 and rows & (rows - 1) == 0
    comp_local = tile_rows[0] - row_index * (cols * comp_per)
    comp_place = ((comp_local // comp_per) ^ col_index) * comp_per + comp_local % comp_per
    holder = tile_cols[0] // targ_per // cols
    targ_place = (holder ^ row_index) * targ_per + tile_cols[0] % targ_per
    targ_group = rows * targ_per
    alive = jnp.arange(tile_values.shape[1], dtype=jnp.int32) < tile_count[0]
    spare = cols * comp_per * targ_group
    slots = jnp.where(alive, comp_place * targ_group + targ_place, spare)

    shape = (min(spare, slots.shape[0]), cols * comp_per, targ_group)
    values, weight, lists = load_tiles(
        slots[None], tile_count, targ_group, shape, tile_values[0], tile_weight[0]
    )

    def forces(comp, targ):
        comp_keep, comp_send, targ_parts = local_grads(
            lists,
            *spread_pairs(comp.astype(jnp.bfloat16), "col"),
            spread(targ.astype(jnp.bfloat16), "row"),
            values,
            weight,
            shape[0],
        )
        comp_sum = collect_pairs(comp_keep, comp_send, "col")
        targ_sum = collect(targ_parts, "row")
        return comp_sum - prior_weight * comp, targ_sum - prior_weight * targ

    places = (compound_pos, target_pos)
    speeds = (compound_mom, target_mom)
    push = forces(*places)
    for leap in range(LEAPS):
        scale = (0.5 if leap == 0 else 1.0) * step_size
        speeds = tuple(p + scale * f for p, f in zip(speeds, push))
        places = tuple(q + step_size * p for q, p in zip(places, speeds))
        push = forces(*places)
    speeds = tuple(p + 0.5 * step_size * f for p, f in zip(speeds, push))
    return (places[0], speeds[0], places[1], speeds[1])


def solution(mesh):
    split = P(("row", "col"), None)
    tiles = P(("row", "col"), None, None, None)
    return jax.shard_map(
        body,
        mesh=mesh,
        in_specs=(split,) * 6 + (P(("row", "col")), tiles, tiles),
        out_specs=(split,) * 4,
        check_vma=False,
    )
```

profile of v0, /device:TPU:0, one launch (start us, length us, event | category | flops | bytes accessed | tf_op | source)
XLA Modules:
  0.0 116.0 jit_solution(14562880367782700042)
XLA Ops:
  1.5 3.9 %collective-permute-start.2 = (bf16[256,128]{1,0:T(8,128)(2,1)S(1)}, bf16[256,128]{1,0:T(8,128)(2,1)S(1)}, u32[]{:S(2)}, u32[]{:S(2)}) collective-permute-start(bf16[256,128]{1,0:T(8,128)(2,1)S(1)} %convert_element_type.231.refs_0_), channel_id=1, source_target_pairs={{0,6},{1,7},{2,4},{3,5},{4,2},{5,3},{6,0},{7,1},{8,14},{9,15},{10,... | collective-permute-start | bytes 196616 | tf_op jit(solution)/shard_map/ppermute | solution.py:245
  6.1 1.6 %collective-permute-done.2.refs_3_ = bf16[256,128]{1,0:T(8,128)(2,1)S(1)} collective-permute-done((bf16[256,128]{1,0:T(8,128)(2,1)S(1)}, bf16[256,128]{1,0:T(8,128)(2,1)S(1)}, u32[]{:S(2)}, u32[]{:S(2)}) %collective-permute-start.2) | collective-permute-done | bytes 65568 | tf_op jit(solution)/shard_map/ppermute | solution.py:245
  7.7 2.0 %collective-permute-done.1.refs_2_ = bf16[256,128]{1,0:T(8,128)(2,1)S(1)} collective-permute-done((bf16[256,128]{1,0:T(8,128)(2,1)S(1)}, bf16[256,128]{1,0:T(8,128)(2,1)S(1)}, u32[]{:S(2)}, u32[]{:S(2)}) %collective-permute-start.1) | collective-permute-done | bytes 65568 | tf_op jit(solution)/shard_map/ppermute | solution.py:245
  11.2 3.6 %collective-permute-start.6 = (bf16[256,128]{1,0:T(8,128)(2,1)S(1)}, bf16[256,128]{1,0:T(8,128)(2,1)S(1)}, u32[]{:S(2)}, u32[]{:S(2)}) collective-permute-start(bf16[256,128]{1,0:T(8,128)(2,1)S(1)} %convert_element_type.232.refs_5_), channel_id=1, source_target_pairs={{0,24},{8,16},{16,8},{24,0},{1,25},{9,17},{17,9},{25,1},{2,26},{10... | collective-permute-start | bytes 196616 | tf_op jit(solution)/shard_map/ppermute | solution.py:245
  17.0 5.5 %tile_load.1 = (bf16[257,128,128]{2,1,0:T(8,128)(2,1)S(1)}, bf16[257,128,128]{2,1,0:T(8,128)(2,1)S(1)}, s32[8,256]{1,0:T(8,128)S(1)}) custom-call(s32[1,256]{1,0:T(1,128)S(1)} %compare_select_fusion.pair_ref, s32[1]{0:T(128)} %copy.13.live_ref, bf16[256,128,128]{2,1,0:T(8,128)(2,1)} %bitcast.64, bf16[256,128,128]{2,1,0:T(8,128)(2,1)} %bitcast.65), custom_call_target="tpu_custom_call" | custom-call | tf_op jit(solution)/shard_map/tile_load/pallas_call | solution.py:201
  22.6 7.8 %tile_force.3 = (bf16[4,256,128]{2,1,0:T(8,128)(2,1)S(1)}, bf16[4,256,128]{2,1,0:T(8,128)(2,1)S(1)}, bf16[256,128]{1,0:T(8,128)(2,1)S(1)}, bf16[256,128]{1,0:T(8...) custom-call(s32[8,256]{1,0:T(8,128)S(1)} %get-tuple-element.25.lists_ref, ...), custom_call_target="tpu_custom_call" | custom-call | tf_op jit(solution)/shard_map/tile_force/pallas_call | solution.py:222
  30.4 1.5 %collective-permute-done.7 = bf16[4,256,128]{2,1,0:T(8,128)(2,1)S(1)} collective-permute-done((bf16[4,256,128]{2,1,0:T(8,128)(2,1)S(1)}, bf16[4,256,128]{2,1,0:T(8,128)(2,1)S(1)}, u32[]{:S(2)}, u32[]{:S(2)}) %collective-permute-start.7) | collective-permute-done | bytes 262176 | tf_op jit(solution)/shard_map/ppermute | solution.py:245
  32.1 3.4 %collective-permute-start.9 = (bf16[256,128]{1,0:T(8,128)(2,1)S(1)}, bf16[256,128]{1,0:T(8,128)(2,1)S(1)}, u32[]{:S(2)}, u32[]{:S(2)}) collective-permute-start(bf16[256,128]{1,0:T(8,128)(2,1)S(1)} %get-tuple-element.62), channel_id=1, source_target_pairs={{0,4},{1,5},{2,6},{3,7},{4,0},{5,1},{6,2},{7,3},{8,12},{9,13},{10,... | collective-permute-start | bytes 196616 | tf_op jit(solution)/shard_map/ppermute | solution.py:245
  38.7 1.5 %collective-permute-start.13 = (bf16[256,128]{1,0:T(8,128)(2,1)S(1)}, bf16[256,128]{1,0:T(8,128)(2,1)S(1)}, u32[]{:S(2)}, u32[]{:S(2)}) collective-permute-start(bf16[256,128]{1,0:T(8,128)(2,1)S(1)} %get-tuple-element.52.refs_0_), channel_id=1, source_target_pairs={{0,6},{1,7},{2,4},{3,5},{4,2},{5,3},{6,0},{7,1},{8,14},{9,15},{10,... | collective-permute-start | bytes 196616 | tf_op jit(solution)/shard_map/ppermute | solution.py:245
  42.2 1.6 %collective-permute-start.15 = (bf16[256,128]{1,0:T(8,128)(2,1)S(1)}, bf16[256,128]{1,0:T(8,128)(2,1)S(1)}, u32[]{:S(2)}, u32[]{:S(2)}) collective-permute-start(bf16[256,128]{1,0:T(8,128)(2,1)S(1)} %get-tuple-element.31), channel_id=1, source_target_pairs={{0,8},{8,0},{16,24},{24,16},{1,9},{9,1},{17,25},{25,17},{2,10},{10... | collective-permute-start | bytes 196616 | tf_op jit(solution)/shard_map/ppermute | solution.py:245
  43.8 2.4 %collective-permute-start.16 = (bf16[256,128]{1,0:T(8,128)(2,1)S(1)}, bf16[256,128]{1,0:T(8,128)(2,1)S(1)}, u32[]{:S(2)}, u32[]{:S(2)}) collective-permute-start(bf16[256,128]{1,0:T(8,128)(2,1)S(1)} %get-tuple-element.32), channel_id=1, source_target_pairs={{0,16},{8,24},{16,0},{24,8},{1,17},{9,25},{17,1},{25,9},{2,18},{10... | collective-permute-start | bytes 196616 | tf_op jit(solution)/shard_map/ppermute | solution.py:245
  46.1 1.8 %collective-permute-start.17 = (bf16[256,128]{1,0:T(8,128)(2,1)S(1)}, bf16[256,128]{1,0:T(8,128)(2,1)S(1)}, u32[]{:S(2)}, u32[]{:S(2)}) collective-permute-start(bf16[256,128]{1,0:T(8,128)(2,1)S(1)} %get-tuple-element.33), channel_id=1, source_target_pairs={{0,24},{8,16},{16,8},{24,0},{1,25},{9,17},{17,9},{25,1},{2,26},{10... | collective-permute-start | bytes 196616 | tf_op jit(solution)/shard_map/ppermute | solution.py:245
  48.0 2.3 %collective-permute-done.16 = bf16[256,128]{1,0:T(8,128)(2,1)S(1)} collective-permute-done((bf16[256,128]{1,0:T(8,128)(2,1)S(1)}, bf16[256,128]{1,0:T(8,128)(2,1)S(1)}, u32[]{:S(2)}, u32[]{:S(2)}) %collective-permute-start.16) | collective-permute-done | bytes 65568 | tf_op jit(solution)/shard_map/ppermute | solution.py:245
  50.4 1.9 %collective-permute-done.17 = bf16[256,128]{1,0:T(8,128)(2,1)S(1)} collective-permute-done((bf16[256,128]{1,0:T(8,128)(2,1)S(1)}, bf16[256,128]{1,0:T(8,128)(2,1)S(1)}, u32[]{:S(2)}, u32[]{:S(2)}) %collective-permute-start.17) | collective-permute-done | bytes 65568 | tf_op jit(solution)/shard_map/ppermute | solution.py:245
  52.3 2.2 %collective-permute-start.20 = (bf16[256,128]{1,0:T(8,128)(2,1)S(1)}, bf16[256,128]{1,0:T(8,128)(2,1)S(1)}, u32[]{:S(2)}, u32[]{:S(2)}) collective-permute-start(bf16[256,128]{1,0:T(8,128)(2,1)S(1)} %get-tuple-element.50.refs_5_), channel_id=1, source_target_pairs={{0,24},{8,16},{16,8},{24,0},{1,25},{9,17},{17,9},{25,1},{2,26},{10... | collective-permute-start | bytes 196616 | tf_op jit(solution)/shard_map/ppermute | solution.py:245
  54.7 2.1 %collective-permute-start.18 = (bf16[256,128]{1,0:T(8,128)(2,1)S(1)}, bf16[256,128]{1,0:T(8,128)(2,1)S(1)}, u32[]{:S(2)}, u32[]{:S(2)}) collective-permute-start(bf16[256,128]{1,0:T(8,128)(2,1)S(1)} %get-tuple-element.50.refs_5_), channel_id=1, source_target_pairs={{0,8},{8,0},{16,24},{24,16},{1,9},{9,1},{17,25},{25,17},{2,10},{10... | collective-permute-start | bytes 196616 | tf_op jit(solution)/shard_map/ppermute | solution.py:245
  56.8 1.9 %collective-permute-done.20.refs_8_ = bf16[256,128]{1,0:T(8,128)(2,1)S(1)} collective-permute-done((bf16[256,128]{1,0:T(8,128)(2,1)S(1)}, bf16[256,128]{1,0:T(8,128)(2,1)S(1)}, u32[]{:S(2)}, u32[]{:S(2)}) %collective-permute-start.20) | collective-permute-done | bytes 65568 | tf_op jit(solution)/shard_map/ppermute | solution.py:245
  58.7 1.4 %collective-permute-done.19.refs_7_ = bf16[256,128]{1,0:T(8,128)(2,1)S(1)} collective-permute-done((bf16[256,128]{1,0:T(8,128)(2,1)S(1)}, bf16[256,128]{1,0:T(8,128)(2,1)S(1)}, u32[]{:S(2)}, u32[]{:S(2)}) %collective-permute-start.19) | collective-permute-done | bytes 65568 | tf_op jit(solution)/shard_map/ppermute | solution.py:245
  60.2 7.8 %tile_force.4 = (bf16[4,256,128]{2,1,0:T(8,128)(2,1)S(1)}, bf16[4,256,128]{2,1,0:T(8,128)(2,1)S(1)}, bf16[256,128]{1,0:T(8,128)(2,1)S(1)}, bf16[256,128]{1,0:T(8...) custom-call(s32[8,256]{1,0:T(8,128)S(1)} %get-tuple-element.25.lists_ref, ...), custom_call_target="tpu_custom_call" | custom-call | tf_op jit(solution)/shard_map/tile_force/pallas_call | solution.py:222
  68.0 1.5 %collective-permute-done.21 = bf16[4,256,128]{2,1,0:T(8,128)(2,1)S(1)} collective-permute-done((bf16[4,256,128]{2,1,0:T(8,128)(2,1)S(1)}, bf16[4,256,128]{2,1,0:T(8,128)(2,1)S(1)}, u32[]{:S(2)}, u32[]{:S(2)}) %collective-permute-start.21) | collective-permute-done | bytes 262176 | tf_op jit(solution)/shard_map/ppermute | solution.py:245
  69.7 3.4 %collective-permute-start.23 = (bf16[256,128]{1,0:T(8,128)(2,1)S(1)}, bf16[256,128]{1,0:T(8,128)(2,1)S(1)}, u32[]{:S(2)}, u32[]{:S(2)}) collective-permute-start(bf16[256,128]{1,0:T(8,128)(2,1)S(1)} %get-tuple-element.59), channel_id=1, source_target_pairs={{0,4},{1,5},{2,6},{3,7},{4,0},{5,1},{6,2},{7,3},{8,12},{9,13},{10,... | collective-permute-start | bytes 196616 | tf_op jit(solution)/shard_map/ppermute | solution.py:245
  76.3 1.5 %collective-permute-start.27 = (bf16[256,128]{1,0:T(8,128)(2,1)S(1)}, bf16[256,128]{1,0:T(8,128)(2,1)S(1)}, u32[]{:S(2)}, u32[]{:S(2)}) collective-permute-start(bf16[256,128]{1,0:T(8,128)(2,1)S(1)} %get-tuple-element.48.refs_0_), channel_id=1, source_target_pairs={{0,6},{1,7},{2,4},{3,5},{4,2},{5,3},{6,0},{7,1},{8,14},{9,15},{10,... | collective-permute-start | bytes 196616 | tf_op jit(solution)/shard_map/ppermute | solution.py:245
  82.1 2.1 %collective-permute-start.31 = (bf16[256,128]{1,0:T(8,128)(2,1)S(1)}, bf16[256,128]{1,0:T(8,128)(2,1)S(1)}, u32[]{:S(2)}, u32[]{:S(2)}) collective-permute-start(bf16[256,128]{1,0:T(8,128)(2,1)S(1)} %get-tuple-element.39), channel_id=1, source_target_pairs={{0,24},{8,16},{16,8},{24,0},{1,25},{9,17},{17,9},{25,1},{2,26},{10... | collective-permute-start | bytes 196616 | tf_op jit(solution)/shard_map/ppermute | solution.py:245
  84.4 3.0 %collective-permute-done.30 = bf16[256,128]{1,0:T(8,128)(2,1)S(1)} collective-permute-done((bf16[256,128]{1,0:T(8,128)(2,1)S(1)}, bf16[256,128]{1,0:T(8,128)(2,1)S(1)}, u32[]{:S(2)}, u32[]{:S(2)}) %collective-permute-start.30) | collective-permute-done | bytes 65568 | tf_op jit(solution)/shard_map/ppermute | solution.py:245
  88.4 2.1 %collective-permute-start.34 = (bf16[256,128]{1,0:T(8,128)(2,1)S(1)}, bf16[256,128]{1,0:T(8,128)(2,1)S(1)}, u32[]{:S(2)}, u32[]{:S(2)}) collective-permute-start(bf16[256,128]{1,0:T(8,128)(2,1)S(1)} %get-tuple-element.46.refs_5_), channel_id=1, source_target_pairs={{0,24},{8,16},{16,8},{24,0},{1,25},{9,17},{17,9},{25,1},{2,26},{10... | collective-permute-start | bytes 196616 | tf_op jit(solution)/shard_map/ppermute | solution.py:245
  91.0 1.8 %collective-permute-start.32 = (bf16[256,128]{1,0:T(8,128)(2,1)S(1)}, bf16[256,128]{1,0:T(8,128)(2,1)S(1)}, u32[]{:S(2)}, u32[]{:S(2)}) collective-permute-start(bf16[256,128]{1,0:T(8,128)(2,1)S(1)} %get-tuple-element.46.refs_5_), channel_id=1, source_target_pairs={{0,8},{8,0},{16,24},{24,16},{1,9},{9,1},{17,25},{25,17},{2,10},{10... | collective-permute-start | bytes 196616 | tf_op jit(solution)/shard_map/ppermute | solution.py:245
  92.9 1.7 %collective-permute-done.34.refs_8_ = bf16[256,128]{1,0:T(8,128)(2,1)S(1)} collective-permute-done((bf16[256,128]{1,0:T(8,128)(2,1)S(1)}, bf16[256,128]{1,0:T(8,128)(2,1)S(1)}, u32[]{:S(2)}, u32[]{:S(2)}) %collective-permute-start.34) | collective-permute-done | bytes 65568 | tf_op jit(solution)/shard_map/ppermute | solution.py:245
  94.5 1.5 %collective-permute-done.33.refs_7_ = bf16[256,128]{1,0:T(8,128)(2,1)S(1)} collective-permute-done((bf16[256,128]{1,0:T(8,128)(2,1)S(1)}, bf16[256,128]{1,0:T(8,128)(2,1)S(1)}, u32[]{:S(2)}, u32[]{:S(2)}) %collective-permute-start.33) | collective-permute-done | bytes 65568 | tf_op jit(solution)/shard_map/ppermute | solution.py:245
  96.0 7.8 %tile_force.5 = (bf16[4,256,128]{2,1,0:T(8,128)(2,1)S(1)}, bf16[4,256,128]{2,1,0:T(8,128)(2,1)S(1)}, bf16[256,128]{1,0:T(8,128)(2,1)S(1)}, bf16[256,128]{1,0:T(8...) custom-call(s32[8,256]{1,0:T(8,128)S(1)} %get-tuple-element.25.lists_ref, ...), custom_call_target="tpu_custom_call" | custom-call | tf_op jit(solution)/shard_map/tile_force/pallas_call | solution.py:222
  105.1 3.2 %collective-permute-start.41 = (bf16[256,128]{1,0:T(8,128)(2,1)S(1)}, bf16[256,128]{1,0:T(8,128)(2,1)S(1)}, u32[]{:S(2)}, u32[]{:S(2)}) collective-permute-start(bf16[256,128]{1,0:T(8,128)(2,1)S(1)} %get-tuple-element.45), channel_id=1, source_target_pairs={{0,24},{8,16},{16,8},{24,0},{1,25},{9,17},{17,9},{25,1},{2,26},{10... | collective-permute-start | bytes 196616 | tf_op jit(solution)/shard_map/ppermute | solution.py:245
  109.2 1.4 %collective-permute-start.38 = (bf16[256,128]{1,0:T(8,128)(2,1)S(1)}, bf16[256,128]{1,0:T(8,128)(2,1)S(1)}, u32[]{:S(2)}, u32[]{:S(2)}) collective-permute-start(bf16[256,128]{1,0:T(8,128)(2,1)S(1)} %get-tuple-element.55), channel_id=1, source_target_pairs={{0,6},{1,7},{2,4},{3,5},{4,2},{5,3},{6,0},{7,1},{8,14},{9,15},{10,... | collective-permute-start | bytes 196616 | tf_op jit(solution)/shard_map/ppermute | solution.py:245
  110.5 1.4 %collective-permute-start.37 = (bf16[256,128]{1,0:T(8,128)(2,1)S(1)}, bf16[256,128]{1,0:T(8,128)(2,1)S(1)}, u32[]{:S(2)}, u32[]{:S(2)}) collective-permute-start(bf16[256,128]{1,0:T(8,128)(2,1)S(1)} %get-tuple-element.56), channel_id=1, source_target_pairs={{0,4},{1,5},{2,6},{3,7},{4,0},{5,1},{6,2},{7,3},{8,12},{9,13},{10,... | collective-permute-start | bytes 196616 | tf_op jit(solution)/shard_map/ppermute | solution.py:245
  (83 shorter events, 26.0 us)
Async XLA Ops:
  1.5 6.1 %collective-permute-start.2 = (bf16[256,128]{1,0:T(8,128)(2,1)S(1)}, bf16[256,128]{1,0:T(8,128)(2,1)S(1)}, u32[]{:S(2)}, u32[]{:S(2)}) collective-permute-start(bf16[256,128]{1,0:T(8,128)(2,1)S(1)} %convert_element_type.231.refs_0_), channel_id=1, source_target_pairs={{0,6},{1,7},{2,4},{3,5},{4,2},{5,3},{6,0},{7,1},{8,14},{9,15},{10,... | collective-permute-start | bytes 196616 | tf_op jit(solution)/shard_map/ppermute | solution.py:245
  10.2 12.3 %collective-permute-start.3 = (bf16[1024,128]{1,0:T(8,128)(2,1)S(1)}, bf16[1024,128]{1,0:T(8,128)(2,1)S(1)}, u32[]{:S(2)}, u32[]{:S(2)}) collective-permute-start(bf16[1024,128]{1,0:T(8,128)(2,1)S(1)} %pad_maximum_fusion), channel_id=1, source_target_pairs={{0,1},{1,0},{2,3},{3,2},{4,5},{5,4},{6,7},{7,6},{8,9},{9,8},{10,11... | collective-permute-start | bytes 786440 | tf_op jit(solution)/shard_map/ppermute | solution.py:245
  11.2 11.2 %collective-permute-start.6 = (bf16[256,128]{1,0:T(8,128)(2,1)S(1)}, bf16[256,128]{1,0:T(8,128)(2,1)S(1)}, u32[]{:S(2)}, u32[]{:S(2)}) collective-permute-start(bf16[256,128]{1,0:T(8,128)(2,1)S(1)} %convert_element_type.232.refs_5_), channel_id=1, source_target_pairs={{0,24},{8,16},{16,8},{24,0},{1,25},{9,17},{17,9},{25,1},{2,26},{10... | collective-permute-start | bytes 196616 | tf_op jit(solution)/shard_map/ppermute | solution.py:245
  14.8 7.6 %collective-permute-start.5 = (bf16[256,128]{1,0:T(8,128)(2,1)S(1)}, bf16[256,128]{1,0:T(8,128)(2,1)S(1)}, u32[]{:S(2)}, u32[]{:S(2)}) collective-permute-start(bf16[256,128]{1,0:T(8,128)(2,1)S(1)} %convert_element_type.232.refs_5_), channel_id=1, source_target_pairs={{0,16},{8,24},{16,0},{24,8},{1,17},{9,25},{17,1},{25,9},{2,18},{10... | collective-permute-start | bytes 196616 | tf_op jit(solution)/shard_map/ppermute | solution.py:245
  14.8 7.7 %collective-permute-start.4 = (bf16[256,128]{1,0:T(8,128)(2,1)S(1)}, bf16[256,128]{1,0:T(8,128)(2,1)S(1)}, u32[]{:S(2)}, u32[]{:S(2)}) collective-permute-start(bf16[256,128]{1,0:T(8,128)(2,1)S(1)} %convert_element_type.232.refs_5_), channel_id=1, source_target_pairs={{0,8},{8,0},{16,24},{24,16},{1,9},{9,1},{17,25},{25,17},{2,10},{10... | collective-permute-start | bytes 196616 | tf_op jit(solution)/shard_map/ppermute | solution.py:245
  32.1 5.3 %collective-permute-start.10 = (bf16[256,128]{1,0:T(8,128)(2,1)S(1)}, bf16[256,128]{1,0:T(8,128)(2,1)S(1)}, u32[]{:S(2)}, u32[]{:S(2)}) collective-permute-start(bf16[256,128]{1,0:T(8,128)(2,1)S(1)} %get-tuple-element.61), channel_id=1, source_target_pairs={{0,6},{1,7},{2,4},{3,5},{4,2},{5,3},{6,0},{7,1},{8,14},{9,15},{10,... | collective-permute-start | bytes 196616 | tf_op jit(solution)/shard_map/ppermute | solution.py:245
  32.1 6.4 %collective-permute-start.9 = (bf16[256,128]{1,0:T(8,128)(2,1)S(1)}, bf16[256,128]{1,0:T(8,128)(2,1)S(1)}, u32[]{:S(2)}, u32[]{:S(2)}) collective-permute-start(bf16[256,128]{1,0:T(8,128)(2,1)S(1)} %get-tuple-element.62), channel_id=1, source_target_pairs={{0,4},{1,5},{2,6},{3,7},{4,0},{5,1},{6,2},{7,3},{8,12},{9,13},{10,... | collective-permute-start | bytes 196616 | tf_op jit(solution)/shard_map/ppermute | solution.py:245
  38.7 7.5 %collective-permute-start.13 = (bf16[256,128]{1,0:T(8,128)(2,1)S(1)}, bf16[256,128]{1,0:T(8,128)(2,1)S(1)}, u32[]{:S(2)}, u32[]{:S(2)}) collective-permute-start(bf16[256,128]{1,0:T(8,128)(2,1)S(1)} %get-tuple-element.52.refs_0_), channel_id=1, source_target_pairs={{0,6},{1,7},{2,4},{3,5},{4,2},{5,3},{6,0},{7,1},{8,14},{9,15},{10,... | collective-permute-start | bytes 196616 | tf_op jit(solution)/shard_map/ppermute | solution.py:245
  40.2 7.8 %collective-permute-start.12 = (bf16[256,128]{1,0:T(8,128)(2,1)S(1)}, bf16[256,128]{1,0:T(8,128)(2,1)S(1)}, u32[]{:S(2)}, u32[]{:S(2)}) collective-permute-start(bf16[256,128]{1,0:T(8,128)(2,1)S(1)} %get-tuple-element.52.refs_0_), channel_id=1, source_target_pairs={{0,4},{1,5},{2,6},{3,7},{4,0},{5,1},{6,2},{7,3},{8,12},{9,13},{10,... | collective-permute-start | bytes 196616 | tf_op jit(solution)/shard_map/ppermute | solution.py:245
  41.1 6.8 %collective-permute-start.11 = (bf16[256,128]{1,0:T(8,128)(2,1)S(1)}, bf16[256,128]{1,0:T(8,128)(2,1)S(1)}, u32[]{:S(2)}, u32[]{:S(2)}) collective-permute-start(bf16[256,128]{1,0:T(8,128)(2,1)S(1)} %get-tuple-element.52.refs_0_), channel_id=1, source_target_pairs={{0,2},{1,3},{2,0},{3,1},{4,6},{5,7},{6,4},{7,5},{8,10},{9,11},{10,... | collective-permute-start | bytes 196616 | tf_op jit(solution)/shard_map/ppermute | solution.py:245
  42.2 5.8 %collective-permute-start.15 = (bf16[256,128]{1,0:T(8,128)(2,1)S(1)}, bf16[256,128]{1,0:T(8,128)(2,1)S(1)}, u32[]{:S(2)}, u32[]{:S(2)}) collective-permute-start(bf16[256,128]{1,0:T(8,128)(2,1)S(1)} %get-tuple-element.31), channel_id=1, source_target_pairs={{0,8},{8,0},{16,24},{24,16},{1,9},{9,1},{17,25},{25,17},{2,10},{10... | collective-permute-start | bytes 196616 | tf_op jit(solution)/shard_map/ppermute | solution.py:245
  43.8 6.6 %collective-permute-start.16 = (bf16[256,128]{1,0:T(8,128)(2,1)S(1)}, bf16[256,128]{1,0:T(8,128)(2,1)S(1)}, u32[]{:S(2)}, u32[]{:S(2)}) collective-permute-start(bf16[256,128]{1,0:T(8,128)(2,1)S(1)} %get-tuple-element.32), channel_id=1, source_target_pairs={{0,16},{8,24},{16,0},{24,8},{1,17},{9,25},{17,1},{25,9},{2,18},{10... | collective-permute-start | bytes 196616 | tf_op jit(solution)/shard_map/ppermute | solution.py:245
  46.1 6.1 %collective-permute-start.17 = (bf16[256,128]{1,0:T(8,128)(2,1)S(1)}, bf16[256,128]{1,0:T(8,128)(2,1)S(1)}, u32[]{:S(2)}, u32[]{:S(2)}) collective-permute-start(bf16[256,128]{1,0:T(8,128)(2,1)S(1)} %get-tuple-element.33), channel_id=1, source_target_pairs={{0,24},{8,16},{16,8},{24,0},{1,25},{9,17},{17,9},{25,1},{2,26},{10... | collective-permute-start | bytes 196616 | tf_op jit(solution)/shard_map/ppermute | solution.py:245
  47.9 12.2 %collective-permute-start.14 = (bf16[1024,128]{1,0:T(8,128)(2,1)S(1)}, bf16[1024,128]{1,0:T(8,128)(2,1)S(1)}, u32[]{:S(2)}, u32[]{:S(2)}) collective-permute-start(bf16[1024,128]{1,0:T(8,128)(2,1)S(1)} %pad_maximum_fusion.1), channel_id=1, source_target_pairs={{0,1},{1,0},{2,3},{3,2},{4,5},{5,4},{6,7},{7,6},{8,9},{9,8},{10,11... | collective-permute-start | bytes 786440 | tf_op jit(solution)/shard_map/ppermute | solution.py:245
  52.3 6.4 %collective-permute-start.20 = (bf16[256,128]{1,0:T(8,128)(2,1)S(1)}, bf16[256,128]{1,0:T(8,128)(2,1)S(1)}, u32[]{:S(2)}, u32[]{:S(2)}) collective-permute-start(bf16[256,128]{1,0:T(8,128)(2,1)S(1)} %get-tuple-element.50.refs_5_), channel_id=1, source_target_pairs={{0,24},{8,16},{16,8},{24,0},{1,25},{9,17},{17,9},{25,1},{2,26},{10... | collective-permute-start | bytes 196616 | tf_op jit(solution)/shard_map/ppermute | solution.py:245
  54.5 5.7 %collective-permute-start.19 = (bf16[256,128]{1,0:T(8,128)(2,1)S(1)}, bf16[256,128]{1,0:T(8,128)(2,1)S(1)}, u32[]{:S(2)}, u32[]{:S(2)}) collective-permute-start(bf16[256,128]{1,0:T(8,128)(2,1)S(1)} %get-tuple-element.50.refs_5_), channel_id=1, source_target_pairs={{0,16},{8,24},{16,0},{24,8},{1,17},{9,25},{17,1},{25,9},{2,18},{10... | collective-permute-start | bytes 196616 | tf_op jit(solution)/shard_map/ppermute | solution.py:245
  54.7 5.4 %collective-permute-start.18 = (bf16[256,128]{1,0:T(8,128)(2,1)S(1)}, bf16[256,128]{1,0:T(8,128)(2,1)S(1)}, u32[]{:S(2)}, u32[]{:S(2)}) collective-permute-start(bf16[256,128]{1,0:T(8,128)(2,1)S(1)} %get-tuple-element.50.refs_5_), channel_id=1, source_target_pairs={{0,8},{8,0},{16,24},{24,16},{1,9},{9,1},{17,25},{25,17},{2,10},{10... | collective-permute-start | bytes 196616 | tf_op jit(solution)/shard_map/ppermute | solution.py:245
  69.7 5.3 %collective-permute-start.24 = (bf16[256,128]{1,0:T(8,128)(2,1)S(1)}, bf16[256,128]{1,0:T(8,128)(2,1)S(1)}, u32[]{:S(2)}, u32[]{:S(2)}) collective-permute-start(bf16[256,128]{1,0:T(8,128)(2,1)S(1)} %get-tuple-element.58), channel_id=1, source_target_pairs={{0,6},{1,7},{2,4},{3,5},{4,2},{5,3},{6,0},{7,1},{8,14},{9,15},{10,... | collective-permute-start | bytes 196616 | tf_op jit(solution)/shard_map/ppermute | solution.py:245
  69.7 6.4 %collective-permute-start.23 = (bf16[256,128]{1,0:T(8,128)(2,1)S(1)}, bf16[256,128]{1,0:T(8,128)(2,1)S(1)}, u32[]{:S(2)}, u32[]{:S(2)}) collective-permute-start(bf16[256,128]{1,0:T(8,128)(2,1)S(1)} %get-tuple-element.59), channel_id=1, source_target_pairs={{0,4},{1,5},{2,6},{3,7},{4,0},{5,1},{6,2},{7,3},{8,12},{9,13},{10,... | collective-permute-start | bytes 196616 | tf_op jit(solution)/shard_map/ppermute | solution.py:245
  76.3 5.9 %collective-permute-start.27 = (bf16[256,128]{1,0:T(8,128)(2,1)S(1)}, bf16[256,128]{1,0:T(8,128)(2,1)S(1)}, u32[]{:S(2)}, u32[]{:S(2)}) collective-permute-start(bf16[256,128]{1,0:T(8,128)(2,1)S(1)} %get-tuple-element.48.refs_0_), channel_id=1, source_target_pairs={{0,6},{1,7},{2,4},{3,5},{4,2},{5,3},{6,0},{7,1},{8,14},{9,15},{10,... | collective-permute-start | bytes 196616 | tf_op jit(solution)/shard_map/ppermute | solution.py:245
  77.8 6.4 %collective-permute-start.26 = (bf16[256,128]{1,0:T(8,128)(2,1)S(1)}, bf16[256,128]{1,0:T(8,128)(2,1)S(1)}, u32[]{:S(2)}, u32[]{:S(2)}) collective-permute-start(bf16[256,128]{1,0:T(8,128)(2,1)S(1)} %get-tuple-element.48.refs_0_), channel_id=1, source_target_pairs={{0,4},{1,5},{2,6},{3,7},{4,0},{5,1},{6,2},{7,3},{8,12},{9,13},{10,... | collective-permute-start | bytes 196616 | tf_op jit(solution)/shard_map/ppermute | solution.py:245
  78.8 5.5 %collective-permute-start.25 = (bf16[256,128]{1,0:T(8,128)(2,1)S(1)}, bf16[256,128]{1,0:T(8,128)(2,1)S(1)}, u32[]{:S(2)}, u32[]{:S(2)}) collective-permute-start(bf16[256,128]{1,0:T(8,128)(2,1)S(1)} %get-tuple-element.48.refs_0_), channel_id=1, source_target_pairs={{0,2},{1,3},{2,0},{3,1},{4,6},{5,7},{6,4},{7,5},{8,10},{9,11},{10,... | collective-permute-start | bytes 196616 | tf_op jit(solution)/shard_map/ppermute | solution.py:245
  81.0 6.4 %collective-permute-start.30 = (bf16[256,128]{1,0:T(8,128)(2,1)S(1)}, bf16[256,128]{1,0:T(8,128)(2,1)S(1)}, u32[]{:S(2)}, u32[]{:S(2)}) collective-permute-start(bf16[256,128]{1,0:T(8,128)(2,1)S(1)} %get-tuple-element.38), channel_id=1, source_target_pairs={{0,16},{8,24},{16,0},{24,8},{1,17},{9,25},{17,1},{25,9},{2,18},{10... | collective-permute-start | bytes 196616 | tf_op jit(solution)/shard_map/ppermute | solution.py:245
  82.1 6.2 %collective-permute-start.31 = (bf16[256,128]{1,0:T(8,128)(2,1)S(1)}, bf16[256,128]{1,0:T(8,128)(2,1)S(1)}, u32[]{:S(2)}, u32[]{:S(2)}) collective-permute-start(bf16[256,128]{1,0:T(8,128)(2,1)S(1)} %get-tuple-element.39), channel_id=1, source_target_pairs={{0,24},{8,16},{16,8},{24,0},{1,25},{9,17},{17,9},{25,1},{2,26},{10... | collective-permute-start | bytes 196616 | tf_op jit(solution)/shard_map/ppermute | solution.py:245
  84.2 11.7 %collective-permute-start.28 = (bf16[1024,128]{1,0:T(8,128)(2,1)S(1)}, bf16[1024,128]{1,0:T(8,128)(2,1)S(1)}, u32[]{:S(2)}, u32[]{:S(2)}) collective-permute-start(bf16[1024,128]{1,0:T(8,128)(2,1)S(1)} %pad_maximum_fusion.2), channel_id=1, source_target_pairs={{0,1},{1,0},{2,3},{3,2},{4,5},{5,4},{6,7},{7,6},{8,9},{9,8},{10,11... | collective-permute-start | bytes 786440 | tf_op jit(solution)/shard_map/ppermute | solution.py:245
  88.4 6.1 %collective-permute-start.34 = (bf16[256,128]{1,0:T(8,128)(2,1)S(1)}, bf16[256,128]{1,0:T(8,128)(2,1)S(1)}, u32[]{:S(2)}, u32[]{:S(2)}) collective-permute-start(bf16[256,128]{1,0:T(8,128)(2,1)S(1)} %get-tuple-element.46.refs_5_), channel_id=1, source_target_pairs={{0,24},{8,16},{16,8},{24,0},{1,25},{9,17},{17,9},{25,1},{2,26},{10... | collective-permute-start | bytes 196616 | tf_op jit(solution)/shard_map/ppermute | solution.py:245
  90.5 5.4 %collective-permute-start.33 = (bf16[256,128]{1,0:T(8,128)(2,1)S(1)}, bf16[256,128]{1,0:T(8,128)(2,1)S(1)}, u32[]{:S(2)}, u32[]{:S(2)}) collective-permute-start(bf16[256,128]{1,0:T(8,128)(2,1)S(1)} %get-tuple-element.46.refs_5_), channel_id=1, source_target_pairs={{0,16},{8,24},{16,0},{24,8},{1,17},{9,25},{17,1},{25,9},{2,18},{10... | collective-permute-start | bytes 196616 | tf_op jit(solution)/shard_map/ppermute | solution.py:245
  91.0 5.0 %collective-permute-start.32 = (bf16[256,128]{1,0:T(8,128)(2,1)S(1)}, bf16[256,128]{1,0:T(8,128)(2,1)S(1)}, u32[]{:S(2)}, u32[]{:S(2)}) collective-permute-start(bf16[256,128]{1,0:T(8,128)(2,1)S(1)} %get-tuple-element.46.refs_5_), channel_id=1, source_target_pairs={{0,8},{8,0},{16,24},{24,16},{1,9},{9,1},{17,25},{25,17},{2,10},{10... | collective-permute-start | bytes 196616 | tf_op jit(solution)/shard_map/ppermute | solution.py:245
  103.8 6.7 %collective-permute-start.39 = (bf16[256,128]{1,0:T(8,128)(2,1)S(1)}, bf16[256,128]{1,0:T(8,128)(2,1)S(1)}, u32[]{:S(2)}, u32[]{:S(2)}) collective-permute-start(bf16[256,128]{1,0:T(8,128)(2,1)S(1)} %get-tuple-element.43), channel_id=1, source_target_pairs={{0,8},{8,0},{16,24},{24,16},{1,9},{9,1},{17,25},{25,17},{2,10},{10... | collective-permute-start | bytes 196616 | tf_op jit(solution)/shard_map/ppermute | solution.py:245
  103.9 8.6 %collective-permute-start.40 = (bf16[256,128]{1,0:T(8,128)(2,1)S(1)}, bf16[256,128]{1,0:T(8,128)(2,1)S(1)}, u32[]{:S(2)}, u32[]{:S(2)}) collective-permute-start(bf16[256,128]{1,0:T(8,128)(2,1)S(1)} %get-tuple-element.44), channel_id=1, source_target_pairs={{0,16},{8,24},{16,0},{24,8},{1,17},{9,25},{17,1},{25,9},{2,18},{10... | collective-permute-start | bytes 196616 | tf_op jit(solution)/shard_map/ppermute | solution.py:245
  105.1 7.4 %collective-permute-start.41 = (bf16[256,128]{1,0:T(8,128)(2,1)S(1)}, bf16[256,128]{1,0:T(8,128)(2,1)S(1)}, u32[]{:S(2)}, u32[]{:S(2)}) collective-permute-start(bf16[256,128]{1,0:T(8,128)(2,1)S(1)} %get-tuple-element.45), channel_id=1, source_target_pairs={{0,24},{8,16},{16,8},{24,0},{1,25},{9,17},{17,9},{25,1},{2,26},{10... | collective-permute-start | bytes 196616 | tf_op jit(solution)/shard_map/ppermute | solution.py:245
  109.2 5.2 %collective-permute-start.38 = (bf16[256,128]{1,0:T(8,128)(2,1)S(1)}, bf16[256,128]{1,0:T(8,128)(2,1)S(1)}, u32[]{:S(2)}, u32[]{:S(2)}) collective-permute-start(bf16[256,128]{1,0:T(8,128)(2,1)S(1)} %get-tuple-element.55), channel_id=1, source_target_pairs={{0,6},{1,7},{2,4},{3,5},{4,2},{5,3},{6,0},{7,1},{8,14},{9,15},{10,... | collective-permute-start | bytes 196616 | tf_op jit(solution)/shard_map/ppermute | solution.py:245
  (16 other events, 194.8 us)
where the time goes:
time: 116 us
  starting transfers between devices  50.5 us (44%)
  waiting for transfers between devices  30.5 us (26%)
  Pallas kernels  28.7 us (25%)
  other arithmetic  4.62 us (4%)
  between operations  1.57 us (1%)
    ppermute x42, starting transfers between devices, swap(): return lax.ppermute(block, axis, [(i, i ^ offset) for i in range(size)])  50.5 us
    ppermute x42, waiting for transfers between devices, swap(): return lax.ppermute(block, axis, [(i, i ^ offset) for i in range(size)])  30.5 us
    pallas_call x3, Pallas kernels, local_grads(): pl.pallas_call(functools.partial(force_kernel, cols, rows), out_shape=[co...  23.3 us
    pallas_call x1, Pallas kernels, load_tiles(): pl.pallas_call(functools.partial(load_kernel, targ_group, shape), out_sha...  5.45 us
  transfers between devices with their start and end apart: 42, of which 23 were waited for; matrix products, arithmetic and copies ran while one was open for 2% of the time, Pallas kernels for 5%

commit v1 on v0

--- a/solution.py
+++ b/solution.py
@@ -11,6 +11,7 @@
 LEAPS = 2
 GROUP = 4
 UNROLL = 4
+SCALE = 2.0**-20
 
 
 degrees_free = 4.0
@@ -91,7 +92,8 @@
 
 
 def force_kernel(cols, rows, lists_ref, *refs):
-    comp_firsts, comp_seconds, refs = refs[: cols // 2], refs[cols // 2], refs[cols // 2 + 1 :]
+    comp_firsts, refs = refs[: cols // 2], refs[cols // 2 :]
+    comp_seconds, refs = refs[: cols // 2], refs[cols // 2 :]
     targ_blocks, refs = refs[:rows], refs[rows:]
     values_ref, weight_ref, refs = refs[0], refs[1], refs[2:]
     comp_keep, comp_send, refs = refs[0], refs[1], refs[2:]
@@ -112,8 +114,7 @@
             fill(n * targ_per + i, tile, targ_tiles, targ_flip, targ_acc)
     for n in range(cols):
         for i in range(comp_per):
-            start = (n // 2 * comp_per * (n % 2) + i) * side
-            tile = (comp_seconds if n % 2 else comp_firsts[n // 2])[start : start + side]
+            tile = (comp_seconds if n % 2 else comp_firsts)[n // 2][i * side : (i + 1) * side]
             fill(n * comp_per + i, tile, comp_tiles, comp_flip, comp_acc)
 
     def steps(count):
@@ -139,24 +140,27 @@
 
     lax.fori_loop(0, steps(pairs), predict, 0)
 
-    one = degrees_free * noise_scale * noise_scale
+    one = jnp.asarray(degrees_free * noise_scale * noise_scale, pred.dtype)
 
     def weigh(step, unused):
         sums = []
         for n in range(UNROLL):
             group = step * UNROLL + n
             spot = lists_ref[GROUP, group]
-            guess = pred[spot].astype(jnp.float32)
+            guess = pred[spot]
             whole = None
-            for m in range(GROUP):
-                slot = lists_ref[m, group]
-                resid = values_ref[slot].astype(jnp.float32) - guess
-                inverse = pl.reciprocal(one + resid * resid, approx=True)
-                scaled = resid * weight_ref[slot].astype(jnp.float32) * inverse
-                whole = scaled if whole is None else whole + scaled
+            for m in range(0, GROUP, 2):
+                slots = lists_ref[m, group], lists_ref[m + 1, group]
+                left, right = (values_ref[slot] - guess for slot in slots)
+                small = right * SCALE
+                left_top, left_low = left * weight_ref[slots[0]], left * left + one
+                right_top, right_low = small * weight_ref[slots[1]], small * right + one * SCALE
+                top = left_top * right_low + right_top * left_low
+                both = top * pl.reciprocal(left_low * right_low, approx=True)
+                whole = both if whole is None else whole + both
             sums.append((spot, whole))
         for spot, whole in sums:
-            total[spot] += whole
+            total[spot] += whole.astype(total.dtype)
         return unused
 
     lax.fori_loop(0, steps(groups), weigh, 0)
@@ -222,7 +226,7 @@
     outs = pl.pallas_call(
         functools.partial(force_kernel, cols, rows),
         out_shape=[comp_shape] * 2 + [targ_shape] * rows,
-        in_specs=[smem] + [vmem] * (cols // 2 + 1 + rows + 2),
+        in_specs=[smem] + [vmem] * (cols + rows + 2),
         out_specs=[vmem] * (2 + rows),
         scratch_shapes=[
             pltpu.VMEM((pairs + 1, side, side), jnp.bfloat16),
@@ -236,7 +240,7 @@
         ],
         compiler_params=pltpu.CompilerParams(vmem_limit_bytes=held + 4 * 2**20),
         name="tile_force",
-    )(lists, *comp_firsts, comp_seconds, *targ_blocks, values, weight)
+    )(lists, *comp_firsts, *comp_seconds, *targ_blocks, values, weight)
     return outs[0], outs[1], outs[2:]
 
 
@@ -259,8 +263,7 @@
 def spread_pairs(block, axis):
     firsts = [block]
     firsts += [swap(block, axis, offset) for offset in range(2, lax.axis_size(axis), 2)]
-    seconds = swap(jnp.concatenate(firsts), axis, 1)
-    return firsts, seconds
+    return firsts, [swap(block, axis, 1) for block in firsts]
 
 
 def collect_pairs(keep, send, axis):

time: 116 us -> 105 us (0.905)
  waiting for transfers between devices: 30.5 us -> 14.8 us
  starting transfers between devices: 50.5 us -> 65.3 us
  Pallas kernels: 28.7 us -> 19 us
    ppermute x42 -> x51, waiting for transfers between devices: 30.5 us -> 14.8 us  [swap(): return lax.ppermute(block, axis, [(i, i ^ offset) for i in range(size)])]
    ppermute x42 -> x51, starting transfers between devices: 50.5 us -> 65.3 us  [swap(): return lax.ppermute(block, axis, [(i, i ^ offset) for i in range(size)])]
    pallas_call x3, Pallas kernels: 23.3 us -> 16.5 us  [local_grads(): pl.pallas_call(functools.partial(force_kernel, cols, rows), out_shape=[co...]
    pallas_call x1, Pallas kernels: 5.45 us -> 2.44 us  [load_tiles(): pl.pallas_call(functools.partial(load_kernel, targ_group, shape), out_sha...]
  transfers between devices with their start and end apart: 42 -> 51, of which waited for: 23 -> 17; matrix products, arithmetic and copies ran while one was open for 2% -> 3% of each run, Pallas kernels for 5% -> 2%
where the time goes in v1:
time: 105 us
  starting transfers between devices  65.3 us (62%)
  Pallas kernels  19 us (18%)
  waiting for transfers between devices  14.8 us (14%)
  other arithmetic  4.57 us (4%)
  between operations  1.52 us (1%)
    ppermute x51, starting transfers between devices, swap(): return lax.ppermute(block, axis, [(i, i ^ offset) for i in range(size)])  65.3 us
    pallas_call x3, Pallas kernels, local_grads(): pl.pallas_call(functools.partial(force_kernel, cols, rows), out_shape=[co...  16.5 us
    ppermute x51, waiting for transfers between devices, swap(): return lax.ppermute(block, axis, [(i, i ^ offset) for i in range(size)])  14.8 us
    pallas_call x1, Pallas kernels, load_tiles(): pl.pallas_call(functools.partial(load_kernel, targ_group, shape), out_sha...  2.44 us
  transfers between devices with their start and end apart: 51, of which 17 were waited for; matrix products, arithmetic and copies ran while one was open for 3% of the time, Pallas kernels for 2%

profile of v1, /device:TPU:0, one launch (start us, length us, event | category | flops | bytes accessed | tf_op | source)
XLA Modules:
  0.0 105.3 jit_solution(9667136384067725705)
XLA Ops:
  1.5 5.0 %collective-permute-start.9 = (bf16[256,128]{1,0:T(8,128)(2,1)S(1)}, bf16[256,128]{1,0:T(8,128)(2,1)S(1)}, u32[]{:S(2)}, u32[]{:S(2)}) collective-permute-start(bf16[256,128]{1,0:T(8,128)(2,1)S(1)} %convert_element_type.232.refs_8_), channel_id=1, source_target_pairs={{0,24},{8,16},{16,8},{24,0},{1,25},{9,17},{17,9},{25,1},{2,26},{10... | collective-permute-start | bytes 196616 | tf_op jit(solution)/shard_map/ppermute | solution.py:249
  7.5 2.4 %collective-permute-start.2 = (bf16[256,128]{1,0:T(8,128)(2,1)S(1)}, bf16[256,128]{1,0:T(8,128)(2,1)S(1)}, u32[]{:S(2)}, u32[]{:S(2)}) collective-permute-start(bf16[256,128]{1,0:T(8,128)(2,1)S(1)} %convert_element_type.231.refs_0_), channel_id=1, source_target_pairs={{0,6},{1,7},{2,4},{3,5},{4,2},{5,3},{6,0},{7,1},{8,14},{9,15},{10,... | collective-permute-start | bytes 196616 | tf_op jit(solution)/shard_map/ppermute | solution.py:249
  12.9 1.3 %collective-permute-done.1.refs_2_ = bf16[256,128]{1,0:T(8,128)(2,1)S(1)} collective-permute-done((bf16[256,128]{1,0:T(8,128)(2,1)S(1)}, bf16[256,128]{1,0:T(8,128)(2,1)S(1)}, u32[]{:S(2)}, u32[]{:S(2)}) %collective-permute-start.1) | collective-permute-done | bytes 65568 | tf_op jit(solution)/shard_map/ppermute | solution.py:249
  15.5 2.4 %tile_load.1 = (bf16[257,128,128]{2,1,0:T(8,128)(2,1)S(1)}, bf16[257,128,128]{2,1,0:T(8,128)(2,1)S(1)}, s32[8,256]{1,0:T(8,128)S(1)}) custom-call(s32[1,256]{1,0:T(1,128)S(1)} %compare_select_fusion.pair_ref, s32[1]{0:T(128)} %copy.13.live_ref, bf16[256,128,128]{2,1,0:T(8,128)(2,1)} %bitcast.64, bf16[256,128,128]{2,1,0:T(8,128)(2,1)} %bitcast.65), custom_call_target="tpu_custom_call" | custom-call | tf_op jit(solution)/shard_map/tile_load/pallas_call | solution.py:205
  18.0 5.5 %tile_force.3 = (bf16[4,256,128]{2,1,0:T(8,128)(2,1)S(1)}, bf16[4,256,128]{2,1,0:T(8,128)(2,1)S(1)}, bf16[256,128]{1,0:T(8,128)(2,1)S(1)}, bf16[256,128]{1,0:T(8...) custom-call(s32[8,256]{1,0:T(8,128)S(1)} %get-tuple-element.25.lists_ref, ...), custom_call_target="tpu_custom_call" | custom-call | tf_op jit(solution)/shard_map/tile_force/pallas_call | solution.py:226
  24.4 3.8 %collective-permute-start.21 = (bf16[256,128]{1,0:T(8,128)(2,1)S(1)}, bf16[256,128]{1,0:T(8,128)(2,1)S(1)}, u32[]{:S(2)}, u32[]{:S(2)}) collective-permute-start(bf16[256,128]{1,0:T(8,128)(2,1)S(1)} %get-tuple-element.31), channel_id=1, source_target_pairs={{0,8},{8,0},{16,24},{24,16},{1,9},{9,1},{17,25},{25,17},{2,10},{10... | collective-permute-start | bytes 196616 | tf_op jit(solution)/shard_map/ppermute | solution.py:249
  28.2 4.3 %collective-permute-start.22 = (bf16[256,128]{1,0:T(8,128)(2,1)S(1)}, bf16[256,128]{1,0:T(8,128)(2,1)S(1)}, u32[]{:S(2)}, u32[]{:S(2)}) collective-permute-start(bf16[256,128]{1,0:T(8,128)(2,1)S(1)} %get-tuple-element.32), channel_id=1, source_target_pairs={{0,16},{8,24},{16,0},{24,8},{1,17},{9,25},{17,1},{25,9},{2,18},{10... | collective-permute-start | bytes 196616 | tf_op jit(solution)/shard_map/ppermute | solution.py:249
  33.6 4.4 %collective-permute-start.11 = (bf16[256,128]{1,0:T(8,128)(2,1)S(1)}, bf16[256,128]{1,0:T(8,128)(2,1)S(1)}, u32[]{:S(2)}, u32[]{:S(2)}) collective-permute-start(bf16[256,128]{1,0:T(8,128)(2,1)S(1)} %get-tuple-element.60), channel_id=1, source_target_pairs={{0,2},{1,3},{2,0},{3,1},{4,6},{5,7},{6,4},{7,5},{8,10},{9,11},{10,... | collective-permute-start | bytes 196616 | tf_op jit(solution)/shard_map/ppermute | solution.py:249
  38.3 1.3 %collective-permute-start.12 = (bf16[256,128]{1,0:T(8,128)(2,1)S(1)}, bf16[256,128]{1,0:T(8,128)(2,1)S(1)}, u32[]{:S(2)}, u32[]{:S(2)}) collective-permute-start(bf16[256,128]{1,0:T(8,128)(2,1)S(1)} %get-tuple-element.62), channel_id=1, source_target_pairs={{0,4},{1,5},{2,6},{3,7},{4,0},{5,1},{6,2},{7,3},{8,12},{9,13},{10,... | collective-permute-start | bytes 196616 | tf_op jit(solution)/shard_map/ppermute | solution.py:249
  39.7 1.8 %collective-permute-start.26 = (bf16[256,128]{1,0:T(8,128)(2,1)S(1)}, bf16[256,128]{1,0:T(8,128)(2,1)S(1)}, u32[]{:S(2)}, u32[]{:S(2)}) collective-permute-start(bf16[256,128]{1,0:T(8,128)(2,1)S(1)} %get-tuple-element.50.refs_8_), channel_id=1, source_target_pairs={{0,24},{8,16},{16,8},{24,0},{1,25},{9,17},{17,9},{25,1},{2,26},{10... | collective-permute-start | bytes 196616 | tf_op jit(solution)/shard_map/ppermute | solution.py:249
  43.4 2.0 %collective-permute-start.16 = (bf16[256,128]{1,0:T(8,128)(2,1)S(1)}, bf16[256,128]{1,0:T(8,128)(2,1)S(1)}, u32[]{:S(2)}, u32[]{:S(2)}) collective-permute-start(bf16[256,128]{1,0:T(8,128)(2,1)S(1)} %get-tuple-element.52.refs_0_), channel_id=1, source_target_pairs={{0,6},{1,7},{2,4},{3,5},{4,2},{5,3},{6,0},{7,1},{8,14},{9,15},{10,... | collective-permute-start | bytes 196616 | tf_op jit(solution)/shard_map/ppermute | solution.py:249
  45.4 1.5 %collective-permute-start.15 = (bf16[256,128]{1,0:T(8,128)(2,1)S(1)}, bf16[256,128]{1,0:T(8,128)(2,1)S(1)}, u32[]{:S(2)}, u32[]{:S(2)}) collective-permute-start(bf16[256,128]{1,0:T(8,128)(2,1)S(1)} %get-tuple-element.52.refs_0_), channel_id=1, source_target_pairs={{0,4},{1,5},{2,6},{3,7},{4,0},{5,1},{6,2},{7,3},{8,12},{9,13},{10,... | collective-permute-start | bytes 196616 | tf_op jit(solution)/shard_map/ppermute | solution.py:249
  46.9 1.5 %collective-permute-start.24 = (bf16[256,128]{1,0:T(8,128)(2,1)S(1)}, bf16[256,128]{1,0:T(8,128)(2,1)S(1)}, u32[]{:S(2)}, u32[]{:S(2)}) collective-permute-start(bf16[256,128]{1,0:T(8,128)(2,1)S(1)} %get-tuple-element.50.refs_8_), channel_id=1, source_target_pairs={{0,8},{8,0},{16,24},{24,16},{1,9},{9,1},{17,25},{25,17},{2,10},{10... | collective-permute-start | bytes 196616 | tf_op jit(solution)/shard_map/ppermute | solution.py:249
  49.8 1.4 %collective-permute-done.14.refs_1_ = bf16[256,128]{1,0:T(8,128)(2,1)S(1)} collective-permute-done((bf16[256,128]{1,0:T(8,128)(2,1)S(1)}, bf16[256,128]{1,0:T(8,128)(2,1)S(1)}, u32[]{:S(2)}, u32[]{:S(2)}) %collective-permute-start.14) | collective-permute-done | bytes 65568 | tf_op jit(solution)/shard_map/ppermute | solution.py:249
  52.4 5.5 %tile_force.4 = (bf16[4,256,128]{2,1,0:T(8,128)(2,1)S(1)}, bf16[4,256,128]{2,1,0:T(8,128)(2,1)S(1)}, bf16[256,128]{1,0:T(8,128)(2,1)S(1)}, bf16[256,128]{1,0:T(8...) custom-call(s32[8,256]{1,0:T(8,128)S(1)} %get-tuple-element.25.lists_ref, ...), custom_call_target="tpu_custom_call" | custom-call | tf_op jit(solution)/shard_map/tile_force/pallas_call | solution.py:226
  58.1 3.3 %collective-permute-start.38 = (bf16[256,128]{1,0:T(8,128)(2,1)S(1)}, bf16[256,128]{1,0:T(8,128)(2,1)S(1)}, u32[]{:S(2)}, u32[]{:S(2)}) collective-permute-start(bf16[256,128]{1,0:T(8,128)(2,1)S(1)} %get-tuple-element.37), channel_id=1, source_target_pairs={{0,8},{8,0},{16,24},{24,16},{1,9},{9,1},{17,25},{25,17},{2,10},{10... | collective-permute-start | bytes 196616 | tf_op jit(solution)/shard_map/ppermute | solution.py:249
  61.4 1.8 %collective-permute-start.39 = (bf16[256,128]{1,0:T(8,128)(2,1)S(1)}, bf16[256,128]{1,0:T(8,128)(2,1)S(1)}, u32[]{:S(2)}, u32[]{:S(2)}) collective-permute-start(bf16[256,128]{1,0:T(8,128)(2,1)S(1)} %get-tuple-element.38), channel_id=1, source_target_pairs={{0,16},{8,24},{16,0},{24,8},{1,17},{9,25},{17,1},{25,9},{2,18},{10... | collective-permute-start | bytes 196616 | tf_op jit(solution)/shard_map/ppermute | solution.py:249
  63.2 1.3 %collective-permute-start.40 = (bf16[256,128]{1,0:T(8,128)(2,1)S(1)}, bf16[256,128]{1,0:T(8,128)(2,1)S(1)}, u32[]{:S(2)}, u32[]{:S(2)}) collective-permute-start(bf16[256,128]{1,0:T(8,128)(2,1)S(1)} %get-tuple-element.39), channel_id=1, source_target_pairs={{0,24},{8,16},{16,8},{24,0},{1,25},{9,17},{17,9},{25,1},{2,26},{10... | collective-permute-start | bytes 196616 | tf_op jit(solution)/shard_map/ppermute | solution.py:249
  64.5 4.1 %collective-permute-start.28 = (bf16[256,128]{1,0:T(8,128)(2,1)S(1)}, bf16[256,128]{1,0:T(8,128)(2,1)S(1)}, u32[]{:S(2)}, u32[]{:S(2)}) collective-permute-start(bf16[256,128]{1,0:T(8,128)(2,1)S(1)} %get-tuple-element.57), channel_id=1, source_target_pairs={{0,2},{1,3},{2,0},{3,1},{4,6},{5,7},{6,4},{7,5},{8,10},{9,11},{10,... | collective-permute-start | bytes 196616 | tf_op jit(solution)/shard_map/ppermute | solution.py:249
  68.8 1.5 %collective-permute-start.29 = (bf16[256,128]{1,0:T(8,128)(2,1)S(1)}, bf16[256,128]{1,0:T(8,128)(2,1)S(1)}, u32[]{:S(2)}, u32[]{:S(2)}) collective-permute-start(bf16[256,128]{1,0:T(8,128)(2,1)S(1)} %get-tuple-element.59), channel_id=1, source_target_pairs={{0,4},{1,5},{2,6},{3,7},{4,0},{5,1},{6,2},{7,3},{8,12},{9,13},{10,... | collective-permute-start | bytes 196616 | tf_op jit(solution)/shard_map/ppermute | solution.py:249
  70.3 2.0 %collective-permute-start.43 = (bf16[256,128]{1,0:T(8,128)(2,1)S(1)}, bf16[256,128]{1,0:T(8,128)(2,1)S(1)}, u32[]{:S(2)}, u32[]{:S(2)}) collective-permute-start(bf16[256,128]{1,0:T(8,128)(2,1)S(1)} %get-tuple-element.46.refs_8_), channel_id=1, source_target_pairs={{0,24},{8,16},{16,8},{24,0},{1,25},{9,17},{17,9},{25,1},{2,26},{10... | collective-permute-start | bytes 196616 | tf_op jit(solution)/shard_map/ppermute | solution.py:249
  73.9 2.1 %collective-permute-start.33 = (bf16[256,128]{1,0:T(8,128)(2,1)S(1)}, bf16[256,128]{1,0:T(8,128)(2,1)S(1)}, u32[]{:S(2)}, u32[]{:S(2)}) collective-permute-start(bf16[256,128]{1,0:T(8,128)(2,1)S(1)} %get-tuple-element.48.refs_0_), channel_id=1, source_target_pairs={{0,6},{1,7},{2,4},{3,5},{4,2},{5,3},{6,0},{7,1},{8,14},{9,15},{10,... | collective-permute-start | bytes 196616 | tf_op jit(solution)/shard_map/ppermute | solution.py:249
  76.0 1.5 %collective-permute-start.32 = (bf16[256,128]{1,0:T(8,128)(2,1)S(1)}, bf16[256,128]{1,0:T(8,128)(2,1)S(1)}, u32[]{:S(2)}, u32[]{:S(2)}) collective-permute-start(bf16[256,128]{1,0:T(8,128)(2,1)S(1)} %get-tuple-element.48.refs_0_), channel_id=1, source_target_pairs={{0,4},{1,5},{2,6},{3,7},{4,0},{5,1},{6,2},{7,3},{8,12},{9,13},{10,... | collective-permute-start | bytes 196616 | tf_op jit(solution)/shard_map/ppermute | solution.py:249
  77.5 1.5 %collective-permute-start.41 = (bf16[256,128]{1,0:T(8,128)(2,1)S(1)}, bf16[256,128]{1,0:T(8,128)(2,1)S(1)}, u32[]{:S(2)}, u32[]{:S(2)}) collective-permute-start(bf16[256,128]{1,0:T(8,128)(2,1)S(1)} %get-tuple-element.46.refs_8_), channel_id=1, source_target_pairs={{0,8},{8,0},{16,24},{24,16},{1,9},{9,1},{17,25},{25,17},{2,10},{10... | collective-permute-start | bytes 196616 | tf_op jit(solution)/shard_map/ppermute | solution.py:249
  80.4 1.4 %collective-permute-done.31.refs_1_ = bf16[256,128]{1,0:T(8,128)(2,1)S(1)} collective-permute-done((bf16[256,128]{1,0:T(8,128)(2,1)S(1)}, bf16[256,128]{1,0:T(8,128)(2,1)S(1)}, u32[]{:S(2)}, u32[]{:S(2)}) %collective-permute-start.31) | collective-permute-done | bytes 65568 | tf_op jit(solution)/shard_map/ppermute | solution.py:249
  83.0 5.5 %tile_force.5 = (bf16[4,256,128]{2,1,0:T(8,128)(2,1)S(1)}, bf16[4,256,128]{2,1,0:T(8,128)(2,1)S(1)}, bf16[256,128]{1,0:T(8,128)(2,1)S(1)}, bf16[256,128]{1,0:T(8...) custom-call(s32[8,256]{1,0:T(8,128)S(1)} %get-tuple-element.25.lists_ref, ...), custom_call_target="tpu_custom_call" | custom-call | tf_op jit(solution)/shard_map/tile_force/pallas_call | solution.py:226
  88.8 3.3 %collective-permute-start.48 = (bf16[256,128]{1,0:T(8,128)(2,1)S(1)}, bf16[256,128]{1,0:T(8,128)(2,1)S(1)}, u32[]{:S(2)}, u32[]{:S(2)}) collective-permute-start(bf16[256,128]{1,0:T(8,128)(2,1)S(1)} %get-tuple-element.43), channel_id=1, source_target_pairs={{0,8},{8,0},{16,24},{24,16},{1,9},{9,1},{17,25},{25,17},{2,10},{10... | collective-permute-start | bytes 196616 | tf_op jit(solution)/shard_map/ppermute | solution.py:249
  92.1 1.8 %collective-permute-start.49 = (bf16[256,128]{1,0:T(8,128)(2,1)S(1)}, bf16[256,128]{1,0:T(8,128)(2,1)S(1)}, u32[]{:S(2)}, u32[]{:S(2)}) collective-permute-start(bf16[256,128]{1,0:T(8,128)(2,1)S(1)} %get-tuple-element.44), channel_id=1, source_target_pairs={{0,16},{8,24},{16,0},{24,8},{1,17},{9,25},{17,1},{25,9},{2,18},{10... | collective-permute-start | bytes 196616 | tf_op jit(solution)/shard_map/ppermute | solution.py:249
  93.8 1.3 %collective-permute-start.50 = (bf16[256,128]{1,0:T(8,128)(2,1)S(1)}, bf16[256,128]{1,0:T(8,128)(2,1)S(1)}, u32[]{:S(2)}, u32[]{:S(2)}) collective-permute-start(bf16[256,128]{1,0:T(8,128)(2,1)S(1)} %get-tuple-element.45), channel_id=1, source_target_pairs={{0,24},{8,16},{16,8},{24,0},{1,25},{9,17},{17,9},{25,1},{2,26},{10... | collective-permute-start | bytes 196616 | tf_op jit(solution)/shard_map/ppermute | solution.py:249
  95.2 4.1 %collective-permute-start.45 = (bf16[256,128]{1,0:T(8,128)(2,1)S(1)}, bf16[256,128]{1,0:T(8,128)(2,1)S(1)}, u32[]{:S(2)}, u32[]{:S(2)}) collective-permute-start(bf16[256,128]{1,0:T(8,128)(2,1)S(1)} %get-tuple-element.54), channel_id=1, source_target_pairs={{0,2},{1,3},{2,0},{3,1},{4,6},{5,7},{6,4},{7,5},{8,10},{9,11},{10,... | collective-permute-start | bytes 196616 | tf_op jit(solution)/shard_map/ppermute | solution.py:249
  99.3 1.5 %collective-permute-start.46 = (bf16[256,128]{1,0:T(8,128)(2,1)S(1)}, bf16[256,128]{1,0:T(8,128)(2,1)S(1)}, u32[]{:S(2)}, u32[]{:S(2)}) collective-permute-start(bf16[256,128]{1,0:T(8,128)(2,1)S(1)} %get-tuple-element.56), channel_id=1, source_target_pairs={{0,4},{1,5},{2,6},{3,7},{4,0},{5,1},{6,2},{7,3},{8,12},{9,13},{10,... | collective-permute-start | bytes 196616 | tf_op jit(solution)/shard_map/ppermute | solution.py:249
  101.9 2.6 %collective-permute-done.47 = bf16[256,128]{1,0:T(8,128)(2,1)S(1)} collective-permute-done((bf16[256,128]{1,0:T(8,128)(2,1)S(1)}, bf16[256,128]{1,0:T(8,128)(2,1)S(1)}, u32[]{:S(2)}, u32[]{:S(2)}) %collective-permute-start.47) | collective-permute-done | bytes 65568 | tf_op jit(solution)/shard_map/ppermute | solution.py:249
  (98 shorter events, 19.1 us)
Async XLA Ops:
  1.5 10.1 %collective-permute-start.9 = (bf16[256,128]{1,0:T(8,128)(2,1)S(1)}, bf16[256,128]{1,0:T(8,128)(2,1)S(1)}, u32[]{:S(2)}, u32[]{:S(2)}) collective-permute-start(bf16[256,128]{1,0:T(8,128)(2,1)S(1)} %convert_element_type.232.refs_8_), channel_id=1, source_target_pairs={{0,24},{8,16},{16,8},{24,0},{1,25},{9,17},{17,9},{25,1},{2,26},{10... | collective-permute-start | bytes 196616 | tf_op jit(solution)/shard_map/ppermute | solution.py:249
  6.6 5.8 %collective-permute-start.8 = (bf16[256,128]{1,0:T(8,128)(2,1)S(1)}, bf16[256,128]{1,0:T(8,128)(2,1)S(1)}, u32[]{:S(2)}, u32[]{:S(2)}) collective-permute-start(bf16[256,128]{1,0:T(8,128)(2,1)S(1)} %convert_element_type.232.refs_8_), channel_id=1, source_target_pairs={{0,16},{8,24},{16,0},{24,8},{1,17},{9,25},{17,1},{25,9},{2,18},{10... | collective-permute-start | bytes 196616 | tf_op jit(solution)/shard_map/ppermute | solution.py:249
  7.5 5.3 %collective-permute-start.2 = (bf16[256,128]{1,0:T(8,128)(2,1)S(1)}, bf16[256,128]{1,0:T(8,128)(2,1)S(1)}, u32[]{:S(2)}, u32[]{:S(2)}) collective-permute-start(bf16[256,128]{1,0:T(8,128)(2,1)S(1)} %convert_element_type.231.refs_0_), channel_id=1, source_target_pairs={{0,6},{1,7},{2,4},{3,5},{4,2},{5,3},{6,0},{7,1},{8,14},{9,15},{10,... | collective-permute-start | bytes 196616 | tf_op jit(solution)/shard_map/ppermute | solution.py:249
  11.7 6.2 %collective-permute-start.7 = (bf16[256,128]{1,0:T(8,128)(2,1)S(1)}, bf16[256,128]{1,0:T(8,128)(2,1)S(1)}, u32[]{:S(2)}, u32[]{:S(2)}) collective-permute-start(bf16[256,128]{1,0:T(8,128)(2,1)S(1)} %convert_element_type.232.refs_8_), channel_id=1, source_target_pairs={{0,8},{8,0},{16,24},{24,16},{1,9},{9,1},{17,25},{25,17},{2,10},{10... | collective-permute-start | bytes 196616 | tf_op jit(solution)/shard_map/ppermute | solution.py:249
  12.4 5.6 %collective-permute-start.3 = (bf16[256,128]{1,0:T(8,128)(2,1)S(1)}, bf16[256,128]{1,0:T(8,128)(2,1)S(1)}, u32[]{:S(2)}, u32[]{:S(2)}) collective-permute-start(bf16[256,128]{1,0:T(8,128)(2,1)S(1)} %convert_element_type.231.refs_0_), channel_id=1, source_target_pairs={{0,1},{1,0},{2,3},{3,2},{4,5},{5,4},{6,7},{7,6},{8,9},{9,8},{10,11... | collective-permute-start | bytes 196616 | tf_op jit(solution)/shard_map/ppermute | solution.py:249
  12.8 5.2 %collective-permute-start.6 = (bf16[256,128]{1,0:T(8,128)(2,1)S(1)}, bf16[256,128]{1,0:T(8,128)(2,1)S(1)}, u32[]{:S(2)}, u32[]{:S(2)}) collective-permute-start(bf16[256,128]{1,0:T(8,128)(2,1)S(1)} %collective-permute-done.2.refs_3_), channel_id=1, source_target_pairs={{0,1},{1,0},{2,3},{3,2},{4,5},{5,4},{6,7},{7,6},{8,9},{9,8},{10,11... | collective-permute-start | bytes 196616 | tf_op jit(solution)/shard_map/ppermute | solution.py:249
  23.5 10.0 %collective-permute-start.10 = (bf16[4,256,128]{2,1,0:T(8,128)(2,1)S(1)}, bf16[4,256,128]{2,1,0:T(8,128)(2,1)S(1)}, u32[]{:S(2)}, u32[]{:S(2)}) collective-permute-start(bf16[4,256,128]{2,1,0:T(8,128)(2,1)S(1)} %get-tuple-element.29), channel_id=1, source_target_pairs={{0,1},{1,0},{2,3},{3,2},{4,5},{5,4},{6,7},{7,6},{8,9},{9,8},{10,11... | collective-permute-start | bytes 786440 | tf_op jit(solution)/shard_map/ppermute | solution.py:249
  24.4 13.9 %collective-permute-start.21 = (bf16[256,128]{1,0:T(8,128)(2,1)S(1)}, bf16[256,128]{1,0:T(8,128)(2,1)S(1)}, u32[]{:S(2)}, u32[]{:S(2)}) collective-permute-start(bf16[256,128]{1,0:T(8,128)(2,1)S(1)} %get-tuple-element.31), channel_id=1, source_target_pairs={{0,8},{8,0},{16,24},{24,16},{1,9},{9,1},{17,25},{25,17},{2,10},{10... | collective-permute-start | bytes 196616 | tf_op jit(solution)/shard_map/ppermute | solution.py:249
  28.2 11.4 %collective-permute-start.22 = (bf16[256,128]{1,0:T(8,128)(2,1)S(1)}, bf16[256,128]{1,0:T(8,128)(2,1)S(1)}, u32[]{:S(2)}, u32[]{:S(2)}) collective-permute-start(bf16[256,128]{1,0:T(8,128)(2,1)S(1)} %get-tuple-element.32), channel_id=1, source_target_pairs={{0,16},{8,24},{16,0},{24,8},{1,17},{9,25},{17,1},{25,9},{2,18},{10... | collective-permute-start | bytes 196616 | tf_op jit(solution)/shard_map/ppermute | solution.py:249
  32.5 7.1 %collective-permute-start.23 = (bf16[256,128]{1,0:T(8,128)(2,1)S(1)}, bf16[256,128]{1,0:T(8,128)(2,1)S(1)}, u32[]{:S(2)}, u32[]{:S(2)}) collective-permute-start(bf16[256,128]{1,0:T(8,128)(2,1)S(1)} %get-tuple-element.33), channel_id=1, source_target_pairs={{0,24},{8,16},{16,8},{24,0},{1,25},{9,17},{17,9},{25,1},{2,26},{10... | collective-permute-start | bytes 196616 | tf_op jit(solution)/shard_map/ppermute | solution.py:249
  33.6 8.5 %collective-permute-start.11 = (bf16[256,128]{1,0:T(8,128)(2,1)S(1)}, bf16[256,128]{1,0:T(8,128)(2,1)S(1)}, u32[]{:S(2)}, u32[]{:S(2)}) collective-permute-start(bf16[256,128]{1,0:T(8,128)(2,1)S(1)} %get-tuple-element.60), channel_id=1, source_target_pairs={{0,2},{1,3},{2,0},{3,1},{4,6},{5,7},{6,4},{7,5},{8,10},{9,11},{10,... | collective-permute-start | bytes 196616 | tf_op jit(solution)/shard_map/ppermute | solution.py:249
  38.0 5.3 %collective-permute-start.13 = (bf16[256,128]{1,0:T(8,128)(2,1)S(1)}, bf16[256,128]{1,0:T(8,128)(2,1)S(1)}, u32[]{:S(2)}, u32[]{:S(2)}) collective-permute-start(bf16[256,128]{1,0:T(8,128)(2,1)S(1)} %get-tuple-element.61), channel_id=1, source_target_pairs={{0,6},{1,7},{2,4},{3,5},{4,2},{5,3},{6,0},{7,1},{8,14},{9,15},{10,... | collective-permute-start | bytes 196616 | tf_op jit(solution)/shard_map/ppermute | solution.py:249
  39.7 7.3 %collective-permute-start.26 = (bf16[256,128]{1,0:T(8,128)(2,1)S(1)}, bf16[256,128]{1,0:T(8,128)(2,1)S(1)}, u32[]{:S(2)}, u32[]{:S(2)}) collective-permute-start(bf16[256,128]{1,0:T(8,128)(2,1)S(1)} %get-tuple-element.50.refs_8_), channel_id=1, source_target_pairs={{0,24},{8,16},{16,8},{24,0},{1,25},{9,17},{17,9},{25,1},{2,26},{10... | collective-permute-start | bytes 196616 | tf_op jit(solution)/shard_map/ppermute | solution.py:249
  41.5 6.9 %collective-permute-start.25 = (bf16[256,128]{1,0:T(8,128)(2,1)S(1)}, bf16[256,128]{1,0:T(8,128)(2,1)S(1)}, u32[]{:S(2)}, u32[]{:S(2)}) collective-permute-start(bf16[256,128]{1,0:T(8,128)(2,1)S(1)} %get-tuple-element.50.refs_8_), channel_id=1, source_target_pairs={{0,16},{8,24},{16,0},{24,8},{1,17},{9,25},{17,1},{25,9},{2,18},{10... | collective-permute-start | bytes 196616 | tf_op jit(solution)/shard_map/ppermute | solution.py:249
  43.4 5.8 %collective-permute-start.16 = (bf16[256,128]{1,0:T(8,128)(2,1)S(1)}, bf16[256,128]{1,0:T(8,128)(2,1)S(1)}, u32[]{:S(2)}, u32[]{:S(2)}) collective-permute-start(bf16[256,128]{1,0:T(8,128)(2,1)S(1)} %get-tuple-element.52.refs_0_), channel_id=1, source_target_pairs={{0,6},{1,7},{2,4},{3,5},{4,2},{5,3},{6,0},{7,1},{8,14},{9,15},{10,... | collective-permute-start | bytes 196616 | tf_op jit(solution)/shard_map/ppermute | solution.py:249
  57.9 6.6 %collective-permute-start.27 = (bf16[4,256,128]{2,1,0:T(8,128)(2,1)S(1)}, bf16[4,256,128]{2,1,0:T(8,128)(2,1)S(1)}, u32[]{:S(2)}, u32[]{:S(2)}) collective-permute-start(bf16[4,256,128]{2,1,0:T(8,128)(2,1)S(1)} %get-tuple-element.35), channel_id=1, source_target_pairs={{0,1},{1,0},{2,3},{3,2},{4,5},{5,4},{6,7},{7,6},{8,9},{9,8},{10,11... | collective-permute-start | bytes 786440 | tf_op jit(solution)/shard_map/ppermute | solution.py:249
  58.1 10.6 %collective-permute-start.38 = (bf16[256,128]{1,0:T(8,128)(2,1)S(1)}, bf16[256,128]{1,0:T(8,128)(2,1)S(1)}, u32[]{:S(2)}, u32[]{:S(2)}) collective-permute-start(bf16[256,128]{1,0:T(8,128)(2,1)S(1)} %get-tuple-element.37), channel_id=1, source_target_pairs={{0,8},{8,0},{16,24},{24,16},{1,9},{9,1},{17,25},{25,17},{2,10},{10... | collective-permute-start | bytes 196616 | tf_op jit(solution)/shard_map/ppermute | solution.py:249
  61.4 8.8 %collective-permute-start.39 = (bf16[256,128]{1,0:T(8,128)(2,1)S(1)}, bf16[256,128]{1,0:T(8,128)(2,1)S(1)}, u32[]{:S(2)}, u32[]{:S(2)}) collective-permute-start(bf16[256,128]{1,0:T(8,128)(2,1)S(1)} %get-tuple-element.38), channel_id=1, source_target_pairs={{0,16},{8,24},{16,0},{24,8},{1,17},{9,25},{17,1},{25,9},{2,18},{10... | collective-permute-start | bytes 196616 | tf_op jit(solution)/shard_map/ppermute | solution.py:249
  63.2 7.0 %collective-permute-start.40 = (bf16[256,128]{1,0:T(8,128)(2,1)S(1)}, bf16[256,128]{1,0:T(8,128)(2,1)S(1)}, u32[]{:S(2)}, u32[]{:S(2)}) collective-permute-start(bf16[256,128]{1,0:T(8,128)(2,1)S(1)} %get-tuple-element.39), channel_id=1, source_target_pairs={{0,24},{8,16},{16,8},{24,0},{1,25},{9,17},{17,9},{25,1},{2,26},{10... | collective-permute-start | bytes 196616 | tf_op jit(solution)/shard_map/ppermute | solution.py:249
  64.5 8.6 %collective-permute-start.28 = (bf16[256,128]{1,0:T(8,128)(2,1)S(1)}, bf16[256,128]{1,0:T(8,128)(2,1)S(1)}, u32[]{:S(2)}, u32[]{:S(2)}) collective-permute-start(bf16[256,128]{1,0:T(8,128)(2,1)S(1)} %get-tuple-element.57), channel_id=1, source_target_pairs={{0,2},{1,3},{2,0},{3,1},{4,6},{5,7},{6,4},{7,5},{8,10},{9,11},{10,... | collective-permute-start | bytes 196616 | tf_op jit(solution)/shard_map/ppermute | solution.py:249
  68.7 5.2 %collective-permute-start.30 = (bf16[256,128]{1,0:T(8,128)(2,1)S(1)}, bf16[256,128]{1,0:T(8,128)(2,1)S(1)}, u32[]{:S(2)}, u32[]{:S(2)}) collective-permute-start(bf16[256,128]{1,0:T(8,128)(2,1)S(1)} %get-tuple-element.58), channel_id=1, source_target_pairs={{0,6},{1,7},{2,4},{3,5},{4,2},{5,3},{6,0},{7,1},{8,14},{9,15},{10,... | collective-permute-start | bytes 196616 | tf_op jit(solution)/shard_map/ppermute | solution.py:249
  68.8 5.1 %collective-permute-start.29 = (bf16[256,128]{1,0:T(8,128)(2,1)S(1)}, bf16[256,128]{1,0:T(8,128)(2,1)S(1)}, u32[]{:S(2)}, u32[]{:S(2)}) collective-permute-start(bf16[256,128]{1,0:T(8,128)(2,1)S(1)} %get-tuple-element.59), channel_id=1, source_target_pairs={{0,4},{1,5},{2,6},{3,7},{4,0},{5,1},{6,2},{7,3},{8,12},{9,13},{10,... | collective-permute-start | bytes 196616 | tf_op jit(solution)/shard_map/ppermute | solution.py:249
  70.3 7.2 %collective-permute-start.43 = (bf16[256,128]{1,0:T(8,128)(2,1)S(1)}, bf16[256,128]{1,0:T(8,128)(2,1)S(1)}, u32[]{:S(2)}, u32[]{:S(2)}) collective-permute-start(bf16[256,128]{1,0:T(8,128)(2,1)S(1)} %get-tuple-element.46.refs_8_), channel_id=1, source_target_pairs={{0,24},{8,16},{16,8},{24,0},{1,25},{9,17},{17,9},{25,1},{2,26},{10... | collective-permute-start | bytes 196616 | tf_op jit(solution)/shard_map/ppermute | solution.py:249
  72.3 7.0 %collective-permute-start.42 = (bf16[256,128]{1,0:T(8,128)(2,1)S(1)}, bf16[256,128]{1,0:T(8,128)(2,1)S(1)}, u32[]{:S(2)}, u32[]{:S(2)}) collective-permute-start(bf16[256,128]{1,0:T(8,128)(2,1)S(1)} %get-tuple-element.46.refs_8_), channel_id=1, source_target_pairs={{0,16},{8,24},{16,0},{24,8},{1,17},{9,25},{17,1},{25,9},{2,18},{10... | collective-permute-start | bytes 196616 | tf_op jit(solution)/shard_map/ppermute | solution.py:249
  73.9 5.7 %collective-permute-start.33 = (bf16[256,128]{1,0:T(8,128)(2,1)S(1)}, bf16[256,128]{1,0:T(8,128)(2,1)S(1)}, u32[]{:S(2)}, u32[]{:S(2)}) collective-permute-start(bf16[256,128]{1,0:T(8,128)(2,1)S(1)} %get-tuple-element.48.refs_0_), channel_id=1, source_target_pairs={{0,6},{1,7},{2,4},{3,5},{4,2},{5,3},{6,0},{7,1},{8,14},{9,15},{10,... | collective-permute-start | bytes 196616 | tf_op jit(solution)/shard_map/ppermute | solution.py:249
  88.5 6.6 %collective-permute-start.44 = (bf16[4,256,128]{2,1,0:T(8,128)(2,1)S(1)}, bf16[4,256,128]{2,1,0:T(8,128)(2,1)S(1)}, u32[]{:S(2)}, u32[]{:S(2)}) collective-permute-start(bf16[4,256,128]{2,1,0:T(8,128)(2,1)S(1)} %get-tuple-element.41), channel_id=1, source_target_pairs={{0,1},{1,0},{2,3},{3,2},{4,5},{5,4},{6,7},{7,6},{8,9},{9,8},{10,11... | collective-permute-start | bytes 786440 | tf_op jit(solution)/shard_map/ppermute | solution.py:249
  88.8 10.6 %collective-permute-start.48 = (bf16[256,128]{1,0:T(8,128)(2,1)S(1)}, bf16[256,128]{1,0:T(8,128)(2,1)S(1)}, u32[]{:S(2)}, u32[]{:S(2)}) collective-permute-start(bf16[256,128]{1,0:T(8,128)(2,1)S(1)} %get-tuple-element.43), channel_id=1, source_target_pairs={{0,8},{8,0},{16,24},{24,16},{1,9},{9,1},{17,25},{25,17},{2,10},{10... | collective-permute-start | bytes 196616 | tf_op jit(solution)/shard_map/ppermute | solution.py:249
  92.1 8.8 %collective-permute-start.49 = (bf16[256,128]{1,0:T(8,128)(2,1)S(1)}, bf16[256,128]{1,0:T(8,128)(2,1)S(1)}, u32[]{:S(2)}, u32[]{:S(2)}) collective-permute-start(bf16[256,128]{1,0:T(8,128)(2,1)S(1)} %get-tuple-element.44), channel_id=1, source_target_pairs={{0,16},{8,24},{16,0},{24,8},{1,17},{9,25},{17,1},{25,9},{2,18},{10... | collective-permute-start | bytes 196616 | tf_op jit(solution)/shard_map/ppermute | solution.py:249
  93.8 7.0 %collective-permute-start.50 = (bf16[256,128]{1,0:T(8,128)(2,1)S(1)}, bf16[256,128]{1,0:T(8,128)(2,1)S(1)}, u32[]{:S(2)}, u32[]{:S(2)}) collective-permute-start(bf16[256,128]{1,0:T(8,128)(2,1)S(1)} %get-tuple-element.45), channel_id=1, source_target_pairs={{0,24},{8,16},{16,8},{24,0},{1,25},{9,17},{17,9},{25,1},{2,26},{10... | collective-permute-start | bytes 196616 | tf_op jit(solution)/shard_map/ppermute | solution.py:249
  95.2 6.7 %collective-permute-start.45 = (bf16[256,128]{1,0:T(8,128)(2,1)S(1)}, bf16[256,128]{1,0:T(8,128)(2,1)S(1)}, u32[]{:S(2)}, u32[]{:S(2)}) collective-permute-start(bf16[256,128]{1,0:T(8,128)(2,1)S(1)} %get-tuple-element.54), channel_id=1, source_target_pairs={{0,2},{1,3},{2,0},{3,1},{4,6},{5,7},{6,4},{7,5},{8,10},{9,11},{10,... | collective-permute-start | bytes 196616 | tf_op jit(solution)/shard_map/ppermute | solution.py:249
  99.3 5.2 %collective-permute-start.47 = (bf16[256,128]{1,0:T(8,128)(2,1)S(1)}, bf16[256,128]{1,0:T(8,128)(2,1)S(1)}, u32[]{:S(2)}, u32[]{:S(2)}) collective-permute-start(bf16[256,128]{1,0:T(8,128)(2,1)S(1)} %get-tuple-element.55), channel_id=1, source_target_pairs={{0,6},{1,7},{2,4},{3,5},{4,2},{5,3},{6,0},{7,1},{8,14},{9,15},{10,... | collective-permute-start | bytes 196616 | tf_op jit(solution)/shard_map/ppermute | solution.py:249
  99.3 5.2 %collective-permute-start.46 = (bf16[256,128]{1,0:T(8,128)(2,1)S(1)}, bf16[256,128]{1,0:T(8,128)(2,1)S(1)}, u32[]{:S(2)}, u32[]{:S(2)}) collective-permute-start(bf16[256,128]{1,0:T(8,128)(2,1)S(1)} %get-tuple-element.56), channel_id=1, source_target_pairs={{0,4},{1,5},{2,6},{3,7},{4,0},{5,1},{6,2},{7,3},{8,12},{9,13},{10,... | collective-permute-start | bytes 196616 | tf_op jit(solution)/shard_map/ppermute | solution.py:249
  (25 other events, 216.0 us)

commit v2 on v0

--- a/solution.py
+++ b/solution.py
@@ -91,7 +91,8 @@
 
 
 def force_kernel(cols, rows, lists_ref, *refs):
-    comp_firsts, comp_seconds, refs = refs[: cols // 2], refs[cols // 2], refs[cols // 2 + 1 :]
+    comp_firsts, refs = refs[: cols // 2], refs[cols // 2 :]
+    comp_seconds, refs = refs[: cols // 2], refs[cols // 2 :]
     targ_blocks, refs = refs[:rows], refs[rows:]
     values_ref, weight_ref, refs = refs[0], refs[1], refs[2:]
     comp_keep, comp_send, refs = refs[0], refs[1], refs[2:]
@@ -112,8 +113,7 @@
             fill(n * targ_per + i, tile, targ_tiles, targ_flip, targ_acc)
     for n in range(cols):
         for i in range(comp_per):
-            start = (n // 2 * comp_per * (n % 2) + i) * side
-            tile = (comp_seconds if n % 2 else comp_firsts[n // 2])[start : start + side]
+            tile = (comp_seconds if n % 2 else comp_firsts)[n // 2][i * side : (i + 1) * side]
             fill(n * comp_per + i, tile, comp_tiles, comp_flip, comp_acc)
 
     def steps(count):
@@ -222,7 +222,7 @@
     outs = pl.pallas_call(
         functools.partial(force_kernel, cols, rows),
         out_shape=[comp_shape] * 2 + [targ_shape] * rows,
-        in_specs=[smem] + [vmem] * (cols // 2 + 1 + rows + 2),
+        in_specs=[smem] + [vmem] * (cols + rows + 2),
         out_specs=[vmem] * (2 + rows),
         scratch_shapes=[
             pltpu.VMEM((pairs + 1, side, side), jnp.bfloat16),
@@ -236,7 +236,7 @@
         ],
         compiler_params=pltpu.CompilerParams(vmem_limit_bytes=held + 4 * 2**20),
         name="tile_force",
-    )(lists, *comp_firsts, comp_seconds, *targ_blocks, values, weight)
+    )(lists, *comp_firsts, *comp_seconds, *targ_blocks, values, weight)
     return outs[0], outs[1], outs[2:]
 
 
@@ -246,21 +246,24 @@
 
 
 def spread(block, axis):
-    return [block] + [swap(block, axis, offset) for offset in range(1, lax.axis_size(axis))]
+    size = lax.axis_size(axis)
+    seconds = [block] + [swap(block, axis, offset) for offset in range(2, size, 2)]
+    return [each for second in seconds for each in (second, swap(second, axis, 1))]
 
 
 def collect(blocks, axis):
     whole = blocks[0].astype(jnp.float32)
-    for offset, block in enumerate(blocks[1:]):
-        whole = whole + swap(block, axis, offset + 1).astype(jnp.float32)
-    return whole
+    for offset in range(2, len(blocks), 2):
+        near = swap(blocks[offset + 1], axis, 1).astype(jnp.float32)
+        far = (blocks[offset].astype(jnp.float32) + near).astype(blocks[offset].dtype)
+        whole = whole + swap(far, axis, offset).astype(jnp.float32)
+    return whole + swap(blocks[1], axis, 1).astype(jnp.float32)
 
 
 def spread_pairs(block, axis):
     firsts = [block]
     firsts += [swap(block, axis, offset) for offset in range(2, lax.axis_size(axis), 2)]
-    seconds = swap(jnp.concatenate(firsts), axis, 1)
-    return firsts, seconds
+    return firsts, [swap(block, axis, 1) for block in firsts]
 
 
 def collect_pairs(keep, send, axis):

time: 116 us -> 101 us (0.87)
  waiting for transfers between devices: 30.5 us -> 23 us
  starting transfers between devices: 50.5 us -> 44.4 us
  Pallas kernels: 28.7 us -> 27.5 us
    ppermute x42 -> x51, waiting for transfers between devices: 30.5 us -> 23 us  [swap(): return lax.ppermute(block, axis, [(i, i ^ offset) for i in range(size)])]
    ppermute x42 -> x51, starting transfers between devices: 50.5 us -> 44.4 us  [swap(): return lax.ppermute(block, axis, [(i, i ^ offset) for i in range(size)])]
  transfers between devices with their start and end apart: 42 -> 51, of which waited for: 23 -> 24; matrix products, arithmetic and copies ran while one was open for 2% -> 3% of each run, Pallas kernels for 5% -> 5%
where the time goes in v2:
time: 101 us
  starting transfers between devices  44.4 us (44%)
  Pallas kernels  27.5 us (27%)
  waiting for transfers between devices  23 us (23%)
  other arithmetic  4.66 us (5%)
  between operations  1.56 us (2%)
    ppermute x51, starting transfers between devices, swap(): return lax.ppermute(block, axis, [(i, i ^ offset) for i in range(size)])  44.4 us
    ppermute x51, waiting for transfers between devices, swap(): return lax.ppermute(block, axis, [(i, i ^ offset) for i in range(size)])  23 us
    pallas_call x3, Pallas kernels, local_grads(): pl.pallas_call(functools.partial(force_kernel, cols, rows), out_shape=[co...  22.3 us
    pallas_call x1, Pallas kernels, load_tiles(): pl.pallas_call(functools.partial(load_kernel, targ_group, shape), out_sha...  5.16 us
  transfers between devices with their start and end apart: 51, of which 24 were waited for; matrix products, arithmetic and copies ran while one was open for 3% of the time, Pallas kernels for 5%

profile of v2, /device:TPU:0, one launch (start us, length us, event | category | flops | bytes accessed | tf_op | source)
XLA Modules:
  0.0 101.1 jit_solution(3916303410157113827)
XLA Ops:
  1.5 4.0 %collective-permute-start.8 = (bf16[256,128]{1,0:T(8,128)(2,1)S(1)}, bf16[256,128]{1,0:T(8,128)(2,1)S(1)}, u32[]{:S(2)}, u32[]{:S(2)}) collective-permute-start(bf16[256,128]{1,0:T(8,128)(2,1)S(1)} %convert_element_type.250.refs_8_), channel_id=1, source_target_pairs={{0,16},{8,24},{16,0},{24,8},{1,17},{9,25},{17,1},{25,9},{2,18},{10... | collective-permute-start | bytes 196616 | tf_op jit(solution)/shard_map/ppermute | solution.py:245
  5.6 1.6 %collective-permute-start.7 = (bf16[256,128]{1,0:T(8,128)(2,1)S(1)}, bf16[256,128]{1,0:T(8,128)(2,1)S(1)}, u32[]{:S(2)}, u32[]{:S(2)}) collective-permute-start(bf16[256,128]{1,0:T(8,128)(2,1)S(1)} %convert_element_type.250.refs_8_), channel_id=1, source_target_pairs={{0,8},{8,0},{16,24},{24,16},{1,9},{9,1},{17,25},{25,17},{2,10},{10... | collective-permute-start | bytes 196616 | tf_op jit(solution)/shard_map/ppermute | solution.py:245
  8.1 2.4 %collective-permute-start.2 = (bf16[256,128]{1,0:T(8,128)(2,1)S(1)}, bf16[256,128]{1,0:T(8,128)(2,1)S(1)}, u32[]{:S(2)}, u32[]{:S(2)}) collective-permute-start(bf16[256,128]{1,0:T(8,128)(2,1)S(1)} %convert_element_type.249.refs_0_), channel_id=1, source_target_pairs={{0,6},{1,7},{2,4},{3,5},{4,2},{5,3},{6,0},{7,1},{8,14},{9,15},{10,... | collective-permute-start | bytes 196616 | tf_op jit(solution)/shard_map/ppermute | solution.py:245
  13.3 1.4 %collective-permute-done.1.refs_2_ = bf16[256,128]{1,0:T(8,128)(2,1)S(1)} collective-permute-done((bf16[256,128]{1,0:T(8,128)(2,1)S(1)}, bf16[256,128]{1,0:T(8,128)(2,1)S(1)}, u32[]{:S(2)}, u32[]{:S(2)}) %collective-permute-start.1) | collective-permute-done | bytes 65568 | tf_op jit(solution)/shard_map/ppermute | solution.py:245
  16.0 5.2 %tile_load.1 = (bf16[257,128,128]{2,1,0:T(8,128)(2,1)S(1)}, bf16[257,128,128]{2,1,0:T(8,128)(2,1)S(1)}, s32[8,256]{1,0:T(8,128)S(1)}) custom-call(s32[1,256]{1,0:T(1,128)S(1)} %compare_select_fusion.pair_ref, s32[1]{0:T(128)} %copy.13.live_ref, bf16[256,128,128]{2,1,0:T(8,128)(2,1)} %bitcast.64, bf16[256,128,128]{2,1,0:T(8,128)(2,1)} %bitcast.65), custom_call_target="tpu_custom_call" | custom-call | tf_op jit(solution)/shard_map/tile_load/pallas_call | solution.py:201
  21.3 7.4 %tile_force.3 = (bf16[4,256,128]{2,1,0:T(8,128)(2,1)S(1)}, bf16[4,256,128]{2,1,0:T(8,128)(2,1)S(1)}, bf16[256,128]{1,0:T(8,128)(2,1)S(1)}, bf16[256,128]{1,0:T(8...) custom-call(s32[8,256]{1,0:T(8,128)S(1)} %get-tuple-element.25.lists_ref, ...), custom_call_target="tpu_custom_call" | custom-call | tf_op jit(solution)/shard_map/tile_force/pallas_call | solution.py:222
  29.5 1.4 %collective-permute-start.23 = (bf16[256,128]{1,0:T(8,128)(2,1)S(1)}, bf16[256,128]{1,0:T(8,128)(2,1)S(1)}, u32[]{:S(2)}, u32[]{:S(2)}) collective-permute-start(bf16[256,128]{1,0:T(8,128)(2,1)S(1)} %get-tuple-element.33), channel_id=1, source_target_pairs={{0,8},{8,0},{16,24},{24,16},{1,9},{9,1},{17,25},{25,17},{2,10},{10... | collective-permute-start | bytes 196616 | tf_op jit(solution)/shard_map/ppermute | solution.py:245
  30.8 2.8 %collective-permute-done.21 = bf16[256,128]{1,0:T(8,128)(2,1)S(1)} collective-permute-done((bf16[256,128]{1,0:T(8,128)(2,1)S(1)}, bf16[256,128]{1,0:T(8,128)(2,1)S(1)}, u32[]{:S(2)}, u32[]{:S(2)}) %collective-permute-start.21) | collective-permute-done | bytes 65568 | tf_op jit(solution)/shard_map/ppermute | solution.py:245
  33.8 1.6 %collective-permute-start.11 = (bf16[256,128]{1,0:T(8,128)(2,1)S(1)}, bf16[256,128]{1,0:T(8,128)(2,1)S(1)}, u32[]{:S(2)}, u32[]{:S(2)}) collective-permute-start(bf16[256,128]{1,0:T(8,128)(2,1)S(1)} %get-tuple-element.58), channel_id=1, source_target_pairs={{0,2},{1,3},{2,0},{3,1},{4,6},{5,7},{6,4},{7,5},{8,10},{9,11},{10,... | collective-permute-start | bytes 196616 | tf_op jit(solution)/shard_map/ppermute | solution.py:245
  35.4 1.4 %collective-permute-start.13 = (bf16[256,128]{1,0:T(8,128)(2,1)S(1)}, bf16[256,128]{1,0:T(8,128)(2,1)S(1)}, u32[]{:S(2)}, u32[]{:S(2)}) collective-permute-start(bf16[256,128]{1,0:T(8,128)(2,1)S(1)} %get-tuple-element.59), channel_id=1, source_target_pairs={{0,6},{1,7},{2,4},{3,5},{4,2},{5,3},{6,0},{7,1},{8,14},{9,15},{10,... | collective-permute-start | bytes 196616 | tf_op jit(solution)/shard_map/ppermute | solution.py:245
  37.3 1.8 %collective-permute-done.22 = bf16[256,128]{1,0:T(8,128)(2,1)S(1)} collective-permute-done((bf16[256,128]{1,0:T(8,128)(2,1)S(1)}, bf16[256,128]{1,0:T(8,128)(2,1)S(1)}, u32[]{:S(2)}, u32[]{:S(2)}) %collective-permute-start.22) | collective-permute-done | bytes 65568 | tf_op jit(solution)/shard_map/ppermute | solution.py:245
  39.2 1.2 %collective-permute-start.25 = (bf16[256,128]{1,0:T(8,128)(2,1)S(1)}, bf16[256,128]{1,0:T(8,128)(2,1)S(1)}, u32[]{:S(2)}, u32[]{:S(2)}) collective-permute-start(bf16[256,128]{1,0:T(8,128)(2,1)S(1)} %fusion.25.refs_8_), channel_id=1, source_target_pairs={{0,16},{8,24},{16,0},{24,8},{1,17},{9,25},{17,1},{25,9},{2,18},{10... | collective-permute-start | bytes 196616 | tf_op jit(solution)/shard_map/ppermute | solution.py:245
  41.5 1.4 %collective-permute-start.16 = (bf16[256,128]{1,0:T(8,128)(2,1)S(1)}, bf16[256,128]{1,0:T(8,128)(2,1)S(1)}, u32[]{:S(2)}, u32[]{:S(2)}) collective-permute-start(bf16[256,128]{1,0:T(8,128)(2,1)S(1)} %get-tuple-element.50.refs_0_), channel_id=1, source_target_pairs={{0,6},{1,7},{2,4},{3,5},{4,2},{5,3},{6,0},{7,1},{8,14},{9,15},{10,... | collective-permute-start | bytes 196616 | tf_op jit(solution)/shard_map/ppermute | solution.py:245
  42.9 1.1 %collective-permute-start.15 = (bf16[256,128]{1,0:T(8,128)(2,1)S(1)}, bf16[256,128]{1,0:T(8,128)(2,1)S(1)}, u32[]{:S(2)}, u32[]{:S(2)}) collective-permute-start(bf16[256,128]{1,0:T(8,128)(2,1)S(1)} %get-tuple-element.50.refs_0_), channel_id=1, source_target_pairs={{0,4},{1,5},{2,6},{3,7},{4,0},{5,1},{6,2},{7,3},{8,12},{9,13},{10,... | collective-permute-start | bytes 196616 | tf_op jit(solution)/shard_map/ppermute | solution.py:245
  45.1 1.6 %collective-permute-start.26 = (bf16[256,128]{1,0:T(8,128)(2,1)S(1)}, bf16[256,128]{1,0:T(8,128)(2,1)S(1)}, u32[]{:S(2)}, u32[]{:S(2)}) collective-permute-start(bf16[256,128]{1,0:T(8,128)(2,1)S(1)} %collective-permute-done.25.refs_10_), channel_id=1, source_target_pairs={{0,8},{8,0},{16,24},{24,16},{1,9},{9,1},{17,25},{25,17},{2,10},{10... | collective-permute-start | bytes 196616 | tf_op jit(solution)/shard_map/ppermute | solution.py:245
  49.5 7.4 %tile_force.4 = (bf16[4,256,128]{2,1,0:T(8,128)(2,1)S(1)}, bf16[4,256,128]{2,1,0:T(8,128)(2,1)S(1)}, bf16[256,128]{1,0:T(8,128)(2,1)S(1)}, bf16[256,128]{1,0:T(8...) custom-call(s32[8,256]{1,0:T(8,128)S(1)} %get-tuple-element.25.lists_ref, ...), custom_call_target="tpu_custom_call" | custom-call | tf_op jit(solution)/shard_map/tile_force/pallas_call | solution.py:222
  57.0 1.5 %collective-permute-start.27 = (bf16[4,256,128]{2,1,0:T(8,128)(2,1)S(1)}, bf16[4,256,128]{2,1,0:T(8,128)(2,1)S(1)}, u32[]{:S(2)}, u32[]{:S(2)}) collective-permute-start(bf16[4,256,128]{2,1,0:T(8,128)(2,1)S(1)} %get-tuple-element.35), channel_id=1, source_target_pairs={{0,1},{1,0},{2,3},{3,2},{4,5},{5,4},{6,7},{7,6},{8,9},{9,8},{10,11... | collective-permute-start | bytes 786440 | tf_op jit(solution)/shard_map/ppermute | solution.py:245
  59.1 2.5 %collective-permute-done.38 = bf16[256,128]{1,0:T(8,128)(2,1)S(1)} collective-permute-done((bf16[256,128]{1,0:T(8,128)(2,1)S(1)}, bf16[256,128]{1,0:T(8,128)(2,1)S(1)}, u32[]{:S(2)}, u32[]{:S(2)}) %collective-permute-start.38) | collective-permute-done | bytes 65568 | tf_op jit(solution)/shard_map/ppermute | solution.py:245
  61.6 1.7 %collective-permute-start.39 = (bf16[256,128]{1,0:T(8,128)(2,1)S(1)}, bf16[256,128]{1,0:T(8,128)(2,1)S(1)}, u32[]{:S(2)}, u32[]{:S(2)}) collective-permute-start(bf16[256,128]{1,0:T(8,128)(2,1)S(1)} %add_convert_fusion.4), channel_id=1, source_target_pairs={{0,16},{8,24},{16,0},{24,8},{1,17},{9,25},{17,1},{25,9},{2,18},{10... | collective-permute-start | bytes 196616 | tf_op jit(solution)/shard_map/ppermute | solution.py:245
  63.3 2.1 %collective-permute-start.28 = (bf16[256,128]{1,0:T(8,128)(2,1)S(1)}, bf16[256,128]{1,0:T(8,128)(2,1)S(1)}, u32[]{:S(2)}, u32[]{:S(2)}) collective-permute-start(bf16[256,128]{1,0:T(8,128)(2,1)S(1)} %get-tuple-element.55), channel_id=1, source_target_pairs={{0,2},{1,3},{2,0},{3,1},{4,6},{5,7},{6,4},{7,5},{8,10},{9,11},{10,... | collective-permute-start | bytes 196616 | tf_op jit(solution)/shard_map/ppermute | solution.py:245
  65.4 1.8 %collective-permute-start.30 = (bf16[256,128]{1,0:T(8,128)(2,1)S(1)}, bf16[256,128]{1,0:T(8,128)(2,1)S(1)}, u32[]{:S(2)}, u32[]{:S(2)}) collective-permute-start(bf16[256,128]{1,0:T(8,128)(2,1)S(1)} %get-tuple-element.56), channel_id=1, source_target_pairs={{0,6},{1,7},{2,4},{3,5},{4,2},{5,3},{6,0},{7,1},{8,14},{9,15},{10,... | collective-permute-start | bytes 196616 | tf_op jit(solution)/shard_map/ppermute | solution.py:245
  67.4 1.2 %collective-permute-start.42 = (bf16[256,128]{1,0:T(8,128)(2,1)S(1)}, bf16[256,128]{1,0:T(8,128)(2,1)S(1)}, u32[]{:S(2)}, u32[]{:S(2)}) collective-permute-start(bf16[256,128]{1,0:T(8,128)(2,1)S(1)} %get-tuple-element.46.refs_8_), channel_id=1, source_target_pairs={{0,16},{8,24},{16,0},{24,8},{1,17},{9,25},{17,1},{25,9},{2,18},{10... | collective-permute-start | bytes 196616 | tf_op jit(solution)/shard_map/ppermute | solution.py:245
  68.6 1.1 %collective-permute-start.41 = (bf16[256,128]{1,0:T(8,128)(2,1)S(1)}, bf16[256,128]{1,0:T(8,128)(2,1)S(1)}, u32[]{:S(2)}, u32[]{:S(2)}) collective-permute-start(bf16[256,128]{1,0:T(8,128)(2,1)S(1)} %get-tuple-element.46.refs_8_), channel_id=1, source_target_pairs={{0,8},{8,0},{16,24},{24,16},{1,9},{9,1},{17,25},{25,17},{2,10},{10... | collective-permute-start | bytes 196616 | tf_op jit(solution)/shard_map/ppermute | solution.py:245
  71.6 1.7 %collective-permute-start.33 = (bf16[256,128]{1,0:T(8,128)(2,1)S(1)}, bf16[256,128]{1,0:T(8,128)(2,1)S(1)}, u32[]{:S(2)}, u32[]{:S(2)}) collective-permute-start(bf16[256,128]{1,0:T(8,128)(2,1)S(1)} %get-tuple-element.48.refs_0_), channel_id=1, source_target_pairs={{0,6},{1,7},{2,4},{3,5},{4,2},{5,3},{6,0},{7,1},{8,14},{9,15},{10,... | collective-permute-start | bytes 196616 | tf_op jit(solution)/shard_map/ppermute | solution.py:245
  73.3 1.5 %collective-permute-start.32 = (bf16[256,128]{1,0:T(8,128)(2,1)S(1)}, bf16[256,128]{1,0:T(8,128)(2,1)S(1)}, u32[]{:S(2)}, u32[]{:S(2)}) collective-permute-start(bf16[256,128]{1,0:T(8,128)(2,1)S(1)} %get-tuple-element.48.refs_0_), channel_id=1, source_target_pairs={{0,4},{1,5},{2,6},{3,7},{4,0},{5,1},{6,2},{7,3},{8,12},{9,13},{10,... | collective-permute-start | bytes 196616 | tf_op jit(solution)/shard_map/ppermute | solution.py:245
  75.2 1.6 %collective-permute-start.43 = (bf16[256,128]{1,0:T(8,128)(2,1)S(1)}, bf16[256,128]{1,0:T(8,128)(2,1)S(1)}, u32[]{:S(2)}, u32[]{:S(2)}) collective-permute-start(bf16[256,128]{1,0:T(8,128)(2,1)S(1)} %collective-permute-done.42.refs_10_), channel_id=1, source_target_pairs={{0,8},{8,0},{16,24},{24,16},{1,9},{9,1},{17,25},{25,17},{2,10},{10... | collective-permute-start | bytes 196616 | tf_op jit(solution)/shard_map/ppermute | solution.py:245
  77.6 1.5 %collective-permute-done.31.refs_1_ = bf16[256,128]{1,0:T(8,128)(2,1)S(1)} collective-permute-done((bf16[256,128]{1,0:T(8,128)(2,1)S(1)}, bf16[256,128]{1,0:T(8,128)(2,1)S(1)}, u32[]{:S(2)}, u32[]{:S(2)}) %collective-permute-start.31) | collective-permute-done | bytes 65568 | tf_op jit(solution)/shard_map/ppermute | solution.py:245
  80.3 7.4 %tile_force.5 = (bf16[4,256,128]{2,1,0:T(8,128)(2,1)S(1)}, bf16[4,256,128]{2,1,0:T(8,128)(2,1)S(1)}, bf16[256,128]{1,0:T(8,128)(2,1)S(1)}, bf16[256,128]{1,0:T(8...) custom-call(s32[8,256]{1,0:T(8,128)S(1)} %get-tuple-element.25.lists_ref, ...), custom_call_target="tpu_custom_call" | custom-call | tf_op jit(solution)/shard_map/tile_force/pallas_call | solution.py:222
  87.8 1.6 %collective-permute-start.44 = (bf16[4,256,128]{2,1,0:T(8,128)(2,1)S(1)}, bf16[4,256,128]{2,1,0:T(8,128)(2,1)S(1)}, u32[]{:S(2)}, u32[]{:S(2)}) collective-permute-start(bf16[4,256,128]{2,1,0:T(8,128)(2,1)S(1)} %get-tuple-element.41), channel_id=1, source_target_pairs={{0,1},{1,0},{2,3},{3,2},{4,5},{5,4},{6,7},{7,6},{8,9},{9,8},{10,11... | collective-permute-start | bytes 786440 | tf_op jit(solution)/shard_map/ppermute | solution.py:245
  89.8 2.4 %collective-permute-done.48 = bf16[256,128]{1,0:T(8,128)(2,1)S(1)} collective-permute-done((bf16[256,128]{1,0:T(8,128)(2,1)S(1)}, bf16[256,128]{1,0:T(8,128)(2,1)S(1)}, u32[]{:S(2)}, u32[]{:S(2)}) %collective-permute-start.48) | collective-permute-done | bytes 65568 | tf_op jit(solution)/shard_map/ppermute | solution.py:245
  93.8 2.2 %collective-permute-start.47 = (bf16[256,128]{1,0:T(8,128)(2,1)S(1)}, bf16[256,128]{1,0:T(8,128)(2,1)S(1)}, u32[]{:S(2)}, u32[]{:S(2)}) collective-permute-start(bf16[256,128]{1,0:T(8,128)(2,1)S(1)} %get-tuple-element.53), channel_id=1, source_target_pairs={{0,6},{1,7},{2,4},{3,5},{4,2},{5,3},{6,0},{7,1},{8,14},{9,15},{10,... | collective-permute-start | bytes 196616 | tf_op jit(solution)/shard_map/ppermute | solution.py:245
  96.7 1.2 %collective-permute-done.49 = bf16[256,128]{1,0:T(8,128)(2,1)S(1)} collective-permute-done((bf16[256,128]{1,0:T(8,128)(2,1)S(1)}, bf16[256,128]{1,0:T(8,128)(2,1)S(1)}, u32[]{:S(2)}, u32[]{:S(2)}) %collective-permute-start.49) | collective-permute-done | bytes 65568 | tf_op jit(solution)/shard_map/ppermute | solution.py:245
  (101 shorter events, 22.7 us)
Async XLA Ops:
  1.5 10.7 %collective-permute-start.8 = (bf16[256,128]{1,0:T(8,128)(2,1)S(1)}, bf16[256,128]{1,0:T(8,128)(2,1)S(1)}, u32[]{:S(2)}, u32[]{:S(2)}) collective-permute-start(bf16[256,128]{1,0:T(8,128)(2,1)S(1)} %convert_element_type.250.refs_8_), channel_id=1, source_target_pairs={{0,16},{8,24},{16,0},{24,8},{1,17},{9,25},{17,1},{25,9},{2,18},{10... | collective-permute-start | bytes 196616 | tf_op jit(solution)/shard_map/ppermute | solution.py:245
  5.6 6.7 %collective-permute-start.7 = (bf16[256,128]{1,0:T(8,128)(2,1)S(1)}, bf16[256,128]{1,0:T(8,128)(2,1)S(1)}, u32[]{:S(2)}, u32[]{:S(2)}) collective-permute-start(bf16[256,128]{1,0:T(8,128)(2,1)S(1)} %convert_element_type.250.refs_8_), channel_id=1, source_target_pairs={{0,8},{8,0},{16,24},{24,16},{1,9},{9,1},{17,25},{25,17},{2,10},{10... | collective-permute-start | bytes 196616 | tf_op jit(solution)/shard_map/ppermute | solution.py:245
  8.1 5.3 %collective-permute-start.2 = (bf16[256,128]{1,0:T(8,128)(2,1)S(1)}, bf16[256,128]{1,0:T(8,128)(2,1)S(1)}, u32[]{:S(2)}, u32[]{:S(2)}) collective-permute-start(bf16[256,128]{1,0:T(8,128)(2,1)S(1)} %convert_element_type.249.refs_0_), channel_id=1, source_target_pairs={{0,6},{1,7},{2,4},{3,5},{4,2},{5,3},{6,0},{7,1},{8,14},{9,15},{10,... | collective-permute-start | bytes 196616 | tf_op jit(solution)/shard_map/ppermute | solution.py:245
  12.2 9.0 %collective-permute-start.3 = (bf16[256,128]{1,0:T(8,128)(2,1)S(1)}, bf16[256,128]{1,0:T(8,128)(2,1)S(1)}, u32[]{:S(2)}, u32[]{:S(2)}) collective-permute-start(bf16[256,128]{1,0:T(8,128)(2,1)S(1)} %convert_element_type.249.refs_0_), channel_id=1, source_target_pairs={{0,1},{1,0},{2,3},{3,2},{4,5},{5,4},{6,7},{7,6},{8,9},{9,8},{10,11... | collective-permute-start | bytes 196616 | tf_op jit(solution)/shard_map/ppermute | solution.py:245
  12.3 8.9 %collective-permute-start.9 = (bf16[256,128]{1,0:T(8,128)(2,1)S(1)}, bf16[256,128]{1,0:T(8,128)(2,1)S(1)}, u32[]{:S(2)}, u32[]{:S(2)}) collective-permute-start(bf16[256,128]{1,0:T(8,128)(2,1)S(1)} %collective-permute-done.8.refs_10_), channel_id=1, source_target_pairs={{0,8},{8,0},{16,24},{24,16},{1,9},{9,1},{17,25},{25,17},{2,10},{10... | collective-permute-start | bytes 196616 | tf_op jit(solution)/shard_map/ppermute | solution.py:245
  13.3 7.9 %collective-permute-start.6 = (bf16[256,128]{1,0:T(8,128)(2,1)S(1)}, bf16[256,128]{1,0:T(8,128)(2,1)S(1)}, u32[]{:S(2)}, u32[]{:S(2)}) collective-permute-start(bf16[256,128]{1,0:T(8,128)(2,1)S(1)} %collective-permute-done.2.refs_3_), channel_id=1, source_target_pairs={{0,1},{1,0},{2,3},{3,2},{4,5},{5,4},{6,7},{7,6},{8,9},{9,8},{10,11... | collective-permute-start | bytes 196616 | tf_op jit(solution)/shard_map/ppermute | solution.py:245
  14.8 6.4 %collective-permute-start.5 = (bf16[256,128]{1,0:T(8,128)(2,1)S(1)}, bf16[256,128]{1,0:T(8,128)(2,1)S(1)}, u32[]{:S(2)}, u32[]{:S(2)}) collective-permute-start(bf16[256,128]{1,0:T(8,128)(2,1)S(1)} %collective-permute-done.1.refs_2_), channel_id=1, source_target_pairs={{0,1},{1,0},{2,3},{3,2},{4,5},{5,4},{6,7},{7,6},{8,9},{9,8},{10,11... | collective-permute-start | bytes 196616 | tf_op jit(solution)/shard_map/ppermute | solution.py:245
  15.3 5.9 %collective-permute-start.4 = (bf16[256,128]{1,0:T(8,128)(2,1)S(1)}, bf16[256,128]{1,0:T(8,128)(2,1)S(1)}, u32[]{:S(2)}, u32[]{:S(2)}) collective-permute-start(bf16[256,128]{1,0:T(8,128)(2,1)S(1)} %collective-permute-done.refs_1_), channel_id=1, source_target_pairs={{0,1},{1,0},{2,3},{3,2},{4,5},{5,4},{6,7},{7,6},{8,9},{9,8},{10,11... | collective-permute-start | bytes 196616 | tf_op jit(solution)/shard_map/ppermute | solution.py:245
  28.7 4.9 %collective-permute-start.21 = (bf16[256,128]{1,0:T(8,128)(2,1)S(1)}, bf16[256,128]{1,0:T(8,128)(2,1)S(1)}, u32[]{:S(2)}, u32[]{:S(2)}) collective-permute-start(bf16[256,128]{1,0:T(8,128)(2,1)S(1)} %get-tuple-element.32), channel_id=1, source_target_pairs={{0,8},{8,0},{16,24},{24,16},{1,9},{9,1},{17,25},{25,17},{2,10},{10... | collective-permute-start | bytes 196616 | tf_op jit(solution)/shard_map/ppermute | solution.py:245
  28.8 4.9 %collective-permute-start.10 = (bf16[4,256,128]{2,1,0:T(8,128)(2,1)S(1)}, bf16[4,256,128]{2,1,0:T(8,128)(2,1)S(1)}, u32[]{:S(2)}, u32[]{:S(2)}) collective-permute-start(bf16[4,256,128]{2,1,0:T(8,128)(2,1)S(1)} %get-tuple-element.29), channel_id=1, source_target_pairs={{0,1},{1,0},{2,3},{3,2},{4,5},{5,4},{6,7},{7,6},{8,9},{9,8},{10,11... | collective-permute-start | bytes 786440 | tf_op jit(solution)/shard_map/ppermute | solution.py:245
  29.5 7.9 %collective-permute-start.23 = (bf16[256,128]{1,0:T(8,128)(2,1)S(1)}, bf16[256,128]{1,0:T(8,128)(2,1)S(1)}, u32[]{:S(2)}, u32[]{:S(2)}) collective-permute-start(bf16[256,128]{1,0:T(8,128)(2,1)S(1)} %get-tuple-element.33), channel_id=1, source_target_pairs={{0,8},{8,0},{16,24},{24,16},{1,9},{9,1},{17,25},{25,17},{2,10},{10... | collective-permute-start | bytes 196616 | tf_op jit(solution)/shard_map/ppermute | solution.py:245
  33.6 5.5 %collective-permute-start.22 = (bf16[256,128]{1,0:T(8,128)(2,1)S(1)}, bf16[256,128]{1,0:T(8,128)(2,1)S(1)}, u32[]{:S(2)}, u32[]{:S(2)}) collective-permute-start(bf16[256,128]{1,0:T(8,128)(2,1)S(1)} %add_convert_fusion.8), channel_id=1, source_target_pairs={{0,16},{8,24},{16,0},{24,8},{1,17},{9,25},{17,1},{25,9},{2,18},{10... | collective-permute-start | bytes 196616 | tf_op jit(solution)/shard_map/ppermute | solution.py:245
  33.8 6.8 %collective-permute-start.11 = (bf16[256,128]{1,0:T(8,128)(2,1)S(1)}, bf16[256,128]{1,0:T(8,128)(2,1)S(1)}, u32[]{:S(2)}, u32[]{:S(2)}) collective-permute-start(bf16[256,128]{1,0:T(8,128)(2,1)S(1)} %get-tuple-element.58), channel_id=1, source_target_pairs={{0,2},{1,3},{2,0},{3,1},{4,6},{5,7},{6,4},{7,5},{8,10},{9,11},{10,... | collective-permute-start | bytes 196616 | tf_op jit(solution)/shard_map/ppermute | solution.py:245
  35.4 5.3 %collective-permute-start.13 = (bf16[256,128]{1,0:T(8,128)(2,1)S(1)}, bf16[256,128]{1,0:T(8,128)(2,1)S(1)}, u32[]{:S(2)}, u32[]{:S(2)}) collective-permute-start(bf16[256,128]{1,0:T(8,128)(2,1)S(1)} %get-tuple-element.59), channel_id=1, source_target_pairs={{0,6},{1,7},{2,4},{3,5},{4,2},{5,3},{6,0},{7,1},{8,14},{9,15},{10,... | collective-permute-start | bytes 196616 | tf_op jit(solution)/shard_map/ppermute | solution.py:245
  39.2 5.9 %collective-permute-start.25 = (bf16[256,128]{1,0:T(8,128)(2,1)S(1)}, bf16[256,128]{1,0:T(8,128)(2,1)S(1)}, u32[]{:S(2)}, u32[]{:S(2)}) collective-permute-start(bf16[256,128]{1,0:T(8,128)(2,1)S(1)} %fusion.25.refs_8_), channel_id=1, source_target_pairs={{0,16},{8,24},{16,0},{24,8},{1,17},{9,25},{17,1},{25,9},{2,18},{10... | collective-permute-start | bytes 196616 | tf_op jit(solution)/shard_map/ppermute | solution.py:245
  40.4 6.3 %collective-permute-start.24 = (bf16[256,128]{1,0:T(8,128)(2,1)S(1)}, bf16[256,128]{1,0:T(8,128)(2,1)S(1)}, u32[]{:S(2)}, u32[]{:S(2)}) collective-permute-start(bf16[256,128]{1,0:T(8,128)(2,1)S(1)} %fusion.25.refs_8_), channel_id=1, source_target_pairs={{0,8},{8,0},{16,24},{24,16},{1,9},{9,1},{17,25},{25,17},{2,10},{10... | collective-permute-start | bytes 196616 | tf_op jit(solution)/shard_map/ppermute | solution.py:245
  41.5 5.9 %collective-permute-start.16 = (bf16[256,128]{1,0:T(8,128)(2,1)S(1)}, bf16[256,128]{1,0:T(8,128)(2,1)S(1)}, u32[]{:S(2)}, u32[]{:S(2)}) collective-permute-start(bf16[256,128]{1,0:T(8,128)(2,1)S(1)} %get-tuple-element.50.refs_0_), channel_id=1, source_target_pairs={{0,6},{1,7},{2,4},{3,5},{4,2},{5,3},{6,0},{7,1},{8,14},{9,15},{10,... | collective-permute-start | bytes 196616 | tf_op jit(solution)/shard_map/ppermute | solution.py:245
  42.9 4.8 %collective-permute-start.15 = (bf16[256,128]{1,0:T(8,128)(2,1)S(1)}, bf16[256,128]{1,0:T(8,128)(2,1)S(1)}, u32[]{:S(2)}, u32[]{:S(2)}) collective-permute-start(bf16[256,128]{1,0:T(8,128)(2,1)S(1)} %get-tuple-element.50.refs_0_), channel_id=1, source_target_pairs={{0,4},{1,5},{2,6},{3,7},{4,0},{5,1},{6,2},{7,3},{8,12},{9,13},{10,... | collective-permute-start | bytes 196616 | tf_op jit(solution)/shard_map/ppermute | solution.py:245
  57.0 4.6 %collective-permute-start.38 = (bf16[256,128]{1,0:T(8,128)(2,1)S(1)}, bf16[256,128]{1,0:T(8,128)(2,1)S(1)}, u32[]{:S(2)}, u32[]{:S(2)}) collective-permute-start(bf16[256,128]{1,0:T(8,128)(2,1)S(1)} %get-tuple-element.38), channel_id=1, source_target_pairs={{0,8},{8,0},{16,24},{24,16},{1,9},{9,1},{17,25},{25,17},{2,10},{10... | collective-permute-start | bytes 196616 | tf_op jit(solution)/shard_map/ppermute | solution.py:245
  57.0 6.2 %collective-permute-start.27 = (bf16[4,256,128]{2,1,0:T(8,128)(2,1)S(1)}, bf16[4,256,128]{2,1,0:T(8,128)(2,1)S(1)}, u32[]{:S(2)}, u32[]{:S(2)}) collective-permute-start(bf16[4,256,128]{2,1,0:T(8,128)(2,1)S(1)} %get-tuple-element.35), channel_id=1, source_target_pairs={{0,1},{1,0},{2,3},{3,2},{4,5},{5,4},{6,7},{7,6},{8,9},{9,8},{10,11... | collective-permute-start | bytes 786440 | tf_op jit(solution)/shard_map/ppermute | solution.py:245
  58.5 8.8 %collective-permute-start.40 = (bf16[256,128]{1,0:T(8,128)(2,1)S(1)}, bf16[256,128]{1,0:T(8,128)(2,1)S(1)}, u32[]{:S(2)}, u32[]{:S(2)}) collective-permute-start(bf16[256,128]{1,0:T(8,128)(2,1)S(1)} %get-tuple-element.39), channel_id=1, source_target_pairs={{0,8},{8,0},{16,24},{24,16},{1,9},{9,1},{17,25},{25,17},{2,10},{10... | collective-permute-start | bytes 196616 | tf_op jit(solution)/shard_map/ppermute | solution.py:245
  61.6 5.7 %collective-permute-start.39 = (bf16[256,128]{1,0:T(8,128)(2,1)S(1)}, bf16[256,128]{1,0:T(8,128)(2,1)S(1)}, u32[]{:S(2)}, u32[]{:S(2)}) collective-permute-start(bf16[256,128]{1,0:T(8,128)(2,1)S(1)} %add_convert_fusion.4), channel_id=1, source_target_pairs={{0,16},{8,24},{16,0},{24,8},{1,17},{9,25},{17,1},{25,9},{2,18},{10... | collective-permute-start | bytes 196616 | tf_op jit(solution)/shard_map/ppermute | solution.py:245
  63.3 6.4 %collective-permute-start.28 = (bf16[256,128]{1,0:T(8,128)(2,1)S(1)}, bf16[256,128]{1,0:T(8,128)(2,1)S(1)}, u32[]{:S(2)}, u32[]{:S(2)}) collective-permute-start(bf16[256,128]{1,0:T(8,128)(2,1)S(1)} %get-tuple-element.55), channel_id=1, source_target_pairs={{0,2},{1,3},{2,0},{3,1},{4,6},{5,7},{6,4},{7,5},{8,10},{9,11},{10,... | collective-permute-start | bytes 196616 | tf_op jit(solution)/shard_map/ppermute | solution.py:245
  65.4 5.2 %collective-permute-start.30 = (bf16[256,128]{1,0:T(8,128)(2,1)S(1)}, bf16[256,128]{1,0:T(8,128)(2,1)S(1)}, u32[]{:S(2)}, u32[]{:S(2)}) collective-permute-start(bf16[256,128]{1,0:T(8,128)(2,1)S(1)} %get-tuple-element.56), channel_id=1, source_target_pairs={{0,6},{1,7},{2,4},{3,5},{4,2},{5,3},{6,0},{7,1},{8,14},{9,15},{10,... | collective-permute-start | bytes 196616 | tf_op jit(solution)/shard_map/ppermute | solution.py:245
  67.4 7.8 %collective-permute-start.42 = (bf16[256,128]{1,0:T(8,128)(2,1)S(1)}, bf16[256,128]{1,0:T(8,128)(2,1)S(1)}, u32[]{:S(2)}, u32[]{:S(2)}) collective-permute-start(bf16[256,128]{1,0:T(8,128)(2,1)S(1)} %get-tuple-element.46.refs_8_), channel_id=1, source_target_pairs={{0,16},{8,24},{16,0},{24,8},{1,17},{9,25},{17,1},{25,9},{2,18},{10... | collective-permute-start | bytes 196616 | tf_op jit(solution)/shard_map/ppermute | solution.py:245
  68.6 8.2 %collective-permute-start.41 = (bf16[256,128]{1,0:T(8,128)(2,1)S(1)}, bf16[256,128]{1,0:T(8,128)(2,1)S(1)}, u32[]{:S(2)}, u32[]{:S(2)}) collective-permute-start(bf16[256,128]{1,0:T(8,128)(2,1)S(1)} %get-tuple-element.46.refs_8_), channel_id=1, source_target_pairs={{0,8},{8,0},{16,24},{24,16},{1,9},{9,1},{17,25},{25,17},{2,10},{10... | collective-permute-start | bytes 196616 | tf_op jit(solution)/shard_map/ppermute | solution.py:245
  71.6 5.2 %collective-permute-start.33 = (bf16[256,128]{1,0:T(8,128)(2,1)S(1)}, bf16[256,128]{1,0:T(8,128)(2,1)S(1)}, u32[]{:S(2)}, u32[]{:S(2)}) collective-permute-start(bf16[256,128]{1,0:T(8,128)(2,1)S(1)} %get-tuple-element.48.refs_0_), channel_id=1, source_target_pairs={{0,6},{1,7},{2,4},{3,5},{4,2},{5,3},{6,0},{7,1},{8,14},{9,15},{10,... | collective-permute-start | bytes 196616 | tf_op jit(solution)/shard_map/ppermute | solution.py:245
  87.8 5.3 %collective-permute-start.44 = (bf16[4,256,128]{2,1,0:T(8,128)(2,1)S(1)}, bf16[4,256,128]{2,1,0:T(8,128)(2,1)S(1)}, u32[]{:S(2)}, u32[]{:S(2)}) collective-permute-start(bf16[4,256,128]{2,1,0:T(8,128)(2,1)S(1)} %get-tuple-element.41), channel_id=1, source_target_pairs={{0,1},{1,0},{2,3},{3,2},{4,5},{5,4},{6,7},{7,6},{8,9},{9,8},{10,11... | collective-permute-start | bytes 786440 | tf_op jit(solution)/shard_map/ppermute | solution.py:245
  89.4 7.3 %collective-permute-start.50 = (bf16[256,128]{1,0:T(8,128)(2,1)S(1)}, bf16[256,128]{1,0:T(8,128)(2,1)S(1)}, u32[]{:S(2)}, u32[]{:S(2)}) collective-permute-start(bf16[256,128]{1,0:T(8,128)(2,1)S(1)} %get-tuple-element.45), channel_id=1, source_target_pairs={{0,8},{8,0},{16,24},{24,16},{1,9},{9,1},{17,25},{25,17},{2,10},{10... | collective-permute-start | bytes 196616 | tf_op jit(solution)/shard_map/ppermute | solution.py:245
  92.2 5.7 %collective-permute-start.49 = (bf16[256,128]{1,0:T(8,128)(2,1)S(1)}, bf16[256,128]{1,0:T(8,128)(2,1)S(1)}, u32[]{:S(2)}, u32[]{:S(2)}) collective-permute-start(bf16[256,128]{1,0:T(8,128)(2,1)S(1)} %add_convert_fusion), channel_id=1, source_target_pairs={{0,16},{8,24},{16,0},{24,8},{1,17},{9,25},{17,1},{25,9},{2,18},{10... | collective-permute-start | bytes 196616 | tf_op jit(solution)/shard_map/ppermute | solution.py:245
  93.2 5.5 %collective-permute-start.45 = (bf16[256,128]{1,0:T(8,128)(2,1)S(1)}, bf16[256,128]{1,0:T(8,128)(2,1)S(1)}, u32[]{:S(2)}, u32[]{:S(2)}) collective-permute-start(bf16[256,128]{1,0:T(8,128)(2,1)S(1)} %get-tuple-element.52), channel_id=1, source_target_pairs={{0,2},{1,3},{2,0},{3,1},{4,6},{5,7},{6,4},{7,5},{8,10},{9,11},{10,... | collective-permute-start | bytes 196616 | tf_op jit(solution)/shard_map/ppermute | solution.py:245
  93.8 5.5 %collective-permute-start.47 = (bf16[256,128]{1,0:T(8,128)(2,1)S(1)}, bf16[256,128]{1,0:T(8,128)(2,1)S(1)}, u32[]{:S(2)}, u32[]{:S(2)}) collective-permute-start(bf16[256,128]{1,0:T(8,128)(2,1)S(1)} %get-tuple-element.53), channel_id=1, source_target_pairs={{0,6},{1,7},{2,4},{3,5},{4,2},{5,3},{6,0},{7,1},{8,14},{9,15},{10,... | collective-permute-start | bytes 196616 | tf_op jit(solution)/shard_map/ppermute | solution.py:245
  (25 other events, 198.7 us)

commit v3 on v2

--- a/solution.py
+++ b/solution.py
@@ -11,6 +11,7 @@
 LEAPS = 2
 GROUP = 4
 UNROLL = 4
+PAIRS = 8
 
 
 degrees_free = 4.0
@@ -116,11 +117,11 @@
             tile = (comp_seconds if n % 2 else comp_firsts)[n // 2][i * side : (i + 1) * side]
             fill(n * comp_per + i, tile, comp_tiles, comp_flip, comp_acc)
 
-    def steps(count):
-        return lax.div(count + (UNROLL - 1), UNROLL)
+    def steps(count, unroll):
+        return lax.div(count + (unroll - 1), unroll)
 
     def pair_at(step):
-        spots = [step * UNROLL + n for n in range(UNROLL)]
+        spots = [step * PAIRS + n for n in range(PAIRS)]
         return [(spot, lists_ref[GROUP + 1, spot], lists_ref[GROUP + 2, spot]) for spot in spots]
 
     last = pred.shape[0] - 1
@@ -137,12 +138,12 @@
             total[spot] = jnp.zeros(total.shape[1:], total.dtype)
         return unused
 
-    lax.fori_loop(0, steps(pairs), predict, 0)
+    lax.fori_loop(0, steps(pairs, PAIRS), predict, 0)
 
     one = degrees_free * noise_scale * noise_scale
+    assert one == 1.0
 
     def weigh(step, unused):
-        sums = []
         for n in range(UNROLL):
             group = step * UNROLL + n
             spot = lists_ref[GROUP, group]
@@ -151,15 +152,16 @@
             for m in range(GROUP):
                 slot = lists_ref[m, group]
                 resid = values_ref[slot].astype(jnp.float32) - guess
-                inverse = pl.reciprocal(one + resid * resid, approx=True)
-                scaled = resid * weight_ref[slot].astype(jnp.float32) * inverse
+                scaled = weight_ref[slot].astype(jnp.float32)
+                if m % 2:
+                    scaled *= pl.reciprocal(resid + pl.reciprocal(resid, approx=True), approx=True)
+                else:
+                    scaled *= resid * pl.reciprocal(one + resid * resid, approx=True)
                 whole = scaled if whole is None else whole + scaled
-            sums.append((spot, whole))
-        for spot, whole in sums:
             total[spot] += whole
         return unused
 
-    lax.fori_loop(0, steps(groups), weigh, 0)
+    lax.fori_loop(0, steps(groups, UNROLL), weigh, 0)
 
     def gather(step, unused):
         parts = []
@@ -173,7 +175,7 @@
             targ_acc[j] += targ_part
         return unused
 
-    lax.fori_loop(0, steps(pairs), gather, 0)
+    lax.fori_loop(0, steps(pairs, PAIRS), gather, 0)
 
     gain = degrees_free + 1.0
     for n in range(cols):

time: 101 us -> 98.6 us (0.976); the launches traced: 101 us -> 99.9 us
  Pallas kernels: 27.5 us -> 23.6 us
  starting transfers between devices: 44.4 us -> 48.1 us
  waiting for transfers between devices: 23 us -> 21.9 us
    ppermute x51, starting transfers between devices: 44.4 us -> 48.1 us  [swap(): return lax.ppermute(block, axis, [(i, i ^ offset) for i in range(size)])]
    pallas_call x3, Pallas kernels: 22.3 us -> 19.1 us  [local_grads(): pl.pallas_call(functools.partial(force_kernel, cols, rows), out_shape=[co...]
    ppermute x51, waiting for transfers between devices: 23 us -> 21.9 us  [swap(): return lax.ppermute(block, axis, [(i, i ^ offset) for i in range(size)])]
  transfers between devices with their start and end apart: 51 -> 51, of which waited for: 24 -> 18; matrix products, arithmetic and copies ran while one was open for 3% -> 3% of each run, Pallas kernels for 5% -> 5%
where the time goes in v3:
time: 98.6 us; the launch traced here: 99.9 us
  starting transfers between devices  48.1 us (49%)
  Pallas kernels  23.6 us (24%)
  waiting for transfers between devices  21.9 us (22%)
  other arithmetic  4.67 us (5%)
  between operations  1.56 us (2%)
    ppermute x51, starting transfers between devices, swap(): return lax.ppermute(block, axis, [(i, i ^ offset) for i in range(size)])  48.1 us
    ppermute x51, waiting for transfers between devices, swap(): return lax.ppermute(block, axis, [(i, i ^ offset) for i in range(size)])  21.9 us
    pallas_call x3, Pallas kernels, local_grads(): pl.pallas_call(functools.partial(force_kernel, cols, rows), out_shape=[co...  19.1 us
    pallas_call x1, Pallas kernels, load_tiles(): pl.pallas_call(functools.partial(load_kernel, targ_group, shape), out_sha...  4.56 us
  transfers between devices with their start and end apart: 51, of which 18 were waited for; matrix products, arithmetic and copies ran while one was open for 3% of the time, Pallas kernels for 5%

profile of v3, /device:TPU:0, one launch (start us, length us, event | category | flops | bytes accessed | tf_op | source)
XLA Modules:
  0.0 99.9 jit_solution(11544616981178392597)
XLA Ops:
  1.5 4.0 %collective-permute-start.8 = (bf16[256,128]{1,0:T(8,128)(2,1)S(1)}, bf16[256,128]{1,0:T(8,128)(2,1)S(1)}, u32[]{:S(2)}, u32[]{:S(2)}) collective-permute-start(bf16[256,128]{1,0:T(8,128)(2,1)S(1)} %convert_element_type.250.refs_8_), channel_id=1, source_target_pairs={{0,16},{8,24},{16,0},{24,8},{1,17},{9,25},{17,1},{25,9},{2,18},{10... | collective-permute-start | bytes 196616 | tf_op jit(solution)/shard_map/ppermute | solution.py:247
  5.6 1.6 %collective-permute-start.7 = (bf16[256,128]{1,0:T(8,128)(2,1)S(1)}, bf16[256,128]{1,0:T(8,128)(2,1)S(1)}, u32[]{:S(2)}, u32[]{:S(2)}) collective-permute-start(bf16[256,128]{1,0:T(8,128)(2,1)S(1)} %convert_element_type.250.refs_8_), channel_id=1, source_target_pairs={{0,8},{8,0},{16,24},{24,16},{1,9},{9,1},{17,25},{25,17},{2,10},{10... | collective-permute-start | bytes 196616 | tf_op jit(solution)/shard_map/ppermute | solution.py:247
  8.1 2.4 %collective-permute-start.2 = (bf16[256,128]{1,0:T(8,128)(2,1)S(1)}, bf16[256,128]{1,0:T(8,128)(2,1)S(1)}, u32[]{:S(2)}, u32[]{:S(2)}) collective-permute-start(bf16[256,128]{1,0:T(8,128)(2,1)S(1)} %convert_element_type.249.refs_0_), channel_id=1, source_target_pairs={{0,6},{1,7},{2,4},{3,5},{4,2},{5,3},{6,0},{7,1},{8,14},{9,15},{10,... | collective-permute-start | bytes 196616 | tf_op jit(solution)/shard_map/ppermute | solution.py:247
  13.3 1.4 %collective-permute-done.1.refs_2_ = bf16[256,128]{1,0:T(8,128)(2,1)S(1)} collective-permute-done((bf16[256,128]{1,0:T(8,128)(2,1)S(1)}, bf16[256,128]{1,0:T(8,128)(2,1)S(1)}, u32[]{:S(2)}, u32[]{:S(2)}) %collective-permute-start.1) | collective-permute-done | bytes 65568 | tf_op jit(solution)/shard_map/ppermute | solution.py:247
  16.0 4.6 %tile_load.1 = (bf16[257,128,128]{2,1,0:T(8,128)(2,1)S(1)}, bf16[257,128,128]{2,1,0:T(8,128)(2,1)S(1)}, s32[8,256]{1,0:T(8,128)S(1)}) custom-call(s32[1,256]{1,0:T(1,128)S(1)} %compare_select_fusion.pair_ref, s32[1]{0:T(128)} %copy.13.live_ref, bf16[256,128,128]{2,1,0:T(8,128)(2,1)} %bitcast.64, bf16[256,128,128]{2,1,0:T(8,128)(2,1)} %bitcast.65), custom_call_target="tpu_custom_call" | custom-call | tf_op jit(solution)/shard_map/tile_load/pallas_call | solution.py:203
  20.7 6.4 %tile_force.3 = (bf16[4,256,128]{2,1,0:T(8,128)(2,1)S(1)}, bf16[4,256,128]{2,1,0:T(8,128)(2,1)S(1)}, bf16[256,128]{1,0:T(8,128)(2,1)S(1)}, bf16[256,128]{1,0:T(8...) custom-call(s32[8,256]{1,0:T(8,128)S(1)} %get-tuple-element.25.lists_ref, ...), custom_call_target="tpu_custom_call" | custom-call | tf_op jit(solution)/shard_map/tile_force/pallas_call | solution.py:224
  27.4 1.8 %collective-permute-start.23 = (bf16[256,128]{1,0:T(8,128)(2,1)S(1)}, bf16[256,128]{1,0:T(8,128)(2,1)S(1)}, u32[]{:S(2)}, u32[]{:S(2)}) collective-permute-start(bf16[256,128]{1,0:T(8,128)(2,1)S(1)} %get-tuple-element.33), channel_id=1, source_target_pairs={{0,8},{8,0},{16,24},{24,16},{1,9},{9,1},{17,25},{25,17},{2,10},{10... | collective-permute-start | bytes 196616 | tf_op jit(solution)/shard_map/ppermute | solution.py:247
  29.2 2.9 %collective-permute-done.21 = bf16[256,128]{1,0:T(8,128)(2,1)S(1)} collective-permute-done((bf16[256,128]{1,0:T(8,128)(2,1)S(1)}, bf16[256,128]{1,0:T(8,128)(2,1)S(1)}, u32[]{:S(2)}, u32[]{:S(2)}) %collective-permute-start.21) | collective-permute-done | bytes 65568 | tf_op jit(solution)/shard_map/ppermute | solution.py:247
  32.1 1.2 %collective-permute-start.22 = (bf16[256,128]{1,0:T(8,128)(2,1)S(1)}, bf16[256,128]{1,0:T(8,128)(2,1)S(1)}, u32[]{:S(2)}, u32[]{:S(2)}) collective-permute-start(bf16[256,128]{1,0:T(8,128)(2,1)S(1)} %add_convert_fusion.8), channel_id=1, source_target_pairs={{0,16},{8,24},{16,0},{24,8},{1,17},{9,25},{17,1},{25,9},{2,18},{10... | collective-permute-start | bytes 196616 | tf_op jit(solution)/shard_map/ppermute | solution.py:247
  33.3 3.2 %collective-permute-start.11 = (bf16[256,128]{1,0:T(8,128)(2,1)S(1)}, bf16[256,128]{1,0:T(8,128)(2,1)S(1)}, u32[]{:S(2)}, u32[]{:S(2)}) collective-permute-start(bf16[256,128]{1,0:T(8,128)(2,1)S(1)} %get-tuple-element.58), channel_id=1, source_target_pairs={{0,2},{1,3},{2,0},{3,1},{4,6},{5,7},{6,4},{7,5},{8,10},{9,11},{10,... | collective-permute-start | bytes 196616 | tf_op jit(solution)/shard_map/ppermute | solution.py:247
  36.5 1.5 %collective-permute-start.12 = (bf16[256,128]{1,0:T(8,128)(2,1)S(1)}, bf16[256,128]{1,0:T(8,128)(2,1)S(1)}, u32[]{:S(2)}, u32[]{:S(2)}) collective-permute-start(bf16[256,128]{1,0:T(8,128)(2,1)S(1)} %get-tuple-element.60), channel_id=1, source_target_pairs={{0,4},{1,5},{2,6},{3,7},{4,0},{5,1},{6,2},{7,3},{8,12},{9,13},{10,... | collective-permute-start | bytes 196616 | tf_op jit(solution)/shard_map/ppermute | solution.py:247
  38.8 1.6 %collective-permute-start.24 = (bf16[256,128]{1,0:T(8,128)(2,1)S(1)}, bf16[256,128]{1,0:T(8,128)(2,1)S(1)}, u32[]{:S(2)}, u32[]{:S(2)}) collective-permute-start(bf16[256,128]{1,0:T(8,128)(2,1)S(1)} %fusion.25.refs_8_), channel_id=1, source_target_pairs={{0,8},{8,0},{16,24},{24,16},{1,9},{9,1},{17,25},{25,17},{2,10},{10... | collective-permute-start | bytes 196616 | tf_op jit(solution)/shard_map/ppermute | solution.py:247
  40.4 1.3 %collective-permute-done.13 = bf16[256,128]{1,0:T(8,128)(2,1)S(1)} collective-permute-done((bf16[256,128]{1,0:T(8,128)(2,1)S(1)}, bf16[256,128]{1,0:T(8,128)(2,1)S(1)}, u32[]{:S(2)}, u32[]{:S(2)}) %collective-permute-start.13) | collective-permute-done | bytes 65568 | tf_op jit(solution)/shard_map/ppermute | solution.py:247
  41.8 2.1 %collective-permute-start.16 = (bf16[256,128]{1,0:T(8,128)(2,1)S(1)}, bf16[256,128]{1,0:T(8,128)(2,1)S(1)}, u32[]{:S(2)}, u32[]{:S(2)}) collective-permute-start(bf16[256,128]{1,0:T(8,128)(2,1)S(1)} %get-tuple-element.50.refs_0_), channel_id=1, source_target_pairs={{0,6},{1,7},{2,4},{3,5},{4,2},{5,3},{6,0},{7,1},{8,14},{9,15},{10,... | collective-permute-start | bytes 196616 | tf_op jit(solution)/shard_map/ppermute | solution.py:247
  44.1 1.3 %collective-permute-start.14 = (bf16[256,128]{1,0:T(8,128)(2,1)S(1)}, bf16[256,128]{1,0:T(8,128)(2,1)S(1)}, u32[]{:S(2)}, u32[]{:S(2)}) collective-permute-start(bf16[256,128]{1,0:T(8,128)(2,1)S(1)} %get-tuple-element.50.refs_0_), channel_id=1, source_target_pairs={{0,2},{1,3},{2,0},{3,1},{4,6},{5,7},{6,4},{7,5},{8,10},{9,11},{10,... | collective-permute-start | bytes 196616 | tf_op jit(solution)/shard_map/ppermute | solution.py:247
  45.4 1.6 %collective-permute-done.16.refs_3_ = bf16[256,128]{1,0:T(8,128)(2,1)S(1)} collective-permute-done((bf16[256,128]{1,0:T(8,128)(2,1)S(1)}, bf16[256,128]{1,0:T(8,128)(2,1)S(1)}, u32[]{:S(2)}, u32[]{:S(2)}) %collective-permute-start.16) | collective-permute-done | bytes 65568 | tf_op jit(solution)/shard_map/ppermute | solution.py:247
  47.0 1.1 %collective-permute-done.15.refs_2_ = bf16[256,128]{1,0:T(8,128)(2,1)S(1)} collective-permute-done((bf16[256,128]{1,0:T(8,128)(2,1)S(1)}, bf16[256,128]{1,0:T(8,128)(2,1)S(1)}, u32[]{:S(2)}, u32[]{:S(2)}) %collective-permute-start.15) | collective-permute-done | bytes 65568 | tf_op jit(solution)/shard_map/ppermute | solution.py:247
  49.6 6.4 %tile_force.4 = (bf16[4,256,128]{2,1,0:T(8,128)(2,1)S(1)}, bf16[4,256,128]{2,1,0:T(8,128)(2,1)S(1)}, bf16[256,128]{1,0:T(8,128)(2,1)S(1)}, bf16[256,128]{1,0:T(8...) custom-call(s32[8,256]{1,0:T(8,128)S(1)} %get-tuple-element.25.lists_ref, ...), custom_call_target="tpu_custom_call" | custom-call | tf_op jit(solution)/shard_map/tile_force/pallas_call | solution.py:224
  58.1 2.5 %collective-permute-done.38 = bf16[256,128]{1,0:T(8,128)(2,1)S(1)} collective-permute-done((bf16[256,128]{1,0:T(8,128)(2,1)S(1)}, bf16[256,128]{1,0:T(8,128)(2,1)S(1)}, u32[]{:S(2)}, u32[]{:S(2)}) %collective-permute-start.38) | collective-permute-done | bytes 65568 | tf_op jit(solution)/shard_map/ppermute | solution.py:247
  60.6 1.6 %collective-permute-start.39 = (bf16[256,128]{1,0:T(8,128)(2,1)S(1)}, bf16[256,128]{1,0:T(8,128)(2,1)S(1)}, u32[]{:S(2)}, u32[]{:S(2)}) collective-permute-start(bf16[256,128]{1,0:T(8,128)(2,1)S(1)} %add_convert_fusion.4), channel_id=1, source_target_pairs={{0,16},{8,24},{16,0},{24,8},{1,17},{9,25},{17,1},{25,9},{2,18},{10... | collective-permute-start | bytes 196616 | tf_op jit(solution)/shard_map/ppermute | solution.py:247
  62.2 2.5 %collective-permute-start.28 = (bf16[256,128]{1,0:T(8,128)(2,1)S(1)}, bf16[256,128]{1,0:T(8,128)(2,1)S(1)}, u32[]{:S(2)}, u32[]{:S(2)}) collective-permute-start(bf16[256,128]{1,0:T(8,128)(2,1)S(1)} %get-tuple-element.55), channel_id=1, source_target_pairs={{0,2},{1,3},{2,0},{3,1},{4,6},{5,7},{6,4},{7,5},{8,10},{9,11},{10,... | collective-permute-start | bytes 196616 | tf_op jit(solution)/shard_map/ppermute | solution.py:247
  64.8 1.5 %collective-permute-start.29 = (bf16[256,128]{1,0:T(8,128)(2,1)S(1)}, bf16[256,128]{1,0:T(8,128)(2,1)S(1)}, u32[]{:S(2)}, u32[]{:S(2)}) collective-permute-start(bf16[256,128]{1,0:T(8,128)(2,1)S(1)} %get-tuple-element.57), channel_id=1, source_target_pairs={{0,4},{1,5},{2,6},{3,7},{4,0},{5,1},{6,2},{7,3},{8,12},{9,13},{10,... | collective-permute-start | bytes 196616 | tf_op jit(solution)/shard_map/ppermute | solution.py:247
  67.6 2.3 %collective-permute-start.41 = (bf16[256,128]{1,0:T(8,128)(2,1)S(1)}, bf16[256,128]{1,0:T(8,128)(2,1)S(1)}, u32[]{:S(2)}, u32[]{:S(2)}) collective-permute-start(bf16[256,128]{1,0:T(8,128)(2,1)S(1)} %get-tuple-element.46.refs_8_), channel_id=1, source_target_pairs={{0,8},{8,0},{16,24},{24,16},{1,9},{9,1},{17,25},{25,17},{2,10},{10... | collective-permute-start | bytes 196616 | tf_op jit(solution)/shard_map/ppermute | solution.py:247
  70.0 2.1 %collective-permute-start.33 = (bf16[256,128]{1,0:T(8,128)(2,1)S(1)}, bf16[256,128]{1,0:T(8,128)(2,1)S(1)}, u32[]{:S(2)}, u32[]{:S(2)}) collective-permute-start(bf16[256,128]{1,0:T(8,128)(2,1)S(1)} %get-tuple-element.48.refs_0_), channel_id=1, source_target_pairs={{0,6},{1,7},{2,4},{3,5},{4,2},{5,3},{6,0},{7,1},{8,14},{9,15},{10,... | collective-permute-start | bytes 196616 | tf_op jit(solution)/shard_map/ppermute | solution.py:247
  72.4 1.2 %collective-permute-start.31 = (bf16[256,128]{1,0:T(8,128)(2,1)S(1)}, bf16[256,128]{1,0:T(8,128)(2,1)S(1)}, u32[]{:S(2)}, u32[]{:S(2)}) collective-permute-start(bf16[256,128]{1,0:T(8,128)(2,1)S(1)} %get-tuple-element.48.refs_0_), channel_id=1, source_target_pairs={{0,2},{1,3},{2,0},{3,1},{4,6},{5,7},{6,4},{7,5},{8,10},{9,11},{10,... | collective-permute-start | bytes 196616 | tf_op jit(solution)/shard_map/ppermute | solution.py:247
  75.3 1.1 %collective-permute-done.32.refs_2_ = bf16[256,128]{1,0:T(8,128)(2,1)S(1)} collective-permute-done((bf16[256,128]{1,0:T(8,128)(2,1)S(1)}, bf16[256,128]{1,0:T(8,128)(2,1)S(1)}, u32[]{:S(2)}, u32[]{:S(2)}) %collective-permute-start.32) | collective-permute-done | bytes 65568 | tf_op jit(solution)/shard_map/ppermute | solution.py:247
  77.9 6.4 %tile_force.5 = (bf16[4,256,128]{2,1,0:T(8,128)(2,1)S(1)}, bf16[4,256,128]{2,1,0:T(8,128)(2,1)S(1)}, bf16[256,128]{1,0:T(8,128)(2,1)S(1)}, bf16[256,128]{1,0:T(8...) custom-call(s32[8,256]{1,0:T(8,128)S(1)} %get-tuple-element.25.lists_ref, ...), custom_call_target="tpu_custom_call" | custom-call | tf_op jit(solution)/shard_map/tile_force/pallas_call | solution.py:224
  86.4 2.4 %collective-permute-done.48 = bf16[256,128]{1,0:T(8,128)(2,1)S(1)} collective-permute-done((bf16[256,128]{1,0:T(8,128)(2,1)S(1)}, bf16[256,128]{1,0:T(8,128)(2,1)S(1)}, u32[]{:S(2)}, u32[]{:S(2)}) %collective-permute-start.48) | collective-permute-done | bytes 65568 | tf_op jit(solution)/shard_map/ppermute | solution.py:247
  88.8 2.2 %collective-permute-start.49 = (bf16[256,128]{1,0:T(8,128)(2,1)S(1)}, bf16[256,128]{1,0:T(8,128)(2,1)S(1)}, u32[]{:S(2)}, u32[]{:S(2)}) collective-permute-start(bf16[256,128]{1,0:T(8,128)(2,1)S(1)} %add_convert_fusion), channel_id=1, source_target_pairs={{0,16},{8,24},{16,0},{24,8},{1,17},{9,25},{17,1},{25,9},{2,18},{10... | collective-permute-start | bytes 196616 | tf_op jit(solution)/shard_map/ppermute | solution.py:247
  91.1 2.8 %collective-permute-start.45 = (bf16[256,128]{1,0:T(8,128)(2,1)S(1)}, bf16[256,128]{1,0:T(8,128)(2,1)S(1)}, u32[]{:S(2)}, u32[]{:S(2)}) collective-permute-start(bf16[256,128]{1,0:T(8,128)(2,1)S(1)} %get-tuple-element.52), channel_id=1, source_target_pairs={{0,2},{1,3},{2,0},{3,1},{4,6},{5,7},{6,4},{7,5},{8,10},{9,11},{10,... | collective-permute-start | bytes 196616 | tf_op jit(solution)/shard_map/ppermute | solution.py:247
  93.9 1.5 %collective-permute-start.46 = (bf16[256,128]{1,0:T(8,128)(2,1)S(1)}, bf16[256,128]{1,0:T(8,128)(2,1)S(1)}, u32[]{:S(2)}, u32[]{:S(2)}) collective-permute-start(bf16[256,128]{1,0:T(8,128)(2,1)S(1)} %get-tuple-element.54), channel_id=1, source_target_pairs={{0,4},{1,5},{2,6},{3,7},{4,0},{5,1},{6,2},{7,3},{8,12},{9,13},{10,... | collective-permute-start | bytes 196616 | tf_op jit(solution)/shard_map/ppermute | solution.py:247
  96.3 2.8 %collective-permute-done.47 = bf16[256,128]{1,0:T(8,128)(2,1)S(1)} collective-permute-done((bf16[256,128]{1,0:T(8,128)(2,1)S(1)}, bf16[256,128]{1,0:T(8,128)(2,1)S(1)}, u32[]{:S(2)}, u32[]{:S(2)}) %collective-permute-start.47) | collective-permute-done | bytes 65568 | tf_op jit(solution)/shard_map/ppermute | solution.py:247
  (101 shorter events, 19.0 us)
Async XLA Ops:
  1.5 10.7 %collective-permute-start.8 = (bf16[256,128]{1,0:T(8,128)(2,1)S(1)}, bf16[256,128]{1,0:T(8,128)(2,1)S(1)}, u32[]{:S(2)}, u32[]{:S(2)}) collective-permute-start(bf16[256,128]{1,0:T(8,128)(2,1)S(1)} %convert_element_type.250.refs_8_), channel_id=1, source_target_pairs={{0,16},{8,24},{16,0},{24,8},{1,17},{9,25},{17,1},{25,9},{2,18},{10... | collective-permute-start | bytes 196616 | tf_op jit(solution)/shard_map/ppermute | solution.py:247
  5.6 6.7 %collective-permute-start.7 = (bf16[256,128]{1,0:T(8,128)(2,1)S(1)}, bf16[256,128]{1,0:T(8,128)(2,1)S(1)}, u32[]{:S(2)}, u32[]{:S(2)}) collective-permute-start(bf16[256,128]{1,0:T(8,128)(2,1)S(1)} %convert_element_type.250.refs_8_), channel_id=1, source_target_pairs={{0,8},{8,0},{16,24},{24,16},{1,9},{9,1},{17,25},{25,17},{2,10},{10... | collective-permute-start | bytes 196616 | tf_op jit(solution)/shard_map/ppermute | solution.py:247
  8.1 5.3 %collective-permute-start.2 = (bf16[256,128]{1,0:T(8,128)(2,1)S(1)}, bf16[256,128]{1,0:T(8,128)(2,1)S(1)}, u32[]{:S(2)}, u32[]{:S(2)}) collective-permute-start(bf16[256,128]{1,0:T(8,128)(2,1)S(1)} %convert_element_type.249.refs_0_), channel_id=1, source_target_pairs={{0,6},{1,7},{2,4},{3,5},{4,2},{5,3},{6,0},{7,1},{8,14},{9,15},{10,... | collective-permute-start | bytes 196616 | tf_op jit(solution)/shard_map/ppermute | solution.py:247
  12.2 8.4 %collective-permute-start.3 = (bf16[256,128]{1,0:T(8,128)(2,1)S(1)}, bf16[256,128]{1,0:T(8,128)(2,1)S(1)}, u32[]{:S(2)}, u32[]{:S(2)}) collective-permute-start(bf16[256,128]{1,0:T(8,128)(2,1)S(1)} %convert_element_type.249.refs_0_), channel_id=1, source_target_pairs={{0,1},{1,0},{2,3},{3,2},{4,5},{5,4},{6,7},{7,6},{8,9},{9,8},{10,11... | collective-permute-start | bytes 196616 | tf_op jit(solution)/shard_map/ppermute | solution.py:247
  12.3 8.3 %collective-permute-start.9 = (bf16[256,128]{1,0:T(8,128)(2,1)S(1)}, bf16[256,128]{1,0:T(8,128)(2,1)S(1)}, u32[]{:S(2)}, u32[]{:S(2)}) collective-permute-start(bf16[256,128]{1,0:T(8,128)(2,1)S(1)} %collective-permute-done.8.refs_10_), channel_id=1, source_target_pairs={{0,8},{8,0},{16,24},{24,16},{1,9},{9,1},{17,25},{25,17},{2,10},{10... | collective-permute-start | bytes 196616 | tf_op jit(solution)/shard_map/ppermute | solution.py:247
  13.3 7.3 %collective-permute-start.6 = (bf16[256,128]{1,0:T(8,128)(2,1)S(1)}, bf16[256,128]{1,0:T(8,128)(2,1)S(1)}, u32[]{:S(2)}, u32[]{:S(2)}) collective-permute-start(bf16[256,128]{1,0:T(8,128)(2,1)S(1)} %collective-permute-done.2.refs_3_), channel_id=1, source_target_pairs={{0,1},{1,0},{2,3},{3,2},{4,5},{5,4},{6,7},{7,6},{8,9},{9,8},{10,11... | collective-permute-start | bytes 196616 | tf_op jit(solution)/shard_map/ppermute | solution.py:247
  14.8 5.8 %collective-permute-start.5 = (bf16[256,128]{1,0:T(8,128)(2,1)S(1)}, bf16[256,128]{1,0:T(8,128)(2,1)S(1)}, u32[]{:S(2)}, u32[]{:S(2)}) collective-permute-start(bf16[256,128]{1,0:T(8,128)(2,1)S(1)} %collective-permute-done.1.refs_2_), channel_id=1, source_target_pairs={{0,1},{1,0},{2,3},{3,2},{4,5},{5,4},{6,7},{7,6},{8,9},{9,8},{10,11... | collective-permute-start | bytes 196616 | tf_op jit(solution)/shard_map/ppermute | solution.py:247
  15.3 5.3 %collective-permute-start.4 = (bf16[256,128]{1,0:T(8,128)(2,1)S(1)}, bf16[256,128]{1,0:T(8,128)(2,1)S(1)}, u32[]{:S(2)}, u32[]{:S(2)}) collective-permute-start(bf16[256,128]{1,0:T(8,128)(2,1)S(1)} %collective-permute-done.refs_1_), channel_id=1, source_target_pairs={{0,1},{1,0},{2,3},{3,2},{4,5},{5,4},{6,7},{7,6},{8,9},{9,8},{10,11... | collective-permute-start | bytes 196616 | tf_op jit(solution)/shard_map/ppermute | solution.py:247
  27.1 6.1 %collective-permute-start.10 = (bf16[4,256,128]{2,1,0:T(8,128)(2,1)S(1)}, bf16[4,256,128]{2,1,0:T(8,128)(2,1)S(1)}, u32[]{:S(2)}, u32[]{:S(2)}) collective-permute-start(bf16[4,256,128]{2,1,0:T(8,128)(2,1)S(1)} %get-tuple-element.29), channel_id=1, source_target_pairs={{0,1},{1,0},{2,3},{3,2},{4,5},{5,4},{6,7},{7,6},{8,9},{9,8},{10,11... | collective-permute-start | bytes 786440 | tf_op jit(solution)/shard_map/ppermute | solution.py:247
  27.4 10.6 %collective-permute-start.23 = (bf16[256,128]{1,0:T(8,128)(2,1)S(1)}, bf16[256,128]{1,0:T(8,128)(2,1)S(1)}, u32[]{:S(2)}, u32[]{:S(2)}) collective-permute-start(bf16[256,128]{1,0:T(8,128)(2,1)S(1)} %get-tuple-element.33), channel_id=1, source_target_pairs={{0,8},{8,0},{16,24},{24,16},{1,9},{9,1},{17,25},{25,17},{2,10},{10... | collective-permute-start | bytes 196616 | tf_op jit(solution)/shard_map/ppermute | solution.py:247
  32.1 6.0 %collective-permute-start.22 = (bf16[256,128]{1,0:T(8,128)(2,1)S(1)}, bf16[256,128]{1,0:T(8,128)(2,1)S(1)}, u32[]{:S(2)}, u32[]{:S(2)}) collective-permute-start(bf16[256,128]{1,0:T(8,128)(2,1)S(1)} %add_convert_fusion.8), channel_id=1, source_target_pairs={{0,16},{8,24},{16,0},{24,8},{1,17},{9,25},{17,1},{25,9},{2,18},{10... | collective-permute-start | bytes 196616 | tf_op jit(solution)/shard_map/ppermute | solution.py:247
  33.3 7.1 %collective-permute-start.11 = (bf16[256,128]{1,0:T(8,128)(2,1)S(1)}, bf16[256,128]{1,0:T(8,128)(2,1)S(1)}, u32[]{:S(2)}, u32[]{:S(2)}) collective-permute-start(bf16[256,128]{1,0:T(8,128)(2,1)S(1)} %get-tuple-element.58), channel_id=1, source_target_pairs={{0,2},{1,3},{2,0},{3,1},{4,6},{5,7},{6,4},{7,5},{8,10},{9,11},{10,... | collective-permute-start | bytes 196616 | tf_op jit(solution)/shard_map/ppermute | solution.py:247
  36.5 5.2 %collective-permute-start.13 = (bf16[256,128]{1,0:T(8,128)(2,1)S(1)}, bf16[256,128]{1,0:T(8,128)(2,1)S(1)}, u32[]{:S(2)}, u32[]{:S(2)}) collective-permute-start(bf16[256,128]{1,0:T(8,128)(2,1)S(1)} %get-tuple-element.59), channel_id=1, source_target_pairs={{0,6},{1,7},{2,4},{3,5},{4,2},{5,3},{6,0},{7,1},{8,14},{9,15},{10,... | collective-permute-start | bytes 196616 | tf_op jit(solution)/shard_map/ppermute | solution.py:247
  36.5 5.2 %collective-permute-start.12 = (bf16[256,128]{1,0:T(8,128)(2,1)S(1)}, bf16[256,128]{1,0:T(8,128)(2,1)S(1)}, u32[]{:S(2)}, u32[]{:S(2)}) collective-permute-start(bf16[256,128]{1,0:T(8,128)(2,1)S(1)} %get-tuple-element.60), channel_id=1, source_target_pairs={{0,4},{1,5},{2,6},{3,7},{4,0},{5,1},{6,2},{7,3},{8,12},{9,13},{10,... | collective-permute-start | bytes 196616 | tf_op jit(solution)/shard_map/ppermute | solution.py:247
  38.1 7.2 %collective-permute-start.25 = (bf16[256,128]{1,0:T(8,128)(2,1)S(1)}, bf16[256,128]{1,0:T(8,128)(2,1)S(1)}, u32[]{:S(2)}, u32[]{:S(2)}) collective-permute-start(bf16[256,128]{1,0:T(8,128)(2,1)S(1)} %fusion.25.refs_8_), channel_id=1, source_target_pairs={{0,16},{8,24},{16,0},{24,8},{1,17},{9,25},{17,1},{25,9},{2,18},{10... | collective-permute-start | bytes 196616 | tf_op jit(solution)/shard_map/ppermute | solution.py:247
  38.8 6.6 %collective-permute-start.24 = (bf16[256,128]{1,0:T(8,128)(2,1)S(1)}, bf16[256,128]{1,0:T(8,128)(2,1)S(1)}, u32[]{:S(2)}, u32[]{:S(2)}) collective-permute-start(bf16[256,128]{1,0:T(8,128)(2,1)S(1)} %fusion.25.refs_8_), channel_id=1, source_target_pairs={{0,8},{8,0},{16,24},{24,16},{1,9},{9,1},{17,25},{25,17},{2,10},{10... | collective-permute-start | bytes 196616 | tf_op jit(solution)/shard_map/ppermute | solution.py:247
  41.8 5.2 %collective-permute-start.16 = (bf16[256,128]{1,0:T(8,128)(2,1)S(1)}, bf16[256,128]{1,0:T(8,128)(2,1)S(1)}, u32[]{:S(2)}, u32[]{:S(2)}) collective-permute-start(bf16[256,128]{1,0:T(8,128)(2,1)S(1)} %get-tuple-element.50.refs_0_), channel_id=1, source_target_pairs={{0,6},{1,7},{2,4},{3,5},{4,2},{5,3},{6,0},{7,1},{8,14},{9,15},{10,... | collective-permute-start | bytes 196616 | tf_op jit(solution)/shard_map/ppermute | solution.py:247
  57.0 5.1 %collective-permute-start.27 = (bf16[4,256,128]{2,1,0:T(8,128)(2,1)S(1)}, bf16[4,256,128]{2,1,0:T(8,128)(2,1)S(1)}, u32[]{:S(2)}, u32[]{:S(2)}) collective-permute-start(bf16[4,256,128]{2,1,0:T(8,128)(2,1)S(1)} %get-tuple-element.35), channel_id=1, source_target_pairs={{0,1},{1,0},{2,3},{3,2},{4,5},{5,4},{6,7},{7,6},{8,9},{9,8},{10,11... | collective-permute-start | bytes 786440 | tf_op jit(solution)/shard_map/ppermute | solution.py:247
  57.0 9.3 %collective-permute-start.40 = (bf16[256,128]{1,0:T(8,128)(2,1)S(1)}, bf16[256,128]{1,0:T(8,128)(2,1)S(1)}, u32[]{:S(2)}, u32[]{:S(2)}) collective-permute-start(bf16[256,128]{1,0:T(8,128)(2,1)S(1)} %get-tuple-element.39), channel_id=1, source_target_pairs={{0,8},{8,0},{16,24},{24,16},{1,9},{9,1},{17,25},{25,17},{2,10},{10... | collective-permute-start | bytes 196616 | tf_op jit(solution)/shard_map/ppermute | solution.py:247
  60.6 5.9 %collective-permute-start.39 = (bf16[256,128]{1,0:T(8,128)(2,1)S(1)}, bf16[256,128]{1,0:T(8,128)(2,1)S(1)}, u32[]{:S(2)}, u32[]{:S(2)}) collective-permute-start(bf16[256,128]{1,0:T(8,128)(2,1)S(1)} %add_convert_fusion.4), channel_id=1, source_target_pairs={{0,16},{8,24},{16,0},{24,8},{1,17},{9,25},{17,1},{25,9},{2,18},{10... | collective-permute-start | bytes 196616 | tf_op jit(solution)/shard_map/ppermute | solution.py:247
  62.2 7.6 %collective-permute-start.28 = (bf16[256,128]{1,0:T(8,128)(2,1)S(1)}, bf16[256,128]{1,0:T(8,128)(2,1)S(1)}, u32[]{:S(2)}, u32[]{:S(2)}) collective-permute-start(bf16[256,128]{1,0:T(8,128)(2,1)S(1)} %get-tuple-element.55), channel_id=1, source_target_pairs={{0,2},{1,3},{2,0},{3,1},{4,6},{5,7},{6,4},{7,5},{8,10},{9,11},{10,... | collective-permute-start | bytes 196616 | tf_op jit(solution)/shard_map/ppermute | solution.py:247
  64.8 5.2 %collective-permute-start.30 = (bf16[256,128]{1,0:T(8,128)(2,1)S(1)}, bf16[256,128]{1,0:T(8,128)(2,1)S(1)}, u32[]{:S(2)}, u32[]{:S(2)}) collective-permute-start(bf16[256,128]{1,0:T(8,128)(2,1)S(1)} %get-tuple-element.56), channel_id=1, source_target_pairs={{0,6},{1,7},{2,4},{3,5},{4,2},{5,3},{6,0},{7,1},{8,14},{9,15},{10,... | collective-permute-start | bytes 196616 | tf_op jit(solution)/shard_map/ppermute | solution.py:247
  64.8 5.2 %collective-permute-start.29 = (bf16[256,128]{1,0:T(8,128)(2,1)S(1)}, bf16[256,128]{1,0:T(8,128)(2,1)S(1)}, u32[]{:S(2)}, u32[]{:S(2)}) collective-permute-start(bf16[256,128]{1,0:T(8,128)(2,1)S(1)} %get-tuple-element.57), channel_id=1, source_target_pairs={{0,4},{1,5},{2,6},{3,7},{4,0},{5,1},{6,2},{7,3},{8,12},{9,13},{10,... | collective-permute-start | bytes 196616 | tf_op jit(solution)/shard_map/ppermute | solution.py:247
  66.6 7.0 %collective-permute-start.42 = (bf16[256,128]{1,0:T(8,128)(2,1)S(1)}, bf16[256,128]{1,0:T(8,128)(2,1)S(1)}, u32[]{:S(2)}, u32[]{:S(2)}) collective-permute-start(bf16[256,128]{1,0:T(8,128)(2,1)S(1)} %get-tuple-element.46.refs_8_), channel_id=1, source_target_pairs={{0,16},{8,24},{16,0},{24,8},{1,17},{9,25},{17,1},{25,9},{2,18},{10... | collective-permute-start | bytes 196616 | tf_op jit(solution)/shard_map/ppermute | solution.py:247
  67.6 6.7 %collective-permute-start.41 = (bf16[256,128]{1,0:T(8,128)(2,1)S(1)}, bf16[256,128]{1,0:T(8,128)(2,1)S(1)}, u32[]{:S(2)}, u32[]{:S(2)}) collective-permute-start(bf16[256,128]{1,0:T(8,128)(2,1)S(1)} %get-tuple-element.46.refs_8_), channel_id=1, source_target_pairs={{0,8},{8,0},{16,24},{24,16},{1,9},{9,1},{17,25},{25,17},{2,10},{10... | collective-permute-start | bytes 196616 | tf_op jit(solution)/shard_map/ppermute | solution.py:247
  70.0 5.2 %collective-permute-start.33 = (bf16[256,128]{1,0:T(8,128)(2,1)S(1)}, bf16[256,128]{1,0:T(8,128)(2,1)S(1)}, u32[]{:S(2)}, u32[]{:S(2)}) collective-permute-start(bf16[256,128]{1,0:T(8,128)(2,1)S(1)} %get-tuple-element.48.refs_0_), channel_id=1, source_target_pairs={{0,6},{1,7},{2,4},{3,5},{4,2},{5,3},{6,0},{7,1},{8,14},{9,15},{10,... | collective-permute-start | bytes 196616 | tf_op jit(solution)/shard_map/ppermute | solution.py:247
  85.4 5.7 %collective-permute-start.44 = (bf16[4,256,128]{2,1,0:T(8,128)(2,1)S(1)}, bf16[4,256,128]{2,1,0:T(8,128)(2,1)S(1)}, u32[]{:S(2)}, u32[]{:S(2)}) collective-permute-start(bf16[4,256,128]{2,1,0:T(8,128)(2,1)S(1)} %get-tuple-element.41), channel_id=1, source_target_pairs={{0,1},{1,0},{2,3},{3,2},{4,5},{5,4},{6,7},{7,6},{8,9},{9,8},{10,11... | collective-permute-start | bytes 786440 | tf_op jit(solution)/shard_map/ppermute | solution.py:247
  85.4 10.1 %collective-permute-start.50 = (bf16[256,128]{1,0:T(8,128)(2,1)S(1)}, bf16[256,128]{1,0:T(8,128)(2,1)S(1)}, u32[]{:S(2)}, u32[]{:S(2)}) collective-permute-start(bf16[256,128]{1,0:T(8,128)(2,1)S(1)} %get-tuple-element.45), channel_id=1, source_target_pairs={{0,8},{8,0},{16,24},{24,16},{1,9},{9,1},{17,25},{25,17},{2,10},{10... | collective-permute-start | bytes 196616 | tf_op jit(solution)/shard_map/ppermute | solution.py:247
  88.8 6.6 %collective-permute-start.49 = (bf16[256,128]{1,0:T(8,128)(2,1)S(1)}, bf16[256,128]{1,0:T(8,128)(2,1)S(1)}, u32[]{:S(2)}, u32[]{:S(2)}) collective-permute-start(bf16[256,128]{1,0:T(8,128)(2,1)S(1)} %add_convert_fusion), channel_id=1, source_target_pairs={{0,16},{8,24},{16,0},{24,8},{1,17},{9,25},{17,1},{25,9},{2,18},{10... | collective-permute-start | bytes 196616 | tf_op jit(solution)/shard_map/ppermute | solution.py:247
  91.1 5.2 %collective-permute-start.45 = (bf16[256,128]{1,0:T(8,128)(2,1)S(1)}, bf16[256,128]{1,0:T(8,128)(2,1)S(1)}, u32[]{:S(2)}, u32[]{:S(2)}) collective-permute-start(bf16[256,128]{1,0:T(8,128)(2,1)S(1)} %get-tuple-element.52), channel_id=1, source_target_pairs={{0,2},{1,3},{2,0},{3,1},{4,6},{5,7},{6,4},{7,5},{8,10},{9,11},{10,... | collective-permute-start | bytes 196616 | tf_op jit(solution)/shard_map/ppermute | solution.py:247
  93.9 5.2 %collective-permute-start.47 = (bf16[256,128]{1,0:T(8,128)(2,1)S(1)}, bf16[256,128]{1,0:T(8,128)(2,1)S(1)}, u32[]{:S(2)}, u32[]{:S(2)}) collective-permute-start(bf16[256,128]{1,0:T(8,128)(2,1)S(1)} %get-tuple-element.53), channel_id=1, source_target_pairs={{0,6},{1,7},{2,4},{3,5},{4,2},{5,3},{6,0},{7,1},{8,14},{9,15},{10,... | collective-permute-start | bytes 196616 | tf_op jit(solution)/shard_map/ppermute | solution.py:247
  93.9 5.2 %collective-permute-start.46 = (bf16[256,128]{1,0:T(8,128)(2,1)S(1)}, bf16[256,128]{1,0:T(8,128)(2,1)S(1)}, u32[]{:S(2)}, u32[]{:S(2)}) collective-permute-start(bf16[256,128]{1,0:T(8,128)(2,1)S(1)} %get-tuple-element.54), channel_id=1, source_target_pairs={{0,4},{1,5},{2,6},{3,7},{4,0},{5,1},{6,2},{7,3},{8,12},{9,13},{10,... | collective-permute-start | bytes 196616 | tf_op jit(solution)/shard_map/ppermute | solution.py:247
  (25 other events, 201.4 us)

commit v4 on v3

--- a/solution.py
+++ b/solution.py
@@ -20,35 +20,24 @@
 step_size = 0.01
 
 
-def load_kernel(targ_group, shape, pair_ref, live_ref, values_hbm, weight_hbm, *refs):
-    values_out, weight_out, lists_ref, sems = refs
-    pairs, comp_tiles, targ_tiles = shape
-    slots = values_hbm.shape[0]
+def tile_copies(values_hbm, weight_hbm, values_ref, weight_ref, sems):
     chunks = sems.shape[1]
-    chunk = slots // chunks
-
-    def copies(index):
+    chunk = values_hbm.shape[0] // chunks
+    for index in range(chunks):
         part = pl.ds(index * chunk, chunk)
-        return (
-            pltpu.make_async_copy(values_hbm.at[part], values_out.at[part], sems.at[0, index]),
-            pltpu.make_async_copy(weight_hbm.at[part], weight_out.at[part], sems.at[1, index]),
-        )
-
-    for index in range(chunks):
-
-        @pl.when(index * chunk < live_ref[0])
-        def _():
-            for copy in copies(index):
-                copy.start()
-
-    values_out[slots] = jnp.zeros_like(values_out[slots])
-    weight_out[slots] = jnp.zeros_like(weight_out[slots])
-
-    across = jnp.broadcast_to(pair_ref[...].astype(jnp.float32), (slots, slots))
+        yield index * chunk, [
+            pltpu.make_async_copy(values_hbm.at[part], values_ref.at[part], sems.at[0, index]),
+            pltpu.make_async_copy(weight_hbm.at[part], weight_ref.at[part], sems.at[1, index]),
+        ]
+
+
+def list_slots(pair, comp_tiles, targ_tiles, pairs):
+    slots = pair.shape[1]
+    across = jnp.broadcast_to(pair.astype(jnp.float32), (slots, slots))
     down = across.T
     at = lax.broadcasted_iota(jnp.int32, (slots, slots), 1).astype(jnp.float32)
     mine = lax.broadcasted_iota(jnp.int32, (slots, slots), 0).astype(jnp.float32)
-    spare = float(comp_tiles * targ_group)
+    spare = float(comp_tiles * targ_tiles)
     same = down == across
 
     def count(mask, axis):
@@ -73,35 +62,61 @@
         return jnp.sum(jnp.where(mask, value - rest, 0.0), axis=0, keepdims=True) + rest
 
     here = place == at
-    comp_tile = jnp.floor((pair + 0.5) * (1.0 / targ_group))
+    comp_tile = jnp.floor((pair + 0.5) * (1.0 / targ_tiles))
     rows = [pick(here & (member == n), mine[:, :1], float(slots)) for n in range(GROUP)]
     rows.append(pick(here & (member == 0.0), rank, float(pairs)))
     here = (rank == at) & opens
     rows.append(pick(here, comp_tile, float(comp_tiles)))
-    rows.append(pick(here, pair - targ_group * comp_tile, float(targ_tiles)))
+    rows.append(pick(here, pair - targ_tiles * comp_tile, float(targ_tiles)))
     totals = [jnp.sum(jnp.where(opens, n, 0.0), axis=0, keepdims=True) for n in (groups, 1.0)]
     rows.append(jnp.where(at[:1] == 0.0, totals[0], totals[1]))
-    lists_ref[...] = jnp.concatenate(rows, axis=0).astype(jnp.int32)
-
-    for index in range(chunks):
-
-        @pl.when(index * chunk < live_ref[0])
-        def _():
-            for copy in copies(index):
-                copy.wait()
-
-
-def force_kernel(cols, rows, lists_ref, *refs):
+    return jnp.concatenate(rows, axis=0).astype(jnp.int32)
+
+
+def force_kernel(cols, rows, first, *refs):
+    if first:
+        live_ref, row_ref, col_ref, refs = *refs[:3], refs[3:]
+    else:
+        lists_ref, refs = refs[0], refs[1:]
     comp_firsts, refs = refs[: cols // 2], refs[cols // 2 :]
     comp_seconds, refs = refs[: cols // 2], refs[cols // 2 :]
     targ_blocks, refs = refs[:rows], refs[rows:]
     values_ref, weight_ref, refs = refs[0], refs[1], refs[2:]
     comp_keep, comp_send, refs = refs[0], refs[1], refs[2:]
     targ_outs, refs = refs[:rows], refs[rows:]
+    if first:
+        values_hbm, weight_hbm = values_ref, weight_ref
+        values_ref, weight_ref, lists_out, refs = *refs[:3], refs[3:]
+        lists_ref, list_sem, sems, refs = *refs[:3], refs[3:]
     pred, total, comp_tiles, comp_flip, targ_tiles, targ_flip, comp_acc, targ_acc = refs
     side = values_ref.shape[1]
     comp_rows, targ_rows = comp_firsts[0].shape[0], targ_blocks[0].shape[0]
     comp_per, targ_per = comp_rows // side, targ_rows // side
+
+    if first:
+        copies = tile_copies(values_hbm, weight_hbm, values_ref, weight_ref, sems)
+        copies = list(copies)
+        for start, both in copies:
+
+            @pl.when(start < live_ref[0])
+            def _():
+                for copy in both:
+                    copy.start()
+
+        slots = values_hbm.shape[0]
+        values_ref[slots] = jnp.zeros_like(values_ref[slots])
+        weight_ref[slots] = jnp.zeros_like(weight_ref[slots])
+        row_index, col_index = lax.axis_index("row"), lax.axis_index("col")
+        local = row_ref[...] - row_index * (cols * comp_per)
+        comp_place = (lax.div(local, comp_per) ^ col_index) * comp_per + lax.rem(local, comp_per)
+        holder = lax.div(col_ref[...], targ_per * cols)
+        targ_place = (holder ^ row_index) * targ_per + lax.rem(col_ref[...], targ_per)
+        alive = lax.broadcasted_iota(jnp.int32, (1, slots), 1) < live_ref[0]
+        spare = cols * comp_per * rows * targ_per
+        pair = jnp.where(alive, comp_place * (rows * targ_per) + targ_place, spare)
+        lists_out[...] = list_slots(pair, cols * comp_per, rows * targ_per, pred.shape[0] - 1)
+        to_scalars = pltpu.make_async_copy(lists_out, lists_ref, list_sem)
+        to_scalars.start()
 
     def fill(spot, tile, tiles, flip, acc):
         tiles[spot] = tile
@@ -116,6 +131,9 @@
         for i in range(comp_per):
             tile = (comp_seconds if n % 2 else comp_firsts)[n // 2][i * side : (i + 1) * side]
             fill(n * comp_per + i, tile, comp_tiles, comp_flip, comp_acc)
+
+    if first:
+        to_scalars.wait()
 
     def steps(count, unroll):
         return lax.div(count + (unroll - 1), unroll)
@@ -139,6 +157,14 @@
         return unused
 
     lax.fori_loop(0, steps(pairs, PAIRS), predict, 0)
+
+    if first:
+        for start, both in copies:
+
+            @pl.when(start < live_ref[0])
+            def _():
+                for copy in both:
+                    copy.wait()
 
     one = degrees_free * noise_scale * noise_scale
     assert one == 1.0
@@ -195,38 +221,37 @@
 hbm = pl.BlockSpec(memory_space=pltpu.HBM)
 
 
-def load_tiles(pairs, live, targ_group, shape, values, weight):
-    slots, side, width = values.shape
-    chunks = slots // math.gcd(slots, 16)
-    held = pltpu.VMEM((slots + 1, side, width), values.dtype)
-    values, weight = (pltpu.with_memory_space_constraint(x, pltpu.HBM) for x in (values, weight))
-    return pl.pallas_call(
-        functools.partial(load_kernel, targ_group, shape),
-        out_shape=[held, held, jax.ShapeDtypeStruct((GROUP + 4, slots), jnp.int32)],
-        in_specs=[vmem, smem, hbm, hbm],
-        out_specs=[vmem] * 3,
-        scratch_shapes=[pltpu.SemaphoreType.DMA((2, chunks))],
-        compiler_params=pltpu.CompilerParams(vmem_limit_bytes=24 * 2**20),
-        name="tile_load",
-    )(pairs, live, values, weight)
-
-
-def local_grads(lists, comp_firsts, comp_seconds, targ_blocks, values, weight, pairs):
+def local_grads(slots_at, comp_firsts, comp_seconds, targ_blocks, values, weight):
+    first = len(slots_at) > 1
     cols, rows = 2 * len(comp_firsts), len(targ_blocks)
     comp_rows, rank = comp_firsts[0].shape
     targ_rows = targ_blocks[0].shape[0]
     side = values.shape[1]
     comp_tiles, targ_tiles = cols * comp_rows // side, rows * targ_rows // side
+    slots = values.shape[0] if first else values.shape[0] - 1
+    pairs = min(comp_tiles * targ_tiles, slots)
+    held = (pairs + 1) * side * side * 6 + (comp_tiles + targ_tiles + 2) * side * rank * 8
+    held += 4 * 2**20 if first else 4 * values.size
     comp_shape = jax.ShapeDtypeStruct((cols // 2, comp_rows, rank), jnp.bfloat16)
     targ_shape = jax.ShapeDtypeStruct((targ_rows, rank), jnp.bfloat16)
-    held = (pairs + 1) * side * side * 6 + (comp_tiles + targ_tiles + 2) * side * rank * 8
-    held += 4 * values.size
+    outs = [comp_shape] * 2 + [targ_shape] * rows
+    scratch = []
+    ins = [smem, vmem, vmem] if first else [smem]
+    if first:
+        lists = (GROUP + 4, slots)
+        outs += [pltpu.VMEM((slots + 1, side, side), x.dtype) for x in (values, weight)]
+        outs += [jax.ShapeDtypeStruct(lists, jnp.int32)]
+        scratch = [pltpu.SMEM(lists, jnp.int32), pltpu.SemaphoreType.DMA]
+        scratch += [pltpu.SemaphoreType.DMA((2, slots // math.gcd(slots, 16)))]
+        values, weight = (pltpu.with_memory_space_constraint(x, pltpu.HBM) for x in (values, weight))
+    ins += [vmem] * (cols + rows) + [hbm if first else vmem] * 2
     outs = pl.pallas_call(
-        functools.partial(force_kernel, cols, rows),
-        out_shape=[comp_shape] * 2 + [targ_shape] * rows,
-        in_specs=[smem] + [vmem] * (cols + rows + 2),
-        out_specs=[vmem] * (2 + rows),
+        functools.partial(force_kernel, cols, rows, first),
+        out_shape=outs,
+        in_specs=ins,
+        out_specs=[vmem] * len(outs),
         scratch_shapes=[
+            *scratch,
             pltpu.VMEM((pairs + 1, side, side), jnp.bfloat16),
             pltpu.VMEM((pairs + 1, side, side), jnp.float32),
             pltpu.VMEM((comp_tiles + 1, side, rank), jnp.bfloat16),
@@ -238,8 +263,8 @@
         ],
         compiler_params=pltpu.CompilerParams(vmem_limit_bytes=held + 4 * 2**20),
         name="tile_force",
-    )(lists, *comp_firsts, *comp_seconds, *targ_blocks, values, weight)
-    return outs[0], outs[1], outs[2:]
+    )(*slots_at, *comp_firsts, *comp_seconds, *targ_blocks, values, weight)
+    return outs[0], outs[1], outs[2 : 2 + rows], outs[2 + rows :]
 
 
 def swap(block, axis, offset):
@@ -290,35 +315,19 @@
     tile_values,
     tile_weight,
 ):
-    side = tile_values.shape[2]
-    comp_per = compound_pos.shape[0] // side
-    targ_per = target_pos.shape[0] // side
     cols, rows = lax.axis_size("col"), lax.axis_size("row")
-    col_index, row_index = lax.axis_index("col"), lax.axis_index("row")
     assert cols & (cols - 1) == 0 and rows & (rows - 1) == 0
-    comp_local = tile_rows[0] - row_index * (cols * comp_per)
-    comp_place = ((comp_local // comp_per) ^ col_index) * comp_per + comp_local % comp_per
-    holder = tile_cols[0] // targ_per // cols
-    targ_place = (holder ^ row_index) * targ_per + tile_cols[0] % targ_per
-    targ_group = rows * targ_per
-    alive = jnp.arange(tile_values.shape[1], dtype=jnp.int32) < tile_count[0]
-    spare = cols * comp_per * targ_group
-    slots = jnp.where(alive, comp_place * targ_group + targ_place, spare)
-
-    shape = (min(spare, slots.shape[0]), cols * comp_per, targ_group)
-    values, weight, lists = load_tiles(
-        slots[None], tile_count, targ_group, shape, tile_values[0], tile_weight[0]
-    )
+    held = (tile_values[0], tile_weight[0], tile_count, tile_rows, tile_cols)
 
     def forces(comp, targ):
-        comp_keep, comp_send, targ_parts = local_grads(
-            lists,
+        nonlocal held
+        comp_keep, comp_send, targ_parts, kept = local_grads(
+            held[2:],
             *spread_pairs(comp.astype(jnp.bfloat16), "col"),
             spread(targ.astype(jnp.bfloat16), "row"),
-            values,
-            weight,
-            shape[0],
+            *held[:2],
         )
+        held = kept or held
         comp_sum = collect_pairs(comp_keep, comp_send, "col")
         targ_sum = collect(targ_parts, "row")
         return comp_sum - prior_weight * comp, targ_sum - prior_weight * targ

time: 98.6 us -> 99 us (level); the launches traced: 99.9 us -> 99.2 us
  starting transfers between devices: 48.1 us -> 58.1 us
  Pallas kernels: 23.6 us -> 16.8 us
  waiting for transfers between devices: 21.9 us -> 17.5 us
  local copies, waits for them, and re-layouts: 0.04 us -> 1.39 us
    ppermute x51, starting transfers between devices: 48.1 us -> 58.1 us  [swap(): return lax.ppermute(block, axis, [(i, i ^ offset) for i in range(size)])]
    pallas_call x4 -> x3, Pallas kernels: 23.6 us -> 16.8 us  [local_grads(): pl.pallas_call(functools.partial(force_kernel, cols, rows, first), out_sh...]
    ppermute x51, waiting for transfers between devices: 21.9 us -> 17.5 us  [swap(): return lax.ppermute(block, axis, [(i, i ^ offset) for i in range(size)])]
    unnamed x12 -> x16, local copies, waits for them, and re-layouts: 0.04 us -> 1.39 us
  transfers between devices with their start and end apart: 51 -> 51, of which waited for: 18 -> 21; matrix products, arithmetic and copies ran while one was open for 3% -> 2% of each run, Pallas kernels for 5% -> 0%
where the time goes in v4:
time: 99 us; the launch traced here: 99.2 us
  starting transfers between devices  58.1 us (59%)
  waiting for transfers between devices  17.5 us (18%)
  Pallas kernels  16.8 us (17%)
  other arithmetic  3.92 us (4%)
  between operations  1.47 us (1%)
  local copies, waits for them, and re-layouts  1.39 us (1%)
    ppermute x51, starting transfers between devices, swap(): return lax.ppermute(block, axis, [(i, i ^ offset) for i in range(size)])  58.1 us
    ppermute x51, waiting for transfers between devices, swap(): return lax.ppermute(block, axis, [(i, i ^ offset) for i in range(size)])  17.5 us
    pallas_call x3, Pallas kernels, local_grads(): pl.pallas_call(functools.partial(force_kernel, cols, rows, first), out_sh...  16.8 us
  transfers between devices with their start and end apart: 51, of which 21 were waited for; matrix products, arithmetic and copies ran while one was open for 2% of the time, Pallas kernels for 0%

profile of v4, /device:TPU:0, one launch (start us, length us, event | category | flops | bytes accessed | tf_op | source)
XLA Modules:
  0.0 99.2 jit_solution(11369880425172912143)
XLA Ops:
  1.5 4.0 %collective-permute-start.8 = (bf16[256,128]{1,0:T(8,128)(2,1)S(1)}, bf16[256,128]{1,0:T(8,128)(2,1)S(1)}, u32[]{:S(2)}, u32[]{:S(2)}) collective-permute-start(bf16[256,128]{1,0:T(8,128)(2,1)S(1)} %convert_element_type.250.refs_11_), channel_id=1, source_target_pairs={{0,16},{8,24},{16,0},{24,8},{1,17},{9,25},{17,1},{25,9},{2,18},{10... | collective-permute-start | bytes 196616 | tf_op jit(solution)/shard_map/ppermute | solution.py:272
  5.6 1.6 %collective-permute-start.7 = (bf16[256,128]{1,0:T(8,128)(2,1)S(1)}, bf16[256,128]{1,0:T(8,128)(2,1)S(1)}, u32[]{:S(2)}, u32[]{:S(2)}) collective-permute-start(bf16[256,128]{1,0:T(8,128)(2,1)S(1)} %convert_element_type.250.refs_11_), channel_id=1, source_target_pairs={{0,8},{8,0},{16,24},{24,16},{1,9},{9,1},{17,25},{25,17},{2,10},{10... | collective-permute-start | bytes 196616 | tf_op jit(solution)/shard_map/ppermute | solution.py:272
  8.1 2.4 %collective-permute-start.2 = (bf16[256,128]{1,0:T(8,128)(2,1)S(1)}, bf16[256,128]{1,0:T(8,128)(2,1)S(1)}, u32[]{:S(2)}, u32[]{:S(2)}) collective-permute-start(bf16[256,128]{1,0:T(8,128)(2,1)S(1)} %convert_element_type.249.refs_3_), channel_id=1, source_target_pairs={{0,6},{1,7},{2,4},{3,5},{4,2},{5,3},{6,0},{7,1},{8,14},{9,15},{10,... | collective-permute-start | bytes 196616 | tf_op jit(solution)/shard_map/ppermute | solution.py:272
  12.1 1.3 %collective-permute-done.2.refs_6_ = bf16[256,128]{1,0:T(8,128)(2,1)S(1)} collective-permute-done((bf16[256,128]{1,0:T(8,128)(2,1)S(1)}, bf16[256,128]{1,0:T(8,128)(2,1)S(1)}, u32[]{:S(2)}, u32[]{:S(2)}) %collective-permute-start.2) | collective-permute-done | bytes 65568 | tf_op jit(solution)/shard_map/ppermute | solution.py:272
  13.3 1.4 %collective-permute-done.1.refs_5_ = bf16[256,128]{1,0:T(8,128)(2,1)S(1)} collective-permute-done((bf16[256,128]{1,0:T(8,128)(2,1)S(1)}, bf16[256,128]{1,0:T(8,128)(2,1)S(1)}, u32[]{:S(2)}, u32[]{:S(2)}) %collective-permute-start.1) | collective-permute-done | bytes 65568 | tf_op jit(solution)/shard_map/ppermute | solution.py:272
  17.9 7.2 %tile_force.3 = (bf16[4,256,128]{2,1,0:T(8,128)(2,1)S(1)}, bf16[4,256,128]{2,1,0:T(8,128)(2,1)S(1)}, bf16[256,128]{1,0:T(8,128)(2,1)S(1)}, bf16[256,128]{1,0:T(8...) custom-call(s32[1]{0:T(128)S(6)} %copy.13.refs_0_, ...), custom_call_target="tpu_custom_call" | custom-call | tf_op jit(solution)/shard_map/tile_force/pallas_call | solution.py:248
  25.3 4.1 %collective-permute-start.10 = (bf16[4,256,128]{2,1,0:T(8,128)(2,1)S(1)}, bf16[4,256,128]{2,1,0:T(8,128)(2,1)S(1)}, u32[]{:S(2)}, u32[]{:S(2)}) collective-permute-start(bf16[4,256,128]{2,1,0:T(8,128)(2,1)S(1)} %get-tuple-element.26), channel_id=1, source_target_pairs={{0,1},{1,0},{2,3},{3,2},{4,5},{5,4},{6,7},{7,6},{8,9},{9,8},{10,11... | collective-permute-start | bytes 786440 | tf_op jit(solution)/shard_map/ppermute | solution.py:272
  29.4 1.7 %collective-permute-start.23 = (bf16[256,128]{1,0:T(8,128)(2,1)S(1)}, bf16[256,128]{1,0:T(8,128)(2,1)S(1)}, u32[]{:S(2)}, u32[]{:S(2)}) collective-permute-start(bf16[256,128]{1,0:T(8,128)(2,1)S(1)} %get-tuple-element.31), channel_id=1, source_target_pairs={{0,8},{8,0},{16,24},{24,16},{1,9},{9,1},{17,25},{25,17},{2,10},{10... | collective-permute-start | bytes 196616 | tf_op jit(solution)/shard_map/ppermute | solution.py:272
  31.2 1.9 %collective-permute-start.11 = (bf16[256,128]{1,0:T(8,128)(2,1)S(1)}, bf16[256,128]{1,0:T(8,128)(2,1)S(1)}, u32[]{:S(2)}, u32[]{:S(2)}) collective-permute-start(bf16[256,128]{1,0:T(8,128)(2,1)S(1)} %get-tuple-element.58), channel_id=1, source_target_pairs={{0,2},{1,3},{2,0},{3,1},{4,6},{5,7},{6,4},{7,5},{8,10},{9,11},{10,... | collective-permute-start | bytes 196616 | tf_op jit(solution)/shard_map/ppermute | solution.py:272
  33.1 3.7 %collective-permute-start.13 = (bf16[256,128]{1,0:T(8,128)(2,1)S(1)}, bf16[256,128]{1,0:T(8,128)(2,1)S(1)}, u32[]{:S(2)}, u32[]{:S(2)}) collective-permute-start(bf16[256,128]{1,0:T(8,128)(2,1)S(1)} %get-tuple-element.59), channel_id=1, source_target_pairs={{0,6},{1,7},{2,4},{3,5},{4,2},{5,3},{6,0},{7,1},{8,14},{9,15},{10,... | collective-permute-start | bytes 196616 | tf_op jit(solution)/shard_map/ppermute | solution.py:272
  38.2 2.1 %collective-permute-start.25 = (bf16[256,128]{1,0:T(8,128)(2,1)S(1)}, bf16[256,128]{1,0:T(8,128)(2,1)S(1)}, u32[]{:S(2)}, u32[]{:S(2)}) collective-permute-start(bf16[256,128]{1,0:T(8,128)(2,1)S(1)} %fusion.25.refs_9_), channel_id=1, source_target_pairs={{0,16},{8,24},{16,0},{24,8},{1,17},{9,25},{17,1},{25,9},{2,18},{10... | collective-permute-start | bytes 196616 | tf_op jit(solution)/shard_map/ppermute | solution.py:272
  42.3 1.9 %collective-permute-start.16 = (bf16[256,128]{1,0:T(8,128)(2,1)S(1)}, bf16[256,128]{1,0:T(8,128)(2,1)S(1)}, u32[]{:S(2)}, u32[]{:S(2)}) collective-permute-start(bf16[256,128]{1,0:T(8,128)(2,1)S(1)} %get-tuple-element.50.refs_1_), channel_id=1, source_target_pairs={{0,6},{1,7},{2,4},{3,5},{4,2},{5,3},{6,0},{7,1},{8,14},{9,15},{10,... | collective-permute-start | bytes 196616 | tf_op jit(solution)/shard_map/ppermute | solution.py:272
  44.2 1.2 %collective-permute-start.15 = (bf16[256,128]{1,0:T(8,128)(2,1)S(1)}, bf16[256,128]{1,0:T(8,128)(2,1)S(1)}, u32[]{:S(2)}, u32[]{:S(2)}) collective-permute-start(bf16[256,128]{1,0:T(8,128)(2,1)S(1)} %get-tuple-element.50.refs_1_), channel_id=1, source_target_pairs={{0,4},{1,5},{2,6},{3,7},{4,0},{5,1},{6,2},{7,3},{8,12},{9,13},{10,... | collective-permute-start | bytes 196616 | tf_op jit(solution)/shard_map/ppermute | solution.py:272
  46.1 1.8 %collective-permute-done.16.refs_4_ = bf16[256,128]{1,0:T(8,128)(2,1)S(1)} collective-permute-done((bf16[256,128]{1,0:T(8,128)(2,1)S(1)}, bf16[256,128]{1,0:T(8,128)(2,1)S(1)}, u32[]{:S(2)}, u32[]{:S(2)}) %collective-permute-start.16) | collective-permute-done | bytes 65568 | tf_op jit(solution)/shard_map/ppermute | solution.py:272
  50.9 4.8 %tile_force.4 = (bf16[4,256,128]{2,1,0:T(8,128)(2,1)S(1)}, bf16[4,256,128]{2,1,0:T(8,128)(2,1)S(1)}, bf16[256,128]{1,0:T(8,128)(2,1)S(1)}, bf16[256,128]{1,0:T(8...) custom-call(s32[8,256]{1,0:T(8,128)S(1)} %get-tuple-element.27.refs_0_, ...), custom_call_target="tpu_custom_call" | custom-call | tf_op jit(solution)/shard_map/tile_force/pallas_call | solution.py:248
  55.8 2.1 %collective-permute-start.27 = (bf16[4,256,128]{2,1,0:T(8,128)(2,1)S(1)}, bf16[4,256,128]{2,1,0:T(8,128)(2,1)S(1)}, u32[]{:S(2)}, u32[]{:S(2)}) collective-permute-start(bf16[4,256,128]{2,1,0:T(8,128)(2,1)S(1)} %get-tuple-element.35), channel_id=1, source_target_pairs={{0,1},{1,0},{2,3},{3,2},{4,5},{5,4},{6,7},{7,6},{8,9},{9,8},{10,11... | collective-permute-start | bytes 786440 | tf_op jit(solution)/shard_map/ppermute | solution.py:272
  57.9 1.7 %collective-permute-start.40 = (bf16[256,128]{1,0:T(8,128)(2,1)S(1)}, bf16[256,128]{1,0:T(8,128)(2,1)S(1)}, u32[]{:S(2)}, u32[]{:S(2)}) collective-permute-start(bf16[256,128]{1,0:T(8,128)(2,1)S(1)} %get-tuple-element.39), channel_id=1, source_target_pairs={{0,8},{8,0},{16,24},{24,16},{1,9},{9,1},{17,25},{25,17},{2,10},{10... | collective-permute-start | bytes 196616 | tf_op jit(solution)/shard_map/ppermute | solution.py:272
  60.1 1.8 %collective-permute-start.39 = (bf16[256,128]{1,0:T(8,128)(2,1)S(1)}, bf16[256,128]{1,0:T(8,128)(2,1)S(1)}, u32[]{:S(2)}, u32[]{:S(2)}) collective-permute-start(bf16[256,128]{1,0:T(8,128)(2,1)S(1)} %add_convert_fusion.4), channel_id=1, source_target_pairs={{0,16},{8,24},{16,0},{24,8},{1,17},{9,25},{17,1},{25,9},{2,18},{10... | collective-permute-start | bytes 196616 | tf_op jit(solution)/shard_map/ppermute | solution.py:272
  62.0 2.7 %collective-permute-start.28 = (bf16[256,128]{1,0:T(8,128)(2,1)S(1)}, bf16[256,128]{1,0:T(8,128)(2,1)S(1)}, u32[]{:S(2)}, u32[]{:S(2)}) collective-permute-start(bf16[256,128]{1,0:T(8,128)(2,1)S(1)} %get-tuple-element.55), channel_id=1, source_target_pairs={{0,2},{1,3},{2,0},{3,1},{4,6},{5,7},{6,4},{7,5},{8,10},{9,11},{10,... | collective-permute-start | bytes 196616 | tf_op jit(solution)/shard_map/ppermute | solution.py:272
  64.7 1.4 %collective-permute-start.30 = (bf16[256,128]{1,0:T(8,128)(2,1)S(1)}, bf16[256,128]{1,0:T(8,128)(2,1)S(1)}, u32[]{:S(2)}, u32[]{:S(2)}) collective-permute-start(bf16[256,128]{1,0:T(8,128)(2,1)S(1)} %get-tuple-element.56), channel_id=1, source_target_pairs={{0,6},{1,7},{2,4},{3,5},{4,2},{5,3},{6,0},{7,1},{8,14},{9,15},{10,... | collective-permute-start | bytes 196616 | tf_op jit(solution)/shard_map/ppermute | solution.py:272
  67.0 1.6 %collective-permute-start.42 = (bf16[256,128]{1,0:T(8,128)(2,1)S(1)}, bf16[256,128]{1,0:T(8,128)(2,1)S(1)}, u32[]{:S(2)}, u32[]{:S(2)}) collective-permute-start(bf16[256,128]{1,0:T(8,128)(2,1)S(1)} %get-tuple-element.46.refs_9_), channel_id=1, source_target_pairs={{0,16},{8,24},{16,0},{24,8},{1,17},{9,25},{17,1},{25,9},{2,18},{10... | collective-permute-start | bytes 196616 | tf_op jit(solution)/shard_map/ppermute | solution.py:272
  68.6 1.6 %collective-permute-start.41 = (bf16[256,128]{1,0:T(8,128)(2,1)S(1)}, bf16[256,128]{1,0:T(8,128)(2,1)S(1)}, u32[]{:S(2)}, u32[]{:S(2)}) collective-permute-start(bf16[256,128]{1,0:T(8,128)(2,1)S(1)} %get-tuple-element.46.refs_9_), channel_id=1, source_target_pairs={{0,8},{8,0},{16,24},{24,16},{1,9},{9,1},{17,25},{25,17},{2,10},{10... | collective-permute-start | bytes 196616 | tf_op jit(solution)/shard_map/ppermute | solution.py:272
  70.7 2.0 %collective-permute-start.33 = (bf16[256,128]{1,0:T(8,128)(2,1)S(1)}, bf16[256,128]{1,0:T(8,128)(2,1)S(1)}, u32[]{:S(2)}, u32[]{:S(2)}) collective-permute-start(bf16[256,128]{1,0:T(8,128)(2,1)S(1)} %get-tuple-element.48.refs_1_), channel_id=1, source_target_pairs={{0,6},{1,7},{2,4},{3,5},{4,2},{5,3},{6,0},{7,1},{8,14},{9,15},{10,... | collective-permute-start | bytes 196616 | tf_op jit(solution)/shard_map/ppermute | solution.py:272
  72.8 1.4 %collective-permute-start.31 = (bf16[256,128]{1,0:T(8,128)(2,1)S(1)}, bf16[256,128]{1,0:T(8,128)(2,1)S(1)}, u32[]{:S(2)}, u32[]{:S(2)}) collective-permute-start(bf16[256,128]{1,0:T(8,128)(2,1)S(1)} %get-tuple-element.48.refs_1_), channel_id=1, source_target_pairs={{0,2},{1,3},{2,0},{3,1},{4,6},{5,7},{6,4},{7,5},{8,10},{9,11},{10,... | collective-permute-start | bytes 196616 | tf_op jit(solution)/shard_map/ppermute | solution.py:272
  74.2 2.3 %collective-permute-start.43 = (bf16[256,128]{1,0:T(8,128)(2,1)S(1)}, bf16[256,128]{1,0:T(8,128)(2,1)S(1)}, u32[]{:S(2)}, u32[]{:S(2)}) collective-permute-start(bf16[256,128]{1,0:T(8,128)(2,1)S(1)} %collective-permute-done.42.refs_11_), channel_id=1, source_target_pairs={{0,8},{8,0},{16,24},{24,16},{1,9},{9,1},{17,25},{25,17},{2,10},{10... | collective-permute-start | bytes 196616 | tf_op jit(solution)/shard_map/ppermute | solution.py:272
  77.6 1.2 %collective-permute-done.43.refs_12_ = bf16[256,128]{1,0:T(8,128)(2,1)S(1)} collective-permute-done((bf16[256,128]{1,0:T(8,128)(2,1)S(1)}, bf16[256,128]{1,0:T(8,128)(2,1)S(1)}, u32[]{:S(2)}, u32[]{:S(2)}) %collective-permute-start.43) | collective-permute-done | bytes 65568 | tf_op jit(solution)/shard_map/ppermute | solution.py:272
  78.8 4.8 %tile_force.5 = (bf16[4,256,128]{2,1,0:T(8,128)(2,1)S(1)}, bf16[4,256,128]{2,1,0:T(8,128)(2,1)S(1)}, bf16[256,128]{1,0:T(8,128)(2,1)S(1)}, bf16[256,128]{1,0:T(8...) custom-call(s32[8,256]{1,0:T(8,128)S(1)} %get-tuple-element.27.refs_0_, ...), custom_call_target="tpu_custom_call" | custom-call | tf_op jit(solution)/shard_map/tile_force/pallas_call | solution.py:248
  83.6 1.8 %collective-permute-start.48 = (bf16[256,128]{1,0:T(8,128)(2,1)S(1)}, bf16[256,128]{1,0:T(8,128)(2,1)S(1)}, u32[]{:S(2)}, u32[]{:S(2)}) collective-permute-start(bf16[256,128]{1,0:T(8,128)(2,1)S(1)} %get-tuple-element.44), channel_id=1, source_target_pairs={{0,8},{8,0},{16,24},{24,16},{1,9},{9,1},{17,25},{25,17},{2,10},{10... | collective-permute-start | bytes 196616 | tf_op jit(solution)/shard_map/ppermute | solution.py:272
  85.7 1.7 %collective-permute-start.50 = (bf16[256,128]{1,0:T(8,128)(2,1)S(1)}, bf16[256,128]{1,0:T(8,128)(2,1)S(1)}, u32[]{:S(2)}, u32[]{:S(2)}) collective-permute-start(bf16[256,128]{1,0:T(8,128)(2,1)S(1)} %get-tuple-element.45), channel_id=1, source_target_pairs={{0,8},{8,0},{16,24},{24,16},{1,9},{9,1},{17,25},{25,17},{2,10},{10... | collective-permute-start | bytes 196616 | tf_op jit(solution)/shard_map/ppermute | solution.py:272
  87.9 2.1 %collective-permute-start.49 = (bf16[256,128]{1,0:T(8,128)(2,1)S(1)}, bf16[256,128]{1,0:T(8,128)(2,1)S(1)}, u32[]{:S(2)}, u32[]{:S(2)}) collective-permute-start(bf16[256,128]{1,0:T(8,128)(2,1)S(1)} %add_convert_fusion), channel_id=1, source_target_pairs={{0,16},{8,24},{16,0},{24,8},{1,17},{9,25},{17,1},{25,9},{2,18},{10... | collective-permute-start | bytes 196616 | tf_op jit(solution)/shard_map/ppermute | solution.py:272
  90.2 2.4 %collective-permute-start.45 = (bf16[256,128]{1,0:T(8,128)(2,1)S(1)}, bf16[256,128]{1,0:T(8,128)(2,1)S(1)}, u32[]{:S(2)}, u32[]{:S(2)}) collective-permute-start(bf16[256,128]{1,0:T(8,128)(2,1)S(1)} %get-tuple-element.52), channel_id=1, source_target_pairs={{0,2},{1,3},{2,0},{3,1},{4,6},{5,7},{6,4},{7,5},{8,10},{9,11},{10,... | collective-permute-start | bytes 196616 | tf_op jit(solution)/shard_map/ppermute | solution.py:272
  95.9 1.9 %collective-permute-done.47 = bf16[256,128]{1,0:T(8,128)(2,1)S(1)} collective-permute-done((bf16[256,128]{1,0:T(8,128)(2,1)S(1)}, bf16[256,128]{1,0:T(8,128)(2,1)S(1)}, u32[]{:S(2)}, u32[]{:S(2)}) %collective-permute-start.47) | collective-permute-done | bytes 65568 | tf_op jit(solution)/shard_map/ppermute | solution.py:272
  (103 shorter events, 22.3 us)
Async XLA Ops:
  1.5 10.0 %collective-permute-start.8 = (bf16[256,128]{1,0:T(8,128)(2,1)S(1)}, bf16[256,128]{1,0:T(8,128)(2,1)S(1)}, u32[]{:S(2)}, u32[]{:S(2)}) collective-permute-start(bf16[256,128]{1,0:T(8,128)(2,1)S(1)} %convert_element_type.250.refs_11_), channel_id=1, source_target_pairs={{0,16},{8,24},{16,0},{24,8},{1,17},{9,25},{17,1},{25,9},{2,18},{10... | collective-permute-start | bytes 196616 | tf_op jit(solution)/shard_map/ppermute | solution.py:272
  5.6 6.0 %collective-permute-start.7 = (bf16[256,128]{1,0:T(8,128)(2,1)S(1)}, bf16[256,128]{1,0:T(8,128)(2,1)S(1)}, u32[]{:S(2)}, u32[]{:S(2)}) collective-permute-start(bf16[256,128]{1,0:T(8,128)(2,1)S(1)} %convert_element_type.250.refs_11_), channel_id=1, source_target_pairs={{0,8},{8,0},{16,24},{24,16},{1,9},{9,1},{17,25},{25,17},{2,10},{10... | collective-permute-start | bytes 196616 | tf_op jit(solution)/shard_map/ppermute | solution.py:272
  8.1 5.3 %collective-permute-start.2 = (bf16[256,128]{1,0:T(8,128)(2,1)S(1)}, bf16[256,128]{1,0:T(8,128)(2,1)S(1)}, u32[]{:S(2)}, u32[]{:S(2)}) collective-permute-start(bf16[256,128]{1,0:T(8,128)(2,1)S(1)} %convert_element_type.249.refs_3_), channel_id=1, source_target_pairs={{0,6},{1,7},{2,4},{3,5},{4,2},{5,3},{6,0},{7,1},{8,14},{9,15},{10,... | collective-permute-start | bytes 196616 | tf_op jit(solution)/shard_map/ppermute | solution.py:272
  11.6 4.5 %collective-permute-start.9 = (bf16[256,128]{1,0:T(8,128)(2,1)S(1)}, bf16[256,128]{1,0:T(8,128)(2,1)S(1)}, u32[]{:S(2)}, u32[]{:S(2)}) collective-permute-start(bf16[256,128]{1,0:T(8,128)(2,1)S(1)} %collective-permute-done.8.refs_13_), channel_id=1, source_target_pairs={{0,8},{8,0},{16,24},{24,16},{1,9},{9,1},{17,25},{25,17},{2,10},{10... | collective-permute-start | bytes 196616 | tf_op jit(solution)/shard_map/ppermute | solution.py:272
  25.1 5.9 %collective-permute-start.21 = (bf16[256,128]{1,0:T(8,128)(2,1)S(1)}, bf16[256,128]{1,0:T(8,128)(2,1)S(1)}, u32[]{:S(2)}, u32[]{:S(2)}) collective-permute-start(bf16[256,128]{1,0:T(8,128)(2,1)S(1)} %get-tuple-element.30), channel_id=1, source_target_pairs={{0,8},{8,0},{16,24},{24,16},{1,9},{9,1},{17,25},{25,17},{2,10},{10... | collective-permute-start | bytes 196616 | tf_op jit(solution)/shard_map/ppermute | solution.py:272
  25.3 5.8 %collective-permute-start.10 = (bf16[4,256,128]{2,1,0:T(8,128)(2,1)S(1)}, bf16[4,256,128]{2,1,0:T(8,128)(2,1)S(1)}, u32[]{:S(2)}, u32[]{:S(2)}) collective-permute-start(bf16[4,256,128]{2,1,0:T(8,128)(2,1)S(1)} %get-tuple-element.26), channel_id=1, source_target_pairs={{0,1},{1,0},{2,3},{3,2},{4,5},{5,4},{6,7},{7,6},{8,9},{9,8},{10,11... | collective-permute-start | bytes 786440 | tf_op jit(solution)/shard_map/ppermute | solution.py:272
  29.4 7.9 %collective-permute-start.23 = (bf16[256,128]{1,0:T(8,128)(2,1)S(1)}, bf16[256,128]{1,0:T(8,128)(2,1)S(1)}, u32[]{:S(2)}, u32[]{:S(2)}) collective-permute-start(bf16[256,128]{1,0:T(8,128)(2,1)S(1)} %get-tuple-element.31), channel_id=1, source_target_pairs={{0,8},{8,0},{16,24},{24,16},{1,9},{9,1},{17,25},{25,17},{2,10},{10... | collective-permute-start | bytes 196616 | tf_op jit(solution)/shard_map/ppermute | solution.py:272
  31.1 7.1 %collective-permute-start.22 = (bf16[256,128]{1,0:T(8,128)(2,1)S(1)}, bf16[256,128]{1,0:T(8,128)(2,1)S(1)}, u32[]{:S(2)}, u32[]{:S(2)}) collective-permute-start(bf16[256,128]{1,0:T(8,128)(2,1)S(1)} %add_convert_fusion.8), channel_id=1, source_target_pairs={{0,16},{8,24},{16,0},{24,8},{1,17},{9,25},{17,1},{25,9},{2,18},{10... | collective-permute-start | bytes 196616 | tf_op jit(solution)/shard_map/ppermute | solution.py:272
  31.2 9.8 %collective-permute-start.11 = (bf16[256,128]{1,0:T(8,128)(2,1)S(1)}, bf16[256,128]{1,0:T(8,128)(2,1)S(1)}, u32[]{:S(2)}, u32[]{:S(2)}) collective-permute-start(bf16[256,128]{1,0:T(8,128)(2,1)S(1)} %get-tuple-element.58), channel_id=1, source_target_pairs={{0,2},{1,3},{2,0},{3,1},{4,6},{5,7},{6,4},{7,5},{8,10},{9,11},{10,... | collective-permute-start | bytes 196616 | tf_op jit(solution)/shard_map/ppermute | solution.py:272
  33.1 8.0 %collective-permute-start.13 = (bf16[256,128]{1,0:T(8,128)(2,1)S(1)}, bf16[256,128]{1,0:T(8,128)(2,1)S(1)}, u32[]{:S(2)}, u32[]{:S(2)}) collective-permute-start(bf16[256,128]{1,0:T(8,128)(2,1)S(1)} %get-tuple-element.59), channel_id=1, source_target_pairs={{0,6},{1,7},{2,4},{3,5},{4,2},{5,3},{6,0},{7,1},{8,14},{9,15},{10,... | collective-permute-start | bytes 196616 | tf_op jit(solution)/shard_map/ppermute | solution.py:272
  36.8 5.4 %collective-permute-start.12 = (bf16[256,128]{1,0:T(8,128)(2,1)S(1)}, bf16[256,128]{1,0:T(8,128)(2,1)S(1)}, u32[]{:S(2)}, u32[]{:S(2)}) collective-permute-start(bf16[256,128]{1,0:T(8,128)(2,1)S(1)} %get-tuple-element.60), channel_id=1, source_target_pairs={{0,4},{1,5},{2,6},{3,7},{4,0},{5,1},{6,2},{7,3},{8,12},{9,13},{10,... | collective-permute-start | bytes 196616 | tf_op jit(solution)/shard_map/ppermute | solution.py:272
  38.2 7.6 %collective-permute-start.25 = (bf16[256,128]{1,0:T(8,128)(2,1)S(1)}, bf16[256,128]{1,0:T(8,128)(2,1)S(1)}, u32[]{:S(2)}, u32[]{:S(2)}) collective-permute-start(bf16[256,128]{1,0:T(8,128)(2,1)S(1)} %fusion.25.refs_9_), channel_id=1, source_target_pairs={{0,16},{8,24},{16,0},{24,8},{1,17},{9,25},{17,1},{25,9},{2,18},{10... | collective-permute-start | bytes 196616 | tf_op jit(solution)/shard_map/ppermute | solution.py:272
  40.3 5.8 %collective-permute-start.24 = (bf16[256,128]{1,0:T(8,128)(2,1)S(1)}, bf16[256,128]{1,0:T(8,128)(2,1)S(1)}, u32[]{:S(2)}, u32[]{:S(2)}) collective-permute-start(bf16[256,128]{1,0:T(8,128)(2,1)S(1)} %fusion.25.refs_9_), channel_id=1, source_target_pairs={{0,8},{8,0},{16,24},{24,16},{1,9},{9,1},{17,25},{25,17},{2,10},{10... | collective-permute-start | bytes 196616 | tf_op jit(solution)/shard_map/ppermute | solution.py:272
  42.3 5.6 %collective-permute-start.16 = (bf16[256,128]{1,0:T(8,128)(2,1)S(1)}, bf16[256,128]{1,0:T(8,128)(2,1)S(1)}, u32[]{:S(2)}, u32[]{:S(2)}) collective-permute-start(bf16[256,128]{1,0:T(8,128)(2,1)S(1)} %get-tuple-element.50.refs_1_), channel_id=1, source_target_pairs={{0,6},{1,7},{2,4},{3,5},{4,2},{5,3},{6,0},{7,1},{8,14},{9,15},{10,... | collective-permute-start | bytes 196616 | tf_op jit(solution)/shard_map/ppermute | solution.py:272
  44.2 4.5 %collective-permute-start.15 = (bf16[256,128]{1,0:T(8,128)(2,1)S(1)}, bf16[256,128]{1,0:T(8,128)(2,1)S(1)}, u32[]{:S(2)}, u32[]{:S(2)}) collective-permute-start(bf16[256,128]{1,0:T(8,128)(2,1)S(1)} %get-tuple-element.50.refs_1_), channel_id=1, source_target_pairs={{0,4},{1,5},{2,6},{3,7},{4,0},{5,1},{6,2},{7,3},{8,12},{9,13},{10,... | collective-permute-start | bytes 196616 | tf_op jit(solution)/shard_map/ppermute | solution.py:272
  55.8 6.1 %collective-permute-start.27 = (bf16[4,256,128]{2,1,0:T(8,128)(2,1)S(1)}, bf16[4,256,128]{2,1,0:T(8,128)(2,1)S(1)}, u32[]{:S(2)}, u32[]{:S(2)}) collective-permute-start(bf16[4,256,128]{2,1,0:T(8,128)(2,1)S(1)} %get-tuple-element.35), channel_id=1, source_target_pairs={{0,1},{1,0},{2,3},{3,2},{4,5},{5,4},{6,7},{7,6},{8,9},{9,8},{10,11... | collective-permute-start | bytes 786440 | tf_op jit(solution)/shard_map/ppermute | solution.py:272
  57.9 8.3 %collective-permute-start.40 = (bf16[256,128]{1,0:T(8,128)(2,1)S(1)}, bf16[256,128]{1,0:T(8,128)(2,1)S(1)}, u32[]{:S(2)}, u32[]{:S(2)}) collective-permute-start(bf16[256,128]{1,0:T(8,128)(2,1)S(1)} %get-tuple-element.39), channel_id=1, source_target_pairs={{0,8},{8,0},{16,24},{24,16},{1,9},{9,1},{17,25},{25,17},{2,10},{10... | collective-permute-start | bytes 196616 | tf_op jit(solution)/shard_map/ppermute | solution.py:272
  60.1 6.8 %collective-permute-start.39 = (bf16[256,128]{1,0:T(8,128)(2,1)S(1)}, bf16[256,128]{1,0:T(8,128)(2,1)S(1)}, u32[]{:S(2)}, u32[]{:S(2)}) collective-permute-start(bf16[256,128]{1,0:T(8,128)(2,1)S(1)} %add_convert_fusion.4), channel_id=1, source_target_pairs={{0,16},{8,24},{16,0},{24,8},{1,17},{9,25},{17,1},{25,9},{2,18},{10... | collective-permute-start | bytes 196616 | tf_op jit(solution)/shard_map/ppermute | solution.py:272
  62.0 8.2 %collective-permute-start.28 = (bf16[256,128]{1,0:T(8,128)(2,1)S(1)}, bf16[256,128]{1,0:T(8,128)(2,1)S(1)}, u32[]{:S(2)}, u32[]{:S(2)}) collective-permute-start(bf16[256,128]{1,0:T(8,128)(2,1)S(1)} %get-tuple-element.55), channel_id=1, source_target_pairs={{0,2},{1,3},{2,0},{3,1},{4,6},{5,7},{6,4},{7,5},{8,10},{9,11},{10,... | collective-permute-start | bytes 196616 | tf_op jit(solution)/shard_map/ppermute | solution.py:272
  64.7 5.5 %collective-permute-start.30 = (bf16[256,128]{1,0:T(8,128)(2,1)S(1)}, bf16[256,128]{1,0:T(8,128)(2,1)S(1)}, u32[]{:S(2)}, u32[]{:S(2)}) collective-permute-start(bf16[256,128]{1,0:T(8,128)(2,1)S(1)} %get-tuple-element.56), channel_id=1, source_target_pairs={{0,6},{1,7},{2,4},{3,5},{4,2},{5,3},{6,0},{7,1},{8,14},{9,15},{10,... | collective-permute-start | bytes 196616 | tf_op jit(solution)/shard_map/ppermute | solution.py:272
  66.1 4.5 %collective-permute-start.29 = (bf16[256,128]{1,0:T(8,128)(2,1)S(1)}, bf16[256,128]{1,0:T(8,128)(2,1)S(1)}, u32[]{:S(2)}, u32[]{:S(2)}) collective-permute-start(bf16[256,128]{1,0:T(8,128)(2,1)S(1)} %get-tuple-element.57), channel_id=1, source_target_pairs={{0,4},{1,5},{2,6},{3,7},{4,0},{5,1},{6,2},{7,3},{8,12},{9,13},{10,... | collective-permute-start | bytes 196616 | tf_op jit(solution)/shard_map/ppermute | solution.py:272
  67.0 7.2 %collective-permute-start.42 = (bf16[256,128]{1,0:T(8,128)(2,1)S(1)}, bf16[256,128]{1,0:T(8,128)(2,1)S(1)}, u32[]{:S(2)}, u32[]{:S(2)}) collective-permute-start(bf16[256,128]{1,0:T(8,128)(2,1)S(1)} %get-tuple-element.46.refs_9_), channel_id=1, source_target_pairs={{0,16},{8,24},{16,0},{24,8},{1,17},{9,25},{17,1},{25,9},{2,18},{10... | collective-permute-start | bytes 196616 | tf_op jit(solution)/shard_map/ppermute | solution.py:272
  68.6 7.9 %collective-permute-start.41 = (bf16[256,128]{1,0:T(8,128)(2,1)S(1)}, bf16[256,128]{1,0:T(8,128)(2,1)S(1)}, u32[]{:S(2)}, u32[]{:S(2)}) collective-permute-start(bf16[256,128]{1,0:T(8,128)(2,1)S(1)} %get-tuple-element.46.refs_9_), channel_id=1, source_target_pairs={{0,8},{8,0},{16,24},{24,16},{1,9},{9,1},{17,25},{25,17},{2,10},{10... | collective-permute-start | bytes 196616 | tf_op jit(solution)/shard_map/ppermute | solution.py:272
  70.7 5.9 %collective-permute-start.33 = (bf16[256,128]{1,0:T(8,128)(2,1)S(1)}, bf16[256,128]{1,0:T(8,128)(2,1)S(1)}, u32[]{:S(2)}, u32[]{:S(2)}) collective-permute-start(bf16[256,128]{1,0:T(8,128)(2,1)S(1)} %get-tuple-element.48.refs_1_), channel_id=1, source_target_pairs={{0,6},{1,7},{2,4},{3,5},{4,2},{5,3},{6,0},{7,1},{8,14},{9,15},{10,... | collective-permute-start | bytes 196616 | tf_op jit(solution)/shard_map/ppermute | solution.py:272
  72.6 4.4 %collective-permute-start.32 = (bf16[256,128]{1,0:T(8,128)(2,1)S(1)}, bf16[256,128]{1,0:T(8,128)(2,1)S(1)}, u32[]{:S(2)}, u32[]{:S(2)}) collective-permute-start(bf16[256,128]{1,0:T(8,128)(2,1)S(1)} %get-tuple-element.48.refs_1_), channel_id=1, source_target_pairs={{0,4},{1,5},{2,6},{3,7},{4,0},{5,1},{6,2},{7,3},{8,12},{9,13},{10,... | collective-permute-start | bytes 196616 | tf_op jit(solution)/shard_map/ppermute | solution.py:272
  74.2 4.5 %collective-permute-start.43 = (bf16[256,128]{1,0:T(8,128)(2,1)S(1)}, bf16[256,128]{1,0:T(8,128)(2,1)S(1)}, u32[]{:S(2)}, u32[]{:S(2)}) collective-permute-start(bf16[256,128]{1,0:T(8,128)(2,1)S(1)} %collective-permute-done.42.refs_11_), channel_id=1, source_target_pairs={{0,8},{8,0},{16,24},{24,16},{1,9},{9,1},{17,25},{25,17},{2,10},{10... | collective-permute-start | bytes 196616 | tf_op jit(solution)/shard_map/ppermute | solution.py:272
  85.4 4.7 %collective-permute-start.44 = (bf16[4,256,128]{2,1,0:T(8,128)(2,1)S(1)}, bf16[4,256,128]{2,1,0:T(8,128)(2,1)S(1)}, u32[]{:S(2)}, u32[]{:S(2)}) collective-permute-start(bf16[4,256,128]{2,1,0:T(8,128)(2,1)S(1)} %get-tuple-element.41), channel_id=1, source_target_pairs={{0,1},{1,0},{2,3},{3,2},{4,5},{5,4},{6,7},{7,6},{8,9},{9,8},{10,11... | collective-permute-start | bytes 786440 | tf_op jit(solution)/shard_map/ppermute | solution.py:272
  85.7 8.5 %collective-permute-start.50 = (bf16[256,128]{1,0:T(8,128)(2,1)S(1)}, bf16[256,128]{1,0:T(8,128)(2,1)S(1)}, u32[]{:S(2)}, u32[]{:S(2)}) collective-permute-start(bf16[256,128]{1,0:T(8,128)(2,1)S(1)} %get-tuple-element.45), channel_id=1, source_target_pairs={{0,8},{8,0},{16,24},{24,16},{1,9},{9,1},{17,25},{25,17},{2,10},{10... | collective-permute-start | bytes 196616 | tf_op jit(solution)/shard_map/ppermute | solution.py:272
  87.9 7.1 %collective-permute-start.49 = (bf16[256,128]{1,0:T(8,128)(2,1)S(1)}, bf16[256,128]{1,0:T(8,128)(2,1)S(1)}, u32[]{:S(2)}, u32[]{:S(2)}) collective-permute-start(bf16[256,128]{1,0:T(8,128)(2,1)S(1)} %add_convert_fusion), channel_id=1, source_target_pairs={{0,16},{8,24},{16,0},{24,8},{1,17},{9,25},{17,1},{25,9},{2,18},{10... | collective-permute-start | bytes 196616 | tf_op jit(solution)/shard_map/ppermute | solution.py:272
  90.2 5.7 %collective-permute-start.45 = (bf16[256,128]{1,0:T(8,128)(2,1)S(1)}, bf16[256,128]{1,0:T(8,128)(2,1)S(1)}, u32[]{:S(2)}, u32[]{:S(2)}) collective-permute-start(bf16[256,128]{1,0:T(8,128)(2,1)S(1)} %get-tuple-element.52), channel_id=1, source_target_pairs={{0,2},{1,3},{2,0},{3,1},{4,6},{5,7},{6,4},{7,5},{8,10},{9,11},{10,... | collective-permute-start | bytes 196616 | tf_op jit(solution)/shard_map/ppermute | solution.py:272
  92.6 5.2 %collective-permute-start.47 = (bf16[256,128]{1,0:T(8,128)(2,1)S(1)}, bf16[256,128]{1,0:T(8,128)(2,1)S(1)}, u32[]{:S(2)}, u32[]{:S(2)}) collective-permute-start(bf16[256,128]{1,0:T(8,128)(2,1)S(1)} %get-tuple-element.53), channel_id=1, source_target_pairs={{0,6},{1,7},{2,4},{3,5},{4,2},{5,3},{6,0},{7,1},{8,14},{9,15},{10,... | collective-permute-start | bytes 196616 | tf_op jit(solution)/shard_map/ppermute | solution.py:272
  93.5 4.9 %collective-permute-start.46 = (bf16[256,128]{1,0:T(8,128)(2,1)S(1)}, bf16[256,128]{1,0:T(8,128)(2,1)S(1)}, u32[]{:S(2)}, u32[]{:S(2)}) collective-permute-start(bf16[256,128]{1,0:T(8,128)(2,1)S(1)} %get-tuple-element.54), channel_id=1, source_target_pairs={{0,4},{1,5},{2,6},{3,7},{4,0},{5,1},{6,2},{7,3},{8,12},{9,13},{10,... | collective-permute-start | bytes 196616 | tf_op jit(solution)/shard_map/ppermute | solution.py:272
  (27 other events, 202.8 us)

commit v5 on v4

--- a/solution.py
+++ b/solution.py
@@ -75,7 +75,7 @@
 
 def force_kernel(cols, rows, first, *refs):
     if first:
-        live_ref, row_ref, col_ref, refs = *refs[:3], refs[3:]
+        live_ref, pair_ref, refs = *refs[:2], refs[2:]
     else:
         lists_ref, refs = refs[0], refs[1:]
     comp_firsts, refs = refs[: cols // 2], refs[cols // 2 :]
@@ -106,15 +106,8 @@
         slots = values_hbm.shape[0]
         values_ref[slots] = jnp.zeros_like(values_ref[slots])
         weight_ref[slots] = jnp.zeros_like(weight_ref[slots])
-        row_index, col_index = lax.axis_index("row"), lax.axis_index("col")
-        local = row_ref[...] - row_index * (cols * comp_per)
-        comp_place = (lax.div(local, comp_per) ^ col_index) * comp_per + lax.rem(local, comp_per)
-        holder = lax.div(col_ref[...], targ_per * cols)
-        targ_place = (holder ^ row_index) * targ_per + lax.rem(col_ref[...], targ_per)
-        alive = lax.broadcasted_iota(jnp.int32, (1, slots), 1) < live_ref[0]
-        spare = cols * comp_per * rows * targ_per
-        pair = jnp.where(alive, comp_place * (rows * targ_per) + targ_place, spare)
-        lists_out[...] = list_slots(pair, cols * comp_per, rows * targ_per, pred.shape[0] - 1)
+        sizes = cols * comp_per, rows * targ_per, pred.shape[0] - 1
+        lists_out[...] = list_slots(pair_ref[...], *sizes)
         to_scalars = pltpu.make_async_copy(lists_out, lists_ref, list_sem)
         to_scalars.start()
 
@@ -236,7 +229,7 @@
     targ_shape = jax.ShapeDtypeStruct((targ_rows, rank), jnp.bfloat16)
     outs = [comp_shape] * 2 + [targ_shape] * rows
     scratch = []
-    ins = [smem, vmem, vmem] if first else [smem]
+    ins = [smem, vmem] if first else [smem]
     if first:
         lists = (GROUP + 4, slots)
         outs += [pltpu.VMEM((slots + 1, side, side), x.dtype) for x in (values, weight)]
@@ -317,7 +310,19 @@
 ):
     cols, rows = lax.axis_size("col"), lax.axis_size("row")
     assert cols & (cols - 1) == 0 and rows & (rows - 1) == 0
-    held = (tile_values[0], tile_weight[0], tile_count, tile_rows, tile_cols)
+    side = tile_values.shape[2]
+    comp_per = compound_pos.shape[0] // side
+    targ_per = target_pos.shape[0] // side
+    col_index, row_index = lax.axis_index("col"), lax.axis_index("row")
+    comp_local = tile_rows - row_index * (cols * comp_per)
+    comp_place = (lax.div(comp_local, comp_per) ^ col_index) * comp_per
+    comp_place += lax.rem(comp_local, comp_per)
+    targ_place = (lax.div(tile_cols, targ_per * cols) ^ row_index) * targ_per
+    targ_place += lax.rem(tile_cols, targ_per)
+    alive = jnp.arange(tile_values.shape[1], dtype=jnp.int32)[None] < tile_count[0]
+    spare = cols * comp_per * rows * targ_per
+    pair = jnp.where(alive, comp_place * (rows * targ_per) + targ_place, spare)
+    held = (tile_values[0], tile_weight[0], tile_count, pair)
 
     def forces(comp, targ):
         nonlocal held

time: 99 us -> 99.8 us (level); the launches traced: 99.2 us -> 98.9 us
  starting transfers between devices: 58.1 us -> 45.4 us
  waiting for transfers between devices: 17.5 us -> 24.3 us
  Pallas kernels: 16.8 us -> 23 us
  local copies, waits for them, and re-layouts: 1.39 us -> 0.04 us
    ppermute x51, starting transfers between devices: 58.1 us -> 45.4 us  [swap(): return lax.ppermute(block, axis, [(i, i ^ offset) for i in range(size)])]
    ppermute x51, waiting for transfers between devices: 17.5 us -> 24.3 us  [swap(): return lax.ppermute(block, axis, [(i, i ^ offset) for i in range(size)])]
    pallas_call x3, Pallas kernels: 16.8 us -> 23 us  [local_grads(): pl.pallas_call(functools.partial(force_kernel, cols, rows, first), out_sh...]
    unnamed x16 -> x12, local copies, waits for them, and re-layouts: 1.39 us -> 0.04 us
  transfers between devices with their start and end apart: 51 -> 51, of which waited for: 21 -> 23; matrix products, arithmetic and copies ran while one was open for 2% -> 3% of each run, Pallas kernels for 0% -> 0%
where the time goes in v5:
time: 99.8 us; the launch traced here: 98.9 us
  starting transfers between devices  45.4 us (45%)
  waiting for transfers between devices  24.3 us (24%)
  Pallas kernels  23 us (23%)
  other arithmetic  4.62 us (5%)
  between operations  1.58 us (2%)
    ppermute x51, starting transfers between devices, swap(): return lax.ppermute(block, axis, [(i, i ^ offset) for i in range(size)])  45.4 us
    ppermute x51, waiting for transfers between devices, swap(): return lax.ppermute(block, axis, [(i, i ^ offset) for i in range(size)])  24.3 us
    pallas_call x3, Pallas kernels, local_grads(): pl.pallas_call(functools.partial(force_kernel, cols, rows, first), out_sh...  23 us
  transfers between devices with their start and end apart: 51, of which 23 were waited for; matrix products, arithmetic and copies ran while one was open for 3% of the time, Pallas kernels for 0%

profile of v5, /device:TPU:0, one launch (start us, length us, event | category | flops | bytes accessed | tf_op | source)
XLA Modules:
  0.0 98.9 jit_solution(16358731281605975048)
XLA Ops:
  1.5 4.0 %collective-permute-start.8 = (bf16[256,128]{1,0:T(8,128)(2,1)S(1)}, bf16[256,128]{1,0:T(8,128)(2,1)S(1)}, u32[]{:S(2)}, u32[]{:S(2)}) collective-permute-start(bf16[256,128]{1,0:T(8,128)(2,1)S(1)} %convert_element_type.250.refs_10_), channel_id=1, source_target_pairs={{0,16},{8,24},{16,0},{24,8},{1,17},{9,25},{17,1},{25,9},{2,18},{10... | collective-permute-start | bytes 196616 | tf_op jit(solution)/shard_map/ppermute | solution.py:265
  5.6 1.6 %collective-permute-start.7 = (bf16[256,128]{1,0:T(8,128)(2,1)S(1)}, bf16[256,128]{1,0:T(8,128)(2,1)S(1)}, u32[]{:S(2)}, u32[]{:S(2)}) collective-permute-start(bf16[256,128]{1,0:T(8,128)(2,1)S(1)} %convert_element_type.250.refs_10_), channel_id=1, source_target_pairs={{0,8},{8,0},{16,24},{24,16},{1,9},{9,1},{17,25},{25,17},{2,10},{10... | collective-permute-start | bytes 196616 | tf_op jit(solution)/shard_map/ppermute | solution.py:265
  8.1 2.4 %collective-permute-start.2 = (bf16[256,128]{1,0:T(8,128)(2,1)S(1)}, bf16[256,128]{1,0:T(8,128)(2,1)S(1)}, u32[]{:S(2)}, u32[]{:S(2)}) collective-permute-start(bf16[256,128]{1,0:T(8,128)(2,1)S(1)} %convert_element_type.249.refs_2_), channel_id=1, source_target_pairs={{0,6},{1,7},{2,4},{3,5},{4,2},{5,3},{6,0},{7,1},{8,14},{9,15},{10,... | collective-permute-start | bytes 196616 | tf_op jit(solution)/shard_map/ppermute | solution.py:265
  13.3 1.4 %collective-permute-done.1.refs_4_ = bf16[256,128]{1,0:T(8,128)(2,1)S(1)} collective-permute-done((bf16[256,128]{1,0:T(8,128)(2,1)S(1)}, bf16[256,128]{1,0:T(8,128)(2,1)S(1)}, u32[]{:S(2)}, u32[]{:S(2)}) %collective-permute-start.1) | collective-permute-done | bytes 65568 | tf_op jit(solution)/shard_map/ppermute | solution.py:265
  16.9 10.3 %tile_force.3 = (bf16[4,256,128]{2,1,0:T(8,128)(2,1)S(1)}, bf16[4,256,128]{2,1,0:T(8,128)(2,1)S(1)}, bf16[256,128]{1,0:T(8,128)(2,1)S(1)}, bf16[256,128]{1,0:T(8...) custom-call(s32[1]{0:T(128)} %copy.13.refs_0_, ...), custom_call_target="tpu_custom_call" | custom-call | tf_op jit(solution)/shard_map/tile_force/pallas_call | solution.py:241
  27.3 1.9 %collective-permute-start.23 = (bf16[256,128]{1,0:T(8,128)(2,1)S(1)}, bf16[256,128]{1,0:T(8,128)(2,1)S(1)}, u32[]{:S(2)}, u32[]{:S(2)}) collective-permute-start(bf16[256,128]{1,0:T(8,128)(2,1)S(1)} %get-tuple-element.31), channel_id=1, source_target_pairs={{0,8},{8,0},{16,24},{24,16},{1,9},{9,1},{17,25},{25,17},{2,10},{10... | collective-permute-start | bytes 196616 | tf_op jit(solution)/shard_map/ppermute | solution.py:265
  29.2 2.8 %collective-permute-done.21 = bf16[256,128]{1,0:T(8,128)(2,1)S(1)} collective-permute-done((bf16[256,128]{1,0:T(8,128)(2,1)S(1)}, bf16[256,128]{1,0:T(8,128)(2,1)S(1)}, u32[]{:S(2)}, u32[]{:S(2)}) %collective-permute-start.21) | collective-permute-done | bytes 65568 | tf_op jit(solution)/shard_map/ppermute | solution.py:265
  32.2 3.2 %collective-permute-start.11 = (bf16[256,128]{1,0:T(8,128)(2,1)S(1)}, bf16[256,128]{1,0:T(8,128)(2,1)S(1)}, u32[]{:S(2)}, u32[]{:S(2)}) collective-permute-start(bf16[256,128]{1,0:T(8,128)(2,1)S(1)} %get-tuple-element.58), channel_id=1, source_target_pairs={{0,2},{1,3},{2,0},{3,1},{4,6},{5,7},{6,4},{7,5},{8,10},{9,11},{10,... | collective-permute-start | bytes 196616 | tf_op jit(solution)/shard_map/ppermute | solution.py:265
  37.3 2.5 %collective-permute-start.25 = (bf16[256,128]{1,0:T(8,128)(2,1)S(1)}, bf16[256,128]{1,0:T(8,128)(2,1)S(1)}, u32[]{:S(2)}, u32[]{:S(2)}) collective-permute-start(bf16[256,128]{1,0:T(8,128)(2,1)S(1)} %fusion.25.refs_9_), channel_id=1, source_target_pairs={{0,16},{8,24},{16,0},{24,8},{1,17},{9,25},{17,1},{25,9},{2,18},{10... | collective-permute-start | bytes 196616 | tf_op jit(solution)/shard_map/ppermute | solution.py:265
  41.0 1.7 %collective-permute-start.16 = (bf16[256,128]{1,0:T(8,128)(2,1)S(1)}, bf16[256,128]{1,0:T(8,128)(2,1)S(1)}, u32[]{:S(2)}, u32[]{:S(2)}) collective-permute-start(bf16[256,128]{1,0:T(8,128)(2,1)S(1)} %get-tuple-element.50.refs_1_), channel_id=1, source_target_pairs={{0,6},{1,7},{2,4},{3,5},{4,2},{5,3},{6,0},{7,1},{8,14},{9,15},{10,... | collective-permute-start | bytes 196616 | tf_op jit(solution)/shard_map/ppermute | solution.py:265
  42.7 1.1 %collective-permute-start.15 = (bf16[256,128]{1,0:T(8,128)(2,1)S(1)}, bf16[256,128]{1,0:T(8,128)(2,1)S(1)}, u32[]{:S(2)}, u32[]{:S(2)}) collective-permute-start(bf16[256,128]{1,0:T(8,128)(2,1)S(1)} %get-tuple-element.50.refs_1_), channel_id=1, source_target_pairs={{0,4},{1,5},{2,6},{3,7},{4,0},{5,1},{6,2},{7,3},{8,12},{9,13},{10,... | collective-permute-start | bytes 196616 | tf_op jit(solution)/shard_map/ppermute | solution.py:265
  44.6 1.0 collective-permute-start.26
  47.0 1.1 %collective-permute-done.14.refs_2_ = bf16[256,128]{1,0:T(8,128)(2,1)S(1)} collective-permute-done((bf16[256,128]{1,0:T(8,128)(2,1)S(1)}, bf16[256,128]{1,0:T(8,128)(2,1)S(1)}, u32[]{:S(2)}, u32[]{:S(2)}) %collective-permute-start.14) | collective-permute-done | bytes 65568 | tf_op jit(solution)/shard_map/ppermute | solution.py:265
  49.3 6.4 %tile_force.4 = (bf16[4,256,128]{2,1,0:T(8,128)(2,1)S(1)}, bf16[4,256,128]{2,1,0:T(8,128)(2,1)S(1)}, bf16[256,128]{1,0:T(8,128)(2,1)S(1)}, bf16[256,128]{1,0:T(8...) custom-call(s32[8,256]{1,0:T(8,128)S(1)} %get-tuple-element.27.refs_0_, ...), custom_call_target="tpu_custom_call" | custom-call | tf_op jit(solution)/shard_map/tile_force/pallas_call | solution.py:241
  55.9 1.9 %collective-permute-start.40 = (bf16[256,128]{1,0:T(8,128)(2,1)S(1)}, bf16[256,128]{1,0:T(8,128)(2,1)S(1)}, u32[]{:S(2)}, u32[]{:S(2)}) collective-permute-start(bf16[256,128]{1,0:T(8,128)(2,1)S(1)} %get-tuple-element.39), channel_id=1, source_target_pairs={{0,8},{8,0},{16,24},{24,16},{1,9},{9,1},{17,25},{25,17},{2,10},{10... | collective-permute-start | bytes 196616 | tf_op jit(solution)/shard_map/ppermute | solution.py:265
  57.8 2.8 %collective-permute-done.38 = bf16[256,128]{1,0:T(8,128)(2,1)S(1)} collective-permute-done((bf16[256,128]{1,0:T(8,128)(2,1)S(1)}, bf16[256,128]{1,0:T(8,128)(2,1)S(1)}, u32[]{:S(2)}, u32[]{:S(2)}) %collective-permute-start.38) | collective-permute-done | bytes 65568 | tf_op jit(solution)/shard_map/ppermute | solution.py:265
  60.6 1.5 %collective-permute-start.39 = (bf16[256,128]{1,0:T(8,128)(2,1)S(1)}, bf16[256,128]{1,0:T(8,128)(2,1)S(1)}, u32[]{:S(2)}, u32[]{:S(2)}) collective-permute-start(bf16[256,128]{1,0:T(8,128)(2,1)S(1)} %add_convert_fusion.4), channel_id=1, source_target_pairs={{0,16},{8,24},{16,0},{24,8},{1,17},{9,25},{17,1},{25,9},{2,18},{10... | collective-permute-start | bytes 196616 | tf_op jit(solution)/shard_map/ppermute | solution.py:265
  62.1 3.7 %collective-permute-start.28 = (bf16[256,128]{1,0:T(8,128)(2,1)S(1)}, bf16[256,128]{1,0:T(8,128)(2,1)S(1)}, u32[]{:S(2)}, u32[]{:S(2)}) collective-permute-start(bf16[256,128]{1,0:T(8,128)(2,1)S(1)} %get-tuple-element.55), channel_id=1, source_target_pairs={{0,2},{1,3},{2,0},{3,1},{4,6},{5,7},{6,4},{7,5},{8,10},{9,11},{10,... | collective-permute-start | bytes 196616 | tf_op jit(solution)/shard_map/ppermute | solution.py:265
  65.9 1.5 %collective-permute-start.29 = (bf16[256,128]{1,0:T(8,128)(2,1)S(1)}, bf16[256,128]{1,0:T(8,128)(2,1)S(1)}, u32[]{:S(2)}, u32[]{:S(2)}) collective-permute-start(bf16[256,128]{1,0:T(8,128)(2,1)S(1)} %get-tuple-element.57), channel_id=1, source_target_pairs={{0,4},{1,5},{2,6},{3,7},{4,0},{5,1},{6,2},{7,3},{8,12},{9,13},{10,... | collective-permute-start | bytes 196616 | tf_op jit(solution)/shard_map/ppermute | solution.py:265
  68.0 1.9 %collective-permute-start.41 = (bf16[256,128]{1,0:T(8,128)(2,1)S(1)}, bf16[256,128]{1,0:T(8,128)(2,1)S(1)}, u32[]{:S(2)}, u32[]{:S(2)}) collective-permute-start(bf16[256,128]{1,0:T(8,128)(2,1)S(1)} %get-tuple-element.46.refs_9_), channel_id=1, source_target_pairs={{0,8},{8,0},{16,24},{24,16},{1,9},{9,1},{17,25},{25,17},{2,10},{10... | collective-permute-start | bytes 196616 | tf_op jit(solution)/shard_map/ppermute | solution.py:265
  69.9 1.1 %collective-permute-done.30 = bf16[256,128]{1,0:T(8,128)(2,1)S(1)} collective-permute-done((bf16[256,128]{1,0:T(8,128)(2,1)S(1)}, bf16[256,128]{1,0:T(8,128)(2,1)S(1)}, u32[]{:S(2)}, u32[]{:S(2)}) %collective-permute-start.30) | collective-permute-done | bytes 65568 | tf_op jit(solution)/shard_map/ppermute | solution.py:265
  71.1 2.1 %collective-permute-start.33 = (bf16[256,128]{1,0:T(8,128)(2,1)S(1)}, bf16[256,128]{1,0:T(8,128)(2,1)S(1)}, u32[]{:S(2)}, u32[]{:S(2)}) collective-permute-start(bf16[256,128]{1,0:T(8,128)(2,1)S(1)} %get-tuple-element.48.refs_1_), channel_id=1, source_target_pairs={{0,6},{1,7},{2,4},{3,5},{4,2},{5,3},{6,0},{7,1},{8,14},{9,15},{10,... | collective-permute-start | bytes 196616 | tf_op jit(solution)/shard_map/ppermute | solution.py:265
  73.4 1.2 %collective-permute-start.31 = (bf16[256,128]{1,0:T(8,128)(2,1)S(1)}, bf16[256,128]{1,0:T(8,128)(2,1)S(1)}, u32[]{:S(2)}, u32[]{:S(2)}) collective-permute-start(bf16[256,128]{1,0:T(8,128)(2,1)S(1)} %get-tuple-element.48.refs_1_), channel_id=1, source_target_pairs={{0,2},{1,3},{2,0},{3,1},{4,6},{5,7},{6,4},{7,5},{8,10},{9,11},{10,... | collective-permute-start | bytes 196616 | tf_op jit(solution)/shard_map/ppermute | solution.py:265
  76.3 1.1 %collective-permute-done.32.refs_3_ = bf16[256,128]{1,0:T(8,128)(2,1)S(1)} collective-permute-done((bf16[256,128]{1,0:T(8,128)(2,1)S(1)}, bf16[256,128]{1,0:T(8,128)(2,1)S(1)}, u32[]{:S(2)}, u32[]{:S(2)}) %collective-permute-start.32) | collective-permute-done | bytes 65568 | tf_op jit(solution)/shard_map/ppermute | solution.py:265
  78.0 1.0 collective-permute-done.43.refs_12_
  79.0 6.4 %tile_force.5 = (bf16[4,256,128]{2,1,0:T(8,128)(2,1)S(1)}, bf16[4,256,128]{2,1,0:T(8,128)(2,1)S(1)}, bf16[256,128]{1,0:T(8,128)(2,1)S(1)}, bf16[256,128]{1,0:T(8...) custom-call(s32[8,256]{1,0:T(8,128)S(1)} %get-tuple-element.27.refs_0_, ...), custom_call_target="tpu_custom_call" | custom-call | tf_op jit(solution)/shard_map/tile_force/pallas_call | solution.py:241
  85.5 1.9 %collective-permute-start.50 = (bf16[256,128]{1,0:T(8,128)(2,1)S(1)}, bf16[256,128]{1,0:T(8,128)(2,1)S(1)}, u32[]{:S(2)}, u32[]{:S(2)}) collective-permute-start(bf16[256,128]{1,0:T(8,128)(2,1)S(1)} %get-tuple-element.45), channel_id=1, source_target_pairs={{0,8},{8,0},{16,24},{24,16},{1,9},{9,1},{17,25},{25,17},{2,10},{10... | collective-permute-start | bytes 196616 | tf_op jit(solution)/shard_map/ppermute | solution.py:265
  87.4 2.8 %collective-permute-done.48 = bf16[256,128]{1,0:T(8,128)(2,1)S(1)} collective-permute-done((bf16[256,128]{1,0:T(8,128)(2,1)S(1)}, bf16[256,128]{1,0:T(8,128)(2,1)S(1)}, u32[]{:S(2)}, u32[]{:S(2)}) %collective-permute-start.48) | collective-permute-done | bytes 65568 | tf_op jit(solution)/shard_map/ppermute | solution.py:265
  90.4 2.3 %collective-permute-start.45 = (bf16[256,128]{1,0:T(8,128)(2,1)S(1)}, bf16[256,128]{1,0:T(8,128)(2,1)S(1)}, u32[]{:S(2)}, u32[]{:S(2)}) collective-permute-start(bf16[256,128]{1,0:T(8,128)(2,1)S(1)} %get-tuple-element.52), channel_id=1, source_target_pairs={{0,2},{1,3},{2,0},{3,1},{4,6},{5,7},{6,4},{7,5},{8,10},{9,11},{10,... | collective-permute-start | bytes 196616 | tf_op jit(solution)/shard_map/ppermute | solution.py:265
  93.2 1.0 %collective-permute-start.46 = (bf16[256,128]{1,0:T(8,128)(2,1)S(1)}, bf16[256,128]{1,0:T(8,128)(2,1)S(1)}, u32[]{:S(2)}, u32[]{:S(2)}) collective-permute-start(bf16[256,128]{1,0:T(8,128)(2,1)S(1)} %get-tuple-element.54), channel_id=1, source_target_pairs={{0,4},{1,5},{2,6},{3,7},{4,0},{5,1},{6,2},{7,3},{8,12},{9,13},{10,... | collective-permute-start | bytes 196616 | tf_op jit(solution)/shard_map/ppermute | solution.py:265
  94.2 1.2 %collective-permute-done.49 = bf16[256,128]{1,0:T(8,128)(2,1)S(1)} collective-permute-done((bf16[256,128]{1,0:T(8,128)(2,1)S(1)}, bf16[256,128]{1,0:T(8,128)(2,1)S(1)}, u32[]{:S(2)}, u32[]{:S(2)}) %collective-permute-start.49) | collective-permute-done | bytes 65568 | tf_op jit(solution)/shard_map/ppermute | solution.py:265
  96.2 1.7 %collective-permute-done.47 = bf16[256,128]{1,0:T(8,128)(2,1)S(1)} collective-permute-done((bf16[256,128]{1,0:T(8,128)(2,1)S(1)}, bf16[256,128]{1,0:T(8,128)(2,1)S(1)}, u32[]{:S(2)}, u32[]{:S(2)}) %collective-permute-start.47) | collective-permute-done | bytes 65568 | tf_op jit(solution)/shard_map/ppermute | solution.py:265
  (100 shorter events, 18.8 us)
Async XLA Ops:
  1.5 10.7 %collective-permute-start.8 = (bf16[256,128]{1,0:T(8,128)(2,1)S(1)}, bf16[256,128]{1,0:T(8,128)(2,1)S(1)}, u32[]{:S(2)}, u32[]{:S(2)}) collective-permute-start(bf16[256,128]{1,0:T(8,128)(2,1)S(1)} %convert_element_type.250.refs_10_), channel_id=1, source_target_pairs={{0,16},{8,24},{16,0},{24,8},{1,17},{9,25},{17,1},{25,9},{2,18},{10... | collective-permute-start | bytes 196616 | tf_op jit(solution)/shard_map/ppermute | solution.py:265
  5.6 6.7 %collective-permute-start.7 = (bf16[256,128]{1,0:T(8,128)(2,1)S(1)}, bf16[256,128]{1,0:T(8,128)(2,1)S(1)}, u32[]{:S(2)}, u32[]{:S(2)}) collective-permute-start(bf16[256,128]{1,0:T(8,128)(2,1)S(1)} %convert_element_type.250.refs_10_), channel_id=1, source_target_pairs={{0,8},{8,0},{16,24},{24,16},{1,9},{9,1},{17,25},{25,17},{2,10},{10... | collective-permute-start | bytes 196616 | tf_op jit(solution)/shard_map/ppermute | solution.py:265
  8.1 5.3 %collective-permute-start.2 = (bf16[256,128]{1,0:T(8,128)(2,1)S(1)}, bf16[256,128]{1,0:T(8,128)(2,1)S(1)}, u32[]{:S(2)}, u32[]{:S(2)}) collective-permute-start(bf16[256,128]{1,0:T(8,128)(2,1)S(1)} %convert_element_type.249.refs_2_), channel_id=1, source_target_pairs={{0,6},{1,7},{2,4},{3,5},{4,2},{5,3},{6,0},{7,1},{8,14},{9,15},{10,... | collective-permute-start | bytes 196616 | tf_op jit(solution)/shard_map/ppermute | solution.py:265
  12.3 4.5 %collective-permute-start.9 = (bf16[256,128]{1,0:T(8,128)(2,1)S(1)}, bf16[256,128]{1,0:T(8,128)(2,1)S(1)}, u32[]{:S(2)}, u32[]{:S(2)}) collective-permute-start(bf16[256,128]{1,0:T(8,128)(2,1)S(1)} %collective-permute-done.8.refs_12_), channel_id=1, source_target_pairs={{0,8},{8,0},{16,24},{24,16},{1,9},{9,1},{17,25},{25,17},{2,10},{10... | collective-permute-start | bytes 196616 | tf_op jit(solution)/shard_map/ppermute | solution.py:265
  27.1 4.9 %collective-permute-start.21 = (bf16[256,128]{1,0:T(8,128)(2,1)S(1)}, bf16[256,128]{1,0:T(8,128)(2,1)S(1)}, u32[]{:S(2)}, u32[]{:S(2)}) collective-permute-start(bf16[256,128]{1,0:T(8,128)(2,1)S(1)} %get-tuple-element.30), channel_id=1, source_target_pairs={{0,8},{8,0},{16,24},{24,16},{1,9},{9,1},{17,25},{25,17},{2,10},{10... | collective-permute-start | bytes 196616 | tf_op jit(solution)/shard_map/ppermute | solution.py:265
  27.2 4.9 %collective-permute-start.10 = (bf16[4,256,128]{2,1,0:T(8,128)(2,1)S(1)}, bf16[4,256,128]{2,1,0:T(8,128)(2,1)S(1)}, u32[]{:S(2)}, u32[]{:S(2)}) collective-permute-start(bf16[4,256,128]{2,1,0:T(8,128)(2,1)S(1)} %get-tuple-element.26), channel_id=1, source_target_pairs={{0,1},{1,0},{2,3},{3,2},{4,5},{5,4},{6,7},{7,6},{8,9},{9,8},{10,11... | collective-permute-start | bytes 786440 | tf_op jit(solution)/shard_map/ppermute | solution.py:265
  27.3 9.6 %collective-permute-start.23 = (bf16[256,128]{1,0:T(8,128)(2,1)S(1)}, bf16[256,128]{1,0:T(8,128)(2,1)S(1)}, u32[]{:S(2)}, u32[]{:S(2)}) collective-permute-start(bf16[256,128]{1,0:T(8,128)(2,1)S(1)} %get-tuple-element.31), channel_id=1, source_target_pairs={{0,8},{8,0},{16,24},{24,16},{1,9},{9,1},{17,25},{25,17},{2,10},{10... | collective-permute-start | bytes 196616 | tf_op jit(solution)/shard_map/ppermute | solution.py:265
  32.0 5.2 %collective-permute-start.22 = (bf16[256,128]{1,0:T(8,128)(2,1)S(1)}, bf16[256,128]{1,0:T(8,128)(2,1)S(1)}, u32[]{:S(2)}, u32[]{:S(2)}) collective-permute-start(bf16[256,128]{1,0:T(8,128)(2,1)S(1)} %add_convert_fusion.8), channel_id=1, source_target_pairs={{0,16},{8,24},{16,0},{24,8},{1,17},{9,25},{17,1},{25,9},{2,18},{10... | collective-permute-start | bytes 196616 | tf_op jit(solution)/shard_map/ppermute | solution.py:265
  32.2 7.7 %collective-permute-start.11 = (bf16[256,128]{1,0:T(8,128)(2,1)S(1)}, bf16[256,128]{1,0:T(8,128)(2,1)S(1)}, u32[]{:S(2)}, u32[]{:S(2)}) collective-permute-start(bf16[256,128]{1,0:T(8,128)(2,1)S(1)} %get-tuple-element.58), channel_id=1, source_target_pairs={{0,2},{1,3},{2,0},{3,1},{4,6},{5,7},{6,4},{7,5},{8,10},{9,11},{10,... | collective-permute-start | bytes 196616 | tf_op jit(solution)/shard_map/ppermute | solution.py:265
  35.3 5.3 %collective-permute-start.13 = (bf16[256,128]{1,0:T(8,128)(2,1)S(1)}, bf16[256,128]{1,0:T(8,128)(2,1)S(1)}, u32[]{:S(2)}, u32[]{:S(2)}) collective-permute-start(bf16[256,128]{1,0:T(8,128)(2,1)S(1)} %get-tuple-element.59), channel_id=1, source_target_pairs={{0,6},{1,7},{2,4},{3,5},{4,2},{5,3},{6,0},{7,1},{8,14},{9,15},{10,... | collective-permute-start | bytes 196616 | tf_op jit(solution)/shard_map/ppermute | solution.py:265
  36.0 5.0 %collective-permute-start.12 = (bf16[256,128]{1,0:T(8,128)(2,1)S(1)}, bf16[256,128]{1,0:T(8,128)(2,1)S(1)}, u32[]{:S(2)}, u32[]{:S(2)}) collective-permute-start(bf16[256,128]{1,0:T(8,128)(2,1)S(1)} %get-tuple-element.60), channel_id=1, source_target_pairs={{0,4},{1,5},{2,6},{3,7},{4,0},{5,1},{6,2},{7,3},{8,12},{9,13},{10,... | collective-permute-start | bytes 196616 | tf_op jit(solution)/shard_map/ppermute | solution.py:265
  37.3 7.3 %collective-permute-start.25 = (bf16[256,128]{1,0:T(8,128)(2,1)S(1)}, bf16[256,128]{1,0:T(8,128)(2,1)S(1)}, u32[]{:S(2)}, u32[]{:S(2)}) collective-permute-start(bf16[256,128]{1,0:T(8,128)(2,1)S(1)} %fusion.25.refs_9_), channel_id=1, source_target_pairs={{0,16},{8,24},{16,0},{24,8},{1,17},{9,25},{17,1},{25,9},{2,18},{10... | collective-permute-start | bytes 196616 | tf_op jit(solution)/shard_map/ppermute | solution.py:265
  39.9 5.7 %collective-permute-start.24 = (bf16[256,128]{1,0:T(8,128)(2,1)S(1)}, bf16[256,128]{1,0:T(8,128)(2,1)S(1)}, u32[]{:S(2)}, u32[]{:S(2)}) collective-permute-start(bf16[256,128]{1,0:T(8,128)(2,1)S(1)} %fusion.25.refs_9_), channel_id=1, source_target_pairs={{0,8},{8,0},{16,24},{24,16},{1,9},{9,1},{17,25},{25,17},{2,10},{10... | collective-permute-start | bytes 196616 | tf_op jit(solution)/shard_map/ppermute | solution.py:265
  41.0 5.2 %collective-permute-start.16 = (bf16[256,128]{1,0:T(8,128)(2,1)S(1)}, bf16[256,128]{1,0:T(8,128)(2,1)S(1)}, u32[]{:S(2)}, u32[]{:S(2)}) collective-permute-start(bf16[256,128]{1,0:T(8,128)(2,1)S(1)} %get-tuple-element.50.refs_1_), channel_id=1, source_target_pairs={{0,6},{1,7},{2,4},{3,5},{4,2},{5,3},{6,0},{7,1},{8,14},{9,15},{10,... | collective-permute-start | bytes 196616 | tf_op jit(solution)/shard_map/ppermute | solution.py:265
  42.7 4.3 %collective-permute-start.15 = (bf16[256,128]{1,0:T(8,128)(2,1)S(1)}, bf16[256,128]{1,0:T(8,128)(2,1)S(1)}, u32[]{:S(2)}, u32[]{:S(2)}) collective-permute-start(bf16[256,128]{1,0:T(8,128)(2,1)S(1)} %get-tuple-element.50.refs_1_), channel_id=1, source_target_pairs={{0,4},{1,5},{2,6},{3,7},{4,0},{5,1},{6,2},{7,3},{8,12},{9,13},{10,... | collective-permute-start | bytes 196616 | tf_op jit(solution)/shard_map/ppermute | solution.py:265
  55.7 4.9 %collective-permute-start.38 = (bf16[256,128]{1,0:T(8,128)(2,1)S(1)}, bf16[256,128]{1,0:T(8,128)(2,1)S(1)}, u32[]{:S(2)}, u32[]{:S(2)}) collective-permute-start(bf16[256,128]{1,0:T(8,128)(2,1)S(1)} %get-tuple-element.38), channel_id=1, source_target_pairs={{0,8},{8,0},{16,24},{24,16},{1,9},{9,1},{17,25},{25,17},{2,10},{10... | collective-permute-start | bytes 196616 | tf_op jit(solution)/shard_map/ppermute | solution.py:265
  55.8 6.3 %collective-permute-start.27 = (bf16[4,256,128]{2,1,0:T(8,128)(2,1)S(1)}, bf16[4,256,128]{2,1,0:T(8,128)(2,1)S(1)}, u32[]{:S(2)}, u32[]{:S(2)}) collective-permute-start(bf16[4,256,128]{2,1,0:T(8,128)(2,1)S(1)} %get-tuple-element.35), channel_id=1, source_target_pairs={{0,1},{1,0},{2,3},{3,2},{4,5},{5,4},{6,7},{7,6},{8,9},{9,8},{10,11... | collective-permute-start | bytes 786440 | tf_op jit(solution)/shard_map/ppermute | solution.py:265
  55.9 11.5 %collective-permute-start.40 = (bf16[256,128]{1,0:T(8,128)(2,1)S(1)}, bf16[256,128]{1,0:T(8,128)(2,1)S(1)}, u32[]{:S(2)}, u32[]{:S(2)}) collective-permute-start(bf16[256,128]{1,0:T(8,128)(2,1)S(1)} %get-tuple-element.39), channel_id=1, source_target_pairs={{0,8},{8,0},{16,24},{24,16},{1,9},{9,1},{17,25},{25,17},{2,10},{10... | collective-permute-start | bytes 196616 | tf_op jit(solution)/shard_map/ppermute | solution.py:265
  60.6 6.8 %collective-permute-start.39 = (bf16[256,128]{1,0:T(8,128)(2,1)S(1)}, bf16[256,128]{1,0:T(8,128)(2,1)S(1)}, u32[]{:S(2)}, u32[]{:S(2)}) collective-permute-start(bf16[256,128]{1,0:T(8,128)(2,1)S(1)} %add_convert_fusion.4), channel_id=1, source_target_pairs={{0,16},{8,24},{16,0},{24,8},{1,17},{9,25},{17,1},{25,9},{2,18},{10... | collective-permute-start | bytes 196616 | tf_op jit(solution)/shard_map/ppermute | solution.py:265
  62.1 7.8 %collective-permute-start.28 = (bf16[256,128]{1,0:T(8,128)(2,1)S(1)}, bf16[256,128]{1,0:T(8,128)(2,1)S(1)}, u32[]{:S(2)}, u32[]{:S(2)}) collective-permute-start(bf16[256,128]{1,0:T(8,128)(2,1)S(1)} %get-tuple-element.55), channel_id=1, source_target_pairs={{0,2},{1,3},{2,0},{3,1},{4,6},{5,7},{6,4},{7,5},{8,10},{9,11},{10,... | collective-permute-start | bytes 196616 | tf_op jit(solution)/shard_map/ppermute | solution.py:265
  65.8 5.2 %collective-permute-start.30 = (bf16[256,128]{1,0:T(8,128)(2,1)S(1)}, bf16[256,128]{1,0:T(8,128)(2,1)S(1)}, u32[]{:S(2)}, u32[]{:S(2)}) collective-permute-start(bf16[256,128]{1,0:T(8,128)(2,1)S(1)} %get-tuple-element.56), channel_id=1, source_target_pairs={{0,6},{1,7},{2,4},{3,5},{4,2},{5,3},{6,0},{7,1},{8,14},{9,15},{10,... | collective-permute-start | bytes 196616 | tf_op jit(solution)/shard_map/ppermute | solution.py:265
  65.9 5.2 %collective-permute-start.29 = (bf16[256,128]{1,0:T(8,128)(2,1)S(1)}, bf16[256,128]{1,0:T(8,128)(2,1)S(1)}, u32[]{:S(2)}, u32[]{:S(2)}) collective-permute-start(bf16[256,128]{1,0:T(8,128)(2,1)S(1)} %get-tuple-element.57), channel_id=1, source_target_pairs={{0,4},{1,5},{2,6},{3,7},{4,0},{5,1},{6,2},{7,3},{8,12},{9,13},{10,... | collective-permute-start | bytes 196616 | tf_op jit(solution)/shard_map/ppermute | solution.py:265
  67.5 7.2 %collective-permute-start.42 = (bf16[256,128]{1,0:T(8,128)(2,1)S(1)}, bf16[256,128]{1,0:T(8,128)(2,1)S(1)}, u32[]{:S(2)}, u32[]{:S(2)}) collective-permute-start(bf16[256,128]{1,0:T(8,128)(2,1)S(1)} %get-tuple-element.46.refs_9_), channel_id=1, source_target_pairs={{0,16},{8,24},{16,0},{24,8},{1,17},{9,25},{17,1},{25,9},{2,18},{10... | collective-permute-start | bytes 196616 | tf_op jit(solution)/shard_map/ppermute | solution.py:265
  68.0 7.5 %collective-permute-start.41 = (bf16[256,128]{1,0:T(8,128)(2,1)S(1)}, bf16[256,128]{1,0:T(8,128)(2,1)S(1)}, u32[]{:S(2)}, u32[]{:S(2)}) collective-permute-start(bf16[256,128]{1,0:T(8,128)(2,1)S(1)} %get-tuple-element.46.refs_9_), channel_id=1, source_target_pairs={{0,8},{8,0},{16,24},{24,16},{1,9},{9,1},{17,25},{25,17},{2,10},{10... | collective-permute-start | bytes 196616 | tf_op jit(solution)/shard_map/ppermute | solution.py:265
  71.1 5.2 %collective-permute-start.33 = (bf16[256,128]{1,0:T(8,128)(2,1)S(1)}, bf16[256,128]{1,0:T(8,128)(2,1)S(1)}, u32[]{:S(2)}, u32[]{:S(2)}) collective-permute-start(bf16[256,128]{1,0:T(8,128)(2,1)S(1)} %get-tuple-element.48.refs_1_), channel_id=1, source_target_pairs={{0,6},{1,7},{2,4},{3,5},{4,2},{5,3},{6,0},{7,1},{8,14},{9,15},{10,... | collective-permute-start | bytes 196616 | tf_op jit(solution)/shard_map/ppermute | solution.py:265
  85.3 4.9 %collective-permute-start.48 = (bf16[256,128]{1,0:T(8,128)(2,1)S(1)}, bf16[256,128]{1,0:T(8,128)(2,1)S(1)}, u32[]{:S(2)}, u32[]{:S(2)}) collective-permute-start(bf16[256,128]{1,0:T(8,128)(2,1)S(1)} %get-tuple-element.44), channel_id=1, source_target_pairs={{0,8},{8,0},{16,24},{24,16},{1,9},{9,1},{17,25},{25,17},{2,10},{10... | collective-permute-start | bytes 196616 | tf_op jit(solution)/shard_map/ppermute | solution.py:265
  85.4 4.9 %collective-permute-start.44 = (bf16[4,256,128]{2,1,0:T(8,128)(2,1)S(1)}, bf16[4,256,128]{2,1,0:T(8,128)(2,1)S(1)}, u32[]{:S(2)}, u32[]{:S(2)}) collective-permute-start(bf16[4,256,128]{2,1,0:T(8,128)(2,1)S(1)} %get-tuple-element.41), channel_id=1, source_target_pairs={{0,1},{1,0},{2,3},{3,2},{4,5},{5,4},{6,7},{7,6},{8,9},{9,8},{10,11... | collective-permute-start | bytes 786440 | tf_op jit(solution)/shard_map/ppermute | solution.py:265
  85.5 8.7 %collective-permute-start.50 = (bf16[256,128]{1,0:T(8,128)(2,1)S(1)}, bf16[256,128]{1,0:T(8,128)(2,1)S(1)}, u32[]{:S(2)}, u32[]{:S(2)}) collective-permute-start(bf16[256,128]{1,0:T(8,128)(2,1)S(1)} %get-tuple-element.45), channel_id=1, source_target_pairs={{0,8},{8,0},{16,24},{24,16},{1,9},{9,1},{17,25},{25,17},{2,10},{10... | collective-permute-start | bytes 196616 | tf_op jit(solution)/shard_map/ppermute | solution.py:265
  90.2 5.2 %collective-permute-start.49 = (bf16[256,128]{1,0:T(8,128)(2,1)S(1)}, bf16[256,128]{1,0:T(8,128)(2,1)S(1)}, u32[]{:S(2)}, u32[]{:S(2)}) collective-permute-start(bf16[256,128]{1,0:T(8,128)(2,1)S(1)} %add_convert_fusion), channel_id=1, source_target_pairs={{0,16},{8,24},{16,0},{24,8},{1,17},{9,25},{17,1},{25,9},{2,18},{10... | collective-permute-start | bytes 196616 | tf_op jit(solution)/shard_map/ppermute | solution.py:265
  90.4 5.9 %collective-permute-start.45 = (bf16[256,128]{1,0:T(8,128)(2,1)S(1)}, bf16[256,128]{1,0:T(8,128)(2,1)S(1)}, u32[]{:S(2)}, u32[]{:S(2)}) collective-permute-start(bf16[256,128]{1,0:T(8,128)(2,1)S(1)} %get-tuple-element.52), channel_id=1, source_target_pairs={{0,2},{1,3},{2,0},{3,1},{4,6},{5,7},{6,4},{7,5},{8,10},{9,11},{10,... | collective-permute-start | bytes 196616 | tf_op jit(solution)/shard_map/ppermute | solution.py:265
  92.7 5.3 %collective-permute-start.47 = (bf16[256,128]{1,0:T(8,128)(2,1)S(1)}, bf16[256,128]{1,0:T(8,128)(2,1)S(1)}, u32[]{:S(2)}, u32[]{:S(2)}) collective-permute-start(bf16[256,128]{1,0:T(8,128)(2,1)S(1)} %get-tuple-element.53), channel_id=1, source_target_pairs={{0,6},{1,7},{2,4},{3,5},{4,2},{5,3},{6,0},{7,1},{8,14},{9,15},{10,... | collective-permute-start | bytes 196616 | tf_op jit(solution)/shard_map/ppermute | solution.py:265
  93.2 5.0 %collective-permute-start.46 = (bf16[256,128]{1,0:T(8,128)(2,1)S(1)}, bf16[256,128]{1,0:T(8,128)(2,1)S(1)}, u32[]{:S(2)}, u32[]{:S(2)}) collective-permute-start(bf16[256,128]{1,0:T(8,128)(2,1)S(1)} %get-tuple-element.54), channel_id=1, source_target_pairs={{0,4},{1,5},{2,6},{3,7},{4,0},{5,1},{6,2},{7,3},{8,12},{9,13},{10,... | collective-permute-start | bytes 196616 | tf_op jit(solution)/shard_map/ppermute | solution.py:265
  (25 other events, 202.6 us)
